TPU v7x, 128 devices: a whole 4x4x4 slice. The times are simulated.
128 devices in a mesh: ctx: 16 (over x, y), tp: 4 (over z), dp: 2 (over core).
Axes of the slice: x: 4, y: 4, z: 4, core: 2. Of those that a mesh axis runs over, the one named last changes fastest.
Arguments:
- grad_out: bfloat16 [2, 4096, 8192], P('dp', 'ctx'), may hold values from -6 to 6
- out_weight: bfloat16 [8192, 4096], P(None, 'tp'), may hold values from -0.09375 to 0.09375
- query_states: bfloat16 [2, 4096, 4096], P('dp', 'ctx', 'tp'), may hold values from -6 to 6
- key_states: bfloat16 [2, 4096, 512], P('dp', 'ctx', 'tp'), may hold values from -6 to 6
- value_tensor: bfloat16 [2, 4096, 512], P('dp', 'ctx', 'tp'), may hold values from -6 to 6
- attn_out: bfloat16 [2, 4096, 4096], P('dp', 'ctx', 'tp'), may hold values from -1.25 to 1.25
- doc_ids: int32 [2, 4096], P('dp'), may hold values from 0 to 31, never falling along the last dimension, each value on 1 to 1024 neighbouring positions
- block_order: int32 [2, 256], P('dp'), may hold values from 0 to 255, as said below
Outputs:
- query_grad: bfloat16 [2, 4096, 4096], P('dp', 'ctx', 'tp')
- key_gradient: bfloat16 [2, 4096, 512], P('dp', 'ctx', 'tp')
- value_gradient: bfloat16 [2, 4096, 512], P('dp', 'ctx', 'tp')
- weight_grad: float32 [8192, 4096], P(('ctx', 'dp'), 'tp')
Inputs may be any that keep to these rules, and one draw needn't show every extreme that they name: `block_order`: for each micro-batch a permutation of the row blocks. The slots that one index of ctx holds in the owner layout receive at most 2 of the row blocks that any one index of ctx holds in token order, and in every draw some index hands exactly 2 blocks to one owner. `doc_ids`: document ids never fall along a micro-batch; every document has 1 to 1024 tokens and one has exactly 1024.
All inputs are finite; a program needn't handle non-finite values.
Results may differ from a plain program's by a relative error of at most 0.022.
Values may be sent and summed in bfloat16 or wider, within the bound.
No kernel may reach another device: no remote copies, remote signals or barrier semaphores. Data moves between devices by JAX's collectives and lax.ppermute only.
A program may use at most 128 MiB of HBM per device.

v0:
```python
import math

import jax
import jax.numpy as jnp
from jax import lax
from jax.sharding import PartitionSpec as P

HEAD_WIDTH = 128
CAP = 2


NEG_FILL = -1e30


def pair_mask(query_pos, query_doc, doc_row, start, length):
    key_pos = start + jnp.arange(length, dtype=jnp.int32)
    inside = key_pos >= 0
    key_doc = jnp.take(doc_row, jnp.clip(key_pos, 0, doc_row.shape[0] - 1))
    return (
        inside[None, :]
        & (query_doc[:, None] == key_doc[None, :])
        & (key_pos[None, :] <= query_pos[:, None])
    )


def add_rows(running, addend, offset):
    current = lax.dynamic_slice_in_dim(running, offset, addend.shape[0], 0)
    return lax.dynamic_update_slice_in_dim(running, current + addend, offset, 0)


def route_tables(slot_blocks, own_index, parties):
    total_blocks = slot_blocks.shape[0]
    slot_ids = jnp.arange(total_blocks, dtype=jnp.int32)
    slot_of_block = jnp.sum(
        jnp.where(slot_blocks[None, :] == slot_ids[:, None], slot_ids[None, :], 0), axis=1
    )
    dest_slot = lax.dynamic_slice_in_dim(slot_of_block, own_index * parties, parties, 0)
    dest_dev = dest_slot // parties
    send_rank = jnp.sum(
        (dest_dev[:, None] == dest_dev[None, :]) & (dest_slot[None, :] < dest_slot[:, None]), axis=1
    )
    send_pos = dest_dev * CAP + send_rank
    buffer_ids = jnp.arange(parties * CAP, dtype=jnp.int32)
    send_select = (buffer_ids[:, None] == send_pos[None, :]).astype(jnp.bfloat16)
    held_blocks = lax.dynamic_slice_in_dim(slot_blocks, own_index * parties, parties, 0)
    source_dev = held_blocks // parties
    local_ids = jnp.arange(parties, dtype=jnp.int32)
    recv_rank = jnp.sum(
        (source_dev[:, None] == source_dev[None, :]) & (local_ids[None, :] < local_ids[:, None]),
        axis=1,
    )
    recv_pos = source_dev * CAP + recv_rank
    recv_select = (recv_pos[:, None] == buffer_ids[None, :]).astype(jnp.bfloat16)
    return (send_select, recv_select, held_blocks)


def pack_rows(matrix, send_select, parties):
    flattened = matrix.reshape(send_select.shape[1], -1)
    packed = jnp.dot(send_select, flattened, preferred_element_type=jnp.float32).astype(
        jnp.bfloat16
    )
    return packed.reshape(parties, -1, matrix.shape[1])


def unpack_rows(received, recv_select):
    feat_width = received.shape[2]
    flattened = received.reshape(recv_select.shape[1], -1)
    placed = jnp.dot(recv_select, flattened, preferred_element_type=jnp.float32).astype(
        jnp.bfloat16
    )
    return placed.reshape(-1, feat_width)


def attend_rows(query_rows, grad_rows, out_rows, query_pos, doc_row, key_local, value_local):
    row_count, feat_width = query_rows.shape
    kv_width = key_local.shape[1]
    kv_heads = kv_width // HEAD_WIDTH
    group_size = feat_width // kv_width
    score_scale = 1.0 / math.sqrt(HEAD_WIDTH)
    key_base = 0
    acc_len = doc_row.shape[0]
    query_doc = jnp.take(doc_row, query_pos)
    query_heads = query_rows.reshape(row_count, kv_heads, group_size, HEAD_WIDTH)
    grad_heads = grad_rows.reshape(row_count, kv_heads, group_size, HEAD_WIDTH)
    out_heads = out_rows.reshape(row_count, kv_heads, group_size, HEAD_WIDTH)
    row_dot = jnp.transpose(
        jnp.sum(grad_heads.astype(jnp.float32) * out_heads.astype(jnp.float32), axis=3), (1, 2, 0)
    )

    def scores_of(key_piece):
        key_heads = key_piece.reshape(key_piece.shape[0], kv_heads, HEAD_WIDTH)
        return (
            jnp.einsum("rkgd,nkd->kgrn", query_heads, key_heads, preferred_element_type=jnp.float32)
            * score_scale
        )

    def stats_step(carried, key_piece, offset):
        allowed = pair_mask(query_pos, query_doc, doc_row, key_base + offset, key_piece.shape[0])

        def stats_update(running):
            run_max, run_sum = running
            scores = jnp.where(allowed, scores_of(key_piece), NEG_FILL)
            new_max = jnp.maximum(run_max, jnp.max(scores, axis=3))
            masked_exp = jnp.where(allowed, jnp.exp(scores - new_max[..., None]), 0.0)
            return (new_max, run_sum * jnp.exp(run_max - new_max) + jnp.sum(masked_exp, axis=3))

        return lax.cond(jnp.any(allowed), stats_update, lambda running: running, carried)

    def make_grad_step(log_norm):

        def grad_step(carried, portion, offset):
            key_piece, value_piece = portion
            length = key_piece.shape[0]
            allowed = pair_mask(query_pos, query_doc, doc_row, key_base + offset, length)

            def grad_update(running):
                query_acc, key_acc, value_acc = running
                key_heads = key_piece.reshape(length, kv_heads, HEAD_WIDTH)
                value_heads = value_piece.reshape(length, kv_heads, HEAD_WIDTH)
                scores = scores_of(key_piece)
                attn_probs = jnp.exp(jnp.where(allowed, scores - log_norm[..., None], NEG_FILL))
                probs_low = attn_probs.astype(jnp.bfloat16)
                value_fragment = jnp.einsum(
                    "kgrn,rkgd->nkd", probs_low, grad_heads, preferred_element_type=jnp.float32
                )
                prob_grad = jnp.einsum(
                    "rkgd,nkd->kgrn", grad_heads, value_heads, preferred_element_type=jnp.float32
                )
                score_grad = (attn_probs * (prob_grad - row_dot[..., None])).astype(jnp.bfloat16)
                query_acc = query_acc + jnp.einsum(
                    "kgrn,nkd->rkgd", score_grad, key_heads, preferred_element_type=jnp.float32
                )
                key_fragment = jnp.einsum(
                    "kgrn,rkgd->nkd", score_grad, query_heads, preferred_element_type=jnp.float32
                )
                key_acc = add_rows(key_acc, key_fragment.reshape(length, kv_width), offset)
                value_acc = add_rows(value_acc, value_fragment.reshape(length, kv_width), offset)
                return (query_acc, key_acc, value_acc)

            return lax.cond(jnp.any(allowed), grad_update, lambda running: running, carried)

        return grad_step

    stats_init = (
        jnp.full((kv_heads, group_size, row_count), NEG_FILL, jnp.float32),
        jnp.zeros((kv_heads, group_size, row_count), jnp.float32),
    )
    grad_init = (
        jnp.zeros((row_count, kv_heads, group_size, HEAD_WIDTH), jnp.float32),
        jnp.zeros((acc_len, kv_width), jnp.float32),
        jnp.zeros((acc_len, kv_width), jnp.float32),
    )
    key_all, value_all = (
        lax.all_gather(key_local, "ctx", axis=0, tiled=True),
        lax.all_gather(value_local, "ctx", axis=0, tiled=True),
    )
    block_len = math.gcd(512, acc_len)
    block_count = acc_len // block_len

    def stats_loop(step_index, running):
        offset = step_index * block_len
        return stats_step(running, lax.dynamic_slice_in_dim(key_all, offset, block_len, 0), offset)

    run_max, run_sum = lax.fori_loop(0, block_count, stats_loop, stats_init)
    grad_step = make_grad_step(run_max + jnp.log(run_sum))

    def grad_loop(step_index, running):
        offset = step_index * block_len
        portion = (
            lax.dynamic_slice_in_dim(key_all, offset, block_len, 0),
            lax.dynamic_slice_in_dim(value_all, offset, block_len, 0),
        )
        return grad_step(running, portion, offset)

    query_acc, key_acc, value_acc = lax.fori_loop(0, block_count, grad_loop, grad_init)
    return ((query_acc * score_scale).reshape(row_count, feat_width), key_acc, value_acc)


def reduce_partials(key_acc, value_acc):
    return (
        lax.psum_scatter(
            key_acc.astype(jnp.bfloat16), "ctx", scatter_dimension=0, tiled=True
        ).astype(jnp.float32),
        lax.psum_scatter(
            value_acc.astype(jnp.bfloat16), "ctx", scatter_dimension=0, tiled=True
        ).astype(jnp.float32),
    )


def on_device(
    grad_out, out_weight, query_states, key_states, value_tensor, attn_out, doc_ids, block_order
):
    row_count = query_states.shape[1]
    parties = lax.axis_size("ctx")
    own_index = lax.axis_index("ctx")
    block_rows = row_count // parties
    score_scale = 1.0 / math.sqrt(HEAD_WIDTH)
    doc_row = doc_ids[0]
    grad_rows = grad_out[0]
    out_rows = attn_out[0]
    attn_grad = jnp.dot(grad_rows, out_weight, preferred_element_type=jnp.float32).astype(
        jnp.bfloat16
    )
    send_select, recv_select, held_blocks = route_tables(block_order[0], own_index, parties)
    received = (
        lax.all_to_all(
            pack_rows(query_states[0], send_select, parties),
            "ctx",
            split_axis=0,
            concat_axis=0,
            tiled=True,
        ),
        lax.all_to_all(
            pack_rows(attn_grad, send_select, parties),
            "ctx",
            split_axis=0,
            concat_axis=0,
            tiled=True,
        ),
        lax.all_to_all(
            pack_rows(out_rows, send_select, parties),
            "ctx",
            split_axis=0,
            concat_axis=0,
            tiled=True,
        ),
    )
    query_own = unpack_rows(received[0], recv_select)
    grad_own = unpack_rows(received[1], recv_select)
    out_own = unpack_rows(received[2], recv_select)
    query_pos = (
        held_blocks[:, None] * block_rows + jnp.arange(block_rows, dtype=jnp.int32)[None, :]
    ).reshape(row_count)
    query_acc, key_acc, value_acc = attend_rows(
        query_own, grad_own, out_own, query_pos, doc_row, key_states[0], value_tensor[0]
    )
    query_grad = query_acc.astype(jnp.bfloat16)
    key_sum, value_sum = reduce_partials(key_acc, value_acc)
    key_gradient = (key_sum * score_scale).astype(jnp.bfloat16)
    value_gradient = value_sum.astype(jnp.bfloat16)
    weight_grad = lax.psum_scatter(
        lax.dot_general(
            grad_rows, out_rows, (((0,), (0,)), ((), ())), preferred_element_type=jnp.float32
        ).astype(jnp.bfloat16),
        ("ctx", "dp"),
        scatter_dimension=0,
        tiled=True,
    ).astype(jnp.float32)
    return (query_grad[None], key_gradient[None], value_gradient[None], weight_grad)


def solution(mesh):
    in_specs = (
        P("dp", "ctx", None),
        P(None, "tp"),
        P("dp", "ctx", "tp"),
        P("dp", "ctx", "tp"),
        P("dp", "ctx", "tp"),
        P("dp", "ctx", "tp"),
        P("dp", None),
        P("dp", None),
    )
    out_specs = (
        P("dp", "ctx", "tp"),
        P("dp", "ctx", "tp"),
        P("dp", "ctx", "tp"),
        P(("ctx", "dp"), "tp"),
    )
    return jax.shard_map(
        on_device, mesh=mesh, in_specs=in_specs, out_specs=out_specs, check_vma=False
    )
```

profile of v0, /device:TPU:0, one launch (start us, length us, event | category | flops | bytes accessed | tf_op | source)
XLA Modules:
  0.0 555.8 jit_solution(6427461994774551280)
XLA Ops:
  7.9 11.5 %fusion.69 = bf16[256,1024]{1,0:T(8,128)(2,1)S(1)} fusion(bf16[8192,1024]{1,0:T(8,128)(2,1)} %param.19, bf16[1,256,8192]{2,1,0:T(8,128)(2,1)} %param.18), kind=kOutput, calls=%fused_computation.78 | convolution fusion | flops 4295229440 | bytes 21495808 | tf_op jit(solution)/shard_map/dot_general | solution.py:201
  21.8 7.2 %all-to-all-start.1 = ((bf16[16,32,1024]{2,1,0:T(8,128)(2,1)}), bf16[16,32,1024]{2,1,0:T(8,128)(2,1)S(1)}, u32[]{:S(2)}, u32[]{:S(2)}) async-start(bf16[16,32,1024]{2,1,0:T(8,128)(2,1)} %reshape.279), calls=%async_computation.1 | async-start | bytes 2097152 | tf_op jit(solution)/shard_map/all_to_all | solution.py:213
  31.8 15.2 %all-to-all-done.1 = bf16[16,32,1024]{2,1,0:T(8,128)(2,1)S(1)} async-done(((bf16[16,32,1024]{2,1,0:T(8,128)(2,1)}), bf16[16,32,1024]{2,1,0:T(8,128)(2,1)S(1)}, u32[]{:S(2)}, u32[]{:S(2)}) %all-to-all-start.1) | async-done | bytes 1048608 | tf_op jit(solution)/shard_map/all_to_all | solution.py:213
  47.0 3.7 all-to-all-start
  55.2 14.0 %all-to-all-done = bf16[16,32,1024]{2,1,0:T(8,128)(2,1)S(1)} async-done(((bf16[16,32,1024]{2,1,0:T(8,128)(2,1)}), bf16[16,32,1024]{2,1,0:T(8,128)(2,1)S(1)}, u32[]{:S(2)}, u32[]{:S(2)}) %all-to-all-start) | async-done | bytes 1048608 | tf_op jit(solution)/shard_map/all_to_all | solution.py:206
  69.2 4.3 all-to-all-start.2
  82.8 6.2 %all-to-all-done.2 = bf16[16,32,1024]{2,1,0:T(8,128)(2,1)} async-done(((bf16[16,32,1024]{2,1,0:T(8,128)(2,1)}), bf16[16,32,1024]{2,1,0:T(8,128)(2,1)}, u32[]{:S(2)}, u32[]{:S(2)}) %all-to-all-start.2) | async-done | bytes 1048608 | tf_op jit(solution)/shard_map/all_to_all | solution.py:220
  91.5 62.0 %while.34 = (s32[]{:T(128)}, f32[1,8,256]{2,1,0:T(8,128)S(1)}, f32[1,8,256]{2,1,0:T(8,128)S(1)}, s32[256]{0:T(256)S(1)}, s32[4096]{0:T(1024)S(1)}, /*index=5*/bf...) while((s32[]{:T(128)}, f32[1,8,256]{2,1,0:T(8,128)S(1)}, ...), condition=%wide.region_9.11_spmd.clone, body=%wide.region_3.10_spmd.clone.sunk | while | flops 277492992 | bytes 9574721 | solution.py:164
  99.3 3.1 gather_fusion
  107.1 3.1 gather_fusion
  114.8 3.1 gather_fusion
  156.6 123.3 %while.35 = (s32[]{:T(128)}, f32[256,1,8,128]{0,3,2,1:T(8,128)S(1)}, f32[4096,128]{1,0:T(8,128)}, f32[4096,128]{1,0:T(8,128)}, s32[256]{0:T(256)S(1)}, /*index=5...) while((s32[]{:T(128)}, ...), condition=%wide.region_15.17_spmd.clone, body=%wide.region_11.16_spmd.clone.sunk | while | flops 1353721088 | bytes 24959408 | solution.py:175
  161.5 10.5 %conditional.7 = ((f32[256,1,8,128]{0,3,2,1:T(8,128)S(1)}, f32[4096,128]{1,0:T(8,128)}, f32[4096,128]{1,0:T(8,128)})) conditional(s32[]{:T(128)} %convert_element_type.171, (f32[256,1,8,128]{0,3,2,1:T(8,128)S(1)}, f32[4096,128]{1,0:T(8,128)}, f32[4096,128]{1,0:T(8,128)}) %tuple.119, (s32[]{:T(128)}, bf16[4096,128]{1,0:T(8,128)(2,1)}, ...), branch_computations={%region_13.14_spmd, %region_14.15_spmd} | conditional | flops 1353056256 | bytes 24797270 | solution.py:140
  176.9 10.5 %conditional.7 = ((f32[256,1,8,128]{0,3,2,1:T(8,128)S(1)}, f32[4096,128]{1,0:T(8,128)}, f32[4096,128]{1,0:T(8,128)})) conditional(s32[]{:T(128)} %convert_element_type.171, (f32[256,1,8,128]{0,3,2,1:T(8,128)S(1)}, f32[4096,128]{1,0:T(8,128)}, f32[4096,128]{1,0:T(8,128)}) %tuple.119, (s32[]{:T(128)}, bf16[4096,128]{1,0:T(8,128)(2,1)}, ...), branch_computations={%region_13.14_spmd, %region_14.15_spmd} | conditional | flops 1353056256 | bytes 24797270 | solution.py:140
  192.4 10.5 %conditional.7 = ((f32[256,1,8,128]{0,3,2,1:T(8,128)S(1)}, f32[4096,128]{1,0:T(8,128)}, f32[4096,128]{1,0:T(8,128)})) conditional(s32[]{:T(128)} %convert_element_type.171, (f32[256,1,8,128]{0,3,2,1:T(8,128)S(1)}, f32[4096,128]{1,0:T(8,128)}, f32[4096,128]{1,0:T(8,128)}) %tuple.119, (s32[]{:T(128)}, bf16[4096,128]{1,0:T(8,128)(2,1)}, ...), branch_computations={%region_13.14_spmd, %region_14.15_spmd} | conditional | flops 1353056256 | bytes 24797270 | solution.py:140
  207.8 10.5 %conditional.7 = ((f32[256,1,8,128]{0,3,2,1:T(8,128)S(1)}, f32[4096,128]{1,0:T(8,128)}, f32[4096,128]{1,0:T(8,128)})) conditional(s32[]{:T(128)} %convert_element_type.171, (f32[256,1,8,128]{0,3,2,1:T(8,128)S(1)}, f32[4096,128]{1,0:T(8,128)}, f32[4096,128]{1,0:T(8,128)}) %tuple.119, (s32[]{:T(128)}, bf16[4096,128]{1,0:T(8,128)(2,1)}, ...), branch_computations={%region_13.14_spmd, %region_14.15_spmd} | conditional | flops 1353056256 | bytes 24797270 | solution.py:140
  223.2 10.5 %conditional.7 = ((f32[256,1,8,128]{0,3,2,1:T(8,128)S(1)}, f32[4096,128]{1,0:T(8,128)}, f32[4096,128]{1,0:T(8,128)})) conditional(s32[]{:T(128)} %convert_element_type.171, (f32[256,1,8,128]{0,3,2,1:T(8,128)S(1)}, f32[4096,128]{1,0:T(8,128)}, f32[4096,128]{1,0:T(8,128)}) %tuple.119, (s32[]{:T(128)}, bf16[4096,128]{1,0:T(8,128)(2,1)}, ...), branch_computations={%region_13.14_spmd, %region_14.15_spmd} | conditional | flops 1353056256 | bytes 24797270 | solution.py:140
  238.6 10.5 %conditional.7 = ((f32[256,1,8,128]{0,3,2,1:T(8,128)S(1)}, f32[4096,128]{1,0:T(8,128)}, f32[4096,128]{1,0:T(8,128)})) conditional(s32[]{:T(128)} %convert_element_type.171, (f32[256,1,8,128]{0,3,2,1:T(8,128)S(1)}, f32[4096,128]{1,0:T(8,128)}, f32[4096,128]{1,0:T(8,128)}) %tuple.119, (s32[]{:T(128)}, bf16[4096,128]{1,0:T(8,128)(2,1)}, ...), branch_computations={%region_13.14_spmd, %region_14.15_spmd} | conditional | flops 1353056256 | bytes 24797270 | solution.py:140
  254.0 10.5 %conditional.7 = ((f32[256,1,8,128]{0,3,2,1:T(8,128)S(1)}, f32[4096,128]{1,0:T(8,128)}, f32[4096,128]{1,0:T(8,128)})) conditional(s32[]{:T(128)} %convert_element_type.171, (f32[256,1,8,128]{0,3,2,1:T(8,128)S(1)}, f32[4096,128]{1,0:T(8,128)}, f32[4096,128]{1,0:T(8,128)}) %tuple.119, (s32[]{:T(128)}, bf16[4096,128]{1,0:T(8,128)(2,1)}, ...), branch_computations={%region_13.14_spmd, %region_14.15_spmd} | conditional | flops 1353056256 | bytes 24797270 | solution.py:140
  269.4 10.5 %conditional.7 = ((f32[256,1,8,128]{0,3,2,1:T(8,128)S(1)}, f32[4096,128]{1,0:T(8,128)}, f32[4096,128]{1,0:T(8,128)})) conditional(s32[]{:T(128)} %convert_element_type.171, (f32[256,1,8,128]{0,3,2,1:T(8,128)S(1)}, f32[4096,128]{1,0:T(8,128)}, f32[4096,128]{1,0:T(8,128)}) %tuple.119, (s32[]{:T(128)}, bf16[4096,128]{1,0:T(8,128)(2,1)}, ...), branch_computations={%region_13.14_spmd, %region_14.15_spmd} | conditional | flops 1353056256 | bytes 24797270 | solution.py:140
  283.0 10.5 %convolution_convert_fusion.6 = bf16[8192,1024]{1,0:T(8,128)(2,1)} fusion(bf16[1,256,8192]{2,1,0:T(8,128)(2,1)} %param.18, bf16[1,256,1024]{2,1,0:T(8,128)(2,1)S(1)} %copy-done.2), kind=kOutput, calls=%fused_computation.74 | convolution fusion | flops 4303355904 | bytes 21495808 | tf_op jit(solution)/shard_map/dot_general | solution.py:242
  297.4 57.0 %reduce-scatter.4.cloned.1.call-done = bf16[256,128]{1,0:T(8,128)(2,1)} async-done(((bf16[4096,128]{1,0:T(8,128)(2,1)}), bf16[256,128]{1,0:T(8,128)(2,1)}) %reduce-scatter.4.cloned.1.call-update) | async-done | bytes 65552 | tf_op jit(solution)/shard_map/reduce_scatter | solution.py:181
  355.8 117.3 %reduce-scatter.8.cloned.1.call-done = bf16[256,1024]{1,0:T(8,128)(2,1)} async-done(((bf16[8192,1024]{1,0:T(8,128)(2,1)}), bf16[256,1024]{1,0:T(8,128)(2,1)}) %reduce-scatter.8.cloned.1.call-update) | async-done | bytes 524304 | tf_op jit(solution)/shard_map/reduce_scatter | solution.py:241
  475.3 73.9 %reduce-scatter.6.cloned.1.call-done = bf16[256,128]{1,0:T(8,128)(2,1)} async-done(((bf16[4096,128]{1,0:T(8,128)(2,1)}), bf16[256,128]{1,0:T(8,128)(2,1)}) %reduce-scatter.6.cloned.1.call-update) | async-done | bytes 65552 | tf_op jit(solution)/shard_map/reduce_scatter | solution.py:184
  (286 shorter events, 221.8 us)
Async XLA Ops:
  7.2 84.3 %all-gather.5.cloned.1.call-start = ((), (), s32[]{:S(2)}) async-start(), calls=%async_computation.9 | async-start | bytes 1114112 | tf_op jit(solution)/shard_map/all_gather | solution.py:154
  7.9 11.8 %copy-start.5 = (s32[1,256]{1,0:T(1,128)S(1)}, s32[1,256]{1,0:T(1,128)}, u32[]{:S(2)}) copy-start(s32[1,256]{1,0:T(1,128)} %param.25) | copy-start | bytes 3076
  19.4 10.4 %copy-start.3 = (bf16[1,256,1024]{2,1,0:T(8,128)(2,1)S(1)}, bf16[1,256,1024]{2,1,0:T(8,128)(2,1)}, u32[]{:S(2)}) copy-start(bf16[1,256,1024]{2,1,0:T(8,128)(2,1)} %param.20) | copy-start | bytes 1572868
  21.8 29.1 %copy-start.1 = (bf16[1,256,1024]{2,1,0:T(8,128)(2,1)S(1)}, bf16[1,256,1024]{2,1,0:T(8,128)(2,1)}, u32[]{:S(2)}) copy-start(bf16[1,256,1024]{2,1,0:T(8,128)(2,1)} %param.23) | copy-start | bytes 1572868
  21.8 25.2 %all-to-all-start.1 = ((bf16[16,32,1024]{2,1,0:T(8,128)(2,1)}), bf16[16,32,1024]{2,1,0:T(8,128)(2,1)S(1)}, u32[]{:S(2)}, u32[]{:S(2)}) async-start(bf16[16,32,1024]{2,1,0:T(8,128)(2,1)} %reshape.279), calls=%async_computation.1 | async-start | bytes 2097152 | tf_op jit(solution)/shard_map/all_to_all | solution.py:213
  29.1 124.5 %all-gather.7.cloned.1.call-start = ((), (), s32[]{:S(2)}) async-start(), calls=%async_computation.10 | async-start | bytes 1114112 | tf_op jit(solution)/shard_map/all_gather | solution.py:155
  31.8 42.0 %copy-start = (s32[1,4096]{1,0:T(1,128)S(1)}, s32[1,4096]{1,0:T(1,128)}, u32[]{:S(2)}) copy-start(s32[1,4096]{1,0:T(1,128)} %param.24) | copy-start | bytes 49156
  47.0 22.2 %all-to-all-start = ((bf16[16,32,1024]{2,1,0:T(8,128)(2,1)}), bf16[16,32,1024]{2,1,0:T(8,128)(2,1)S(1)}, u32[]{:S(2)}, u32[]{:S(2)}) async-start(bf16[16,32,1024]{2,1,0:T(8,128)(2,1)} %reshape.276), calls=%async_computation | async-start | bytes 2097152 | tf_op jit(solution)/shard_map/all_to_all | solution.py:206
  69.2 19.8 %all-to-all-start.2 = ((bf16[16,32,1024]{2,1,0:T(8,128)(2,1)}), bf16[16,32,1024]{2,1,0:T(8,128)(2,1)}, u32[]{:S(2)}, u32[]{:S(2)}) async-start(bf16[16,32,1024]{2,1,0:T(8,128)(2,1)} %reshape.281), calls=%async_computation.2 | async-start | bytes 2097152 | tf_op jit(solution)/shard_map/all_to_all | solution.py:220
  73.5 280.8 %reduce-scatter.4.cloned.1.call-start = ((), (), s32[]{:S(2)}) async-start(), calls=%async_computation.6 | async-start | bytes 1114112 | tf_op jit(solution)/shard_map/reduce_scatter | solution.py:181
  153.5 3.1 copy-start.4
  279.9 3.0 copy-start.2
  282.7 190.5 %reduce-scatter.8.cloned.1.call-start = ((), (), s32[]{:S(2)}) async-start(), calls=%async_computation.8 | async-start | bytes 17301504 | tf_op jit(solution)/shard_map/reduce_scatter | solution.py:241
  293.5 255.7 %reduce-scatter.6.cloned.1.call-start = ((), (), s32[]{:S(2)}) async-start(), calls=%async_computation.7 | async-start | bytes 1114112 | tf_op jit(solution)/shard_map/reduce_scatter | solution.py:184
Sparse Core Ops, SparseCore 0:
  10.1 57.6 all-gather.4
  70.0 45.4 all-gather.6
  282.8 71.5 reduce-scatter.3
  358.6 114.4 reduce-scatter.7
  477.1 72.0 reduce-scatter.5
where the time goes:
time: 558 us; the launch traced here: 556 us
  waiting for transfers between devices  285 us (51%)
  matrix products  125 us (22%)
  local copies, waits for them, and re-layouts  69.1 us (12%)
  other arithmetic  35.1 us (6%)
  starting transfers between devices  15.8 us (3%)
  between operations  14 us (3%)
  loops' own time  11.7 us (2%)
    reduce_scatter x1, waiting for transfers between devices, on_device(): lax.psum_scatter(lax.dot_general(grad_rows, out_rows, (((0,), (0,)), ((),...  117 us
    reduce_scatter x1, waiting for transfers between devices, reduce_partials(): lax.psum_scatter(value_acc.astype(jnp.bfloat16), 'ctx', scatter_dimension...  73.9 us
    reduce_scatter x1, waiting for transfers between devices, reduce_partials(): lax.psum_scatter(key_acc.astype(jnp.bfloat16), 'ctx', scatter_dimension=0...  57 us
    gather x16, local copies, waits for them, and re-layouts, pair_mask(): key_doc = jnp.take(doc_row, jnp.clip(key_pos, 0, doc_row.shape[0] - 1))  50.3 us
    dot_general x16, matrix products, scores_of(): jnp.einsum('rkgd,nkd->kgrn', query_heads, key_heads, preferred_element_ty...  26.4 us
    dot_general x8, matrix products, grad_update(): jnp.einsum('kgrn,rkgd->nkd', probs_low, grad_heads, preferred_element_typ...  22.3 us
    dot_general x8, matrix products, grad_update(): jnp.einsum('kgrn,rkgd->nkd', score_grad, query_heads, preferred_element_t...  19.1 us
    dot_general x8, matrix products, grad_update(): jnp.einsum('rkgd,nkd->kgrn', grad_heads, value_heads, preferred_element_t...  18.2 us
  transfers between devices with their start and end apart: 8, of which 6 were waited for; matrix products, arithmetic and copies ran while one was open for 19% of the time, Pallas kernels for 0%

commit v1 on v0

v1 whole, which is shorter than its diff:
```python
import math

import jax
import jax.numpy as jnp
from jax import lax
from jax.experimental import pallas as pl
from jax.experimental.pallas import tpu as pltpu
from jax.sharding import PartitionSpec as P

HEAD = 128
CAP = 2
SIDE = 4
BACK = 4
RUN = 256
BLK = 256
COLS = 256
NEG = -1e30
MIB = 1024 * 1024
NT = (((1,), (1,)), ((), ()))
TN = (((0,), (0,)), ((), ()))


def grid_shift(dx, dy):
    return [
        (x * SIDE + y, ((x + dx) % SIDE) * SIDE + (y + dy) % SIDE)
        for x in range(SIDE)
        for y in range(SIDE)
    ]


def run_shift(k, parties):
    return [(i, (i + k) % parties) for i in range(parties)]


XP, XM, YP, YM = (1, 0), (-1, 0), (0, 1), (0, -1)


def hop(value, way):
    return lax.ppermute(value, "ctx", grid_shift(*way))


def swap_cores(value):
    return lax.ppermute(value, "dp", [(0, 1), (1, 0)])


def pick_kernel(core_ref, in_ref, out_ref):
    out_ref[...] = in_ref[...]


def other_half(grad_rows, core):
    tokens, width = grad_rows.shape
    return pl.pallas_call(
        pick_kernel,
        grid_spec=pltpu.PrefetchScalarGridSpec(
            num_scalar_prefetch=1,
            grid=(width // (2 * BLK),),
            in_specs=[pl.BlockSpec((tokens, BLK), lambda i, core_ref: (0, 2 * i + 1 - core_ref[0]))],
            out_specs=pl.BlockSpec((tokens, BLK), lambda i, core_ref: (0, i)),
        ),
        out_shape=jax.ShapeDtypeStruct((tokens, width // 2), grad_rows.dtype),
        cost_estimate=pl.CostEstimate(
            flops=0, bytes_accessed=2 * tokens * width, transcendentals=0
        ),
        name="other_half",
    )(core.reshape(1), grad_rows)


def pieces(table, core, grads, outs, specs, steps, dtype, joined=False, name="pieces"):
    grad_own, grad_rec = grads
    out_own, out_rec = outs
    tokens = out_own.shape[0]
    flat = jnp.concatenate([jnp.stack([jnp.int32(0) + v for v in row]) for row in table])
    flat = jnp.concatenate([flat, core.reshape(1)]).astype(jnp.int32)
    core_at = len(table) * steps
    in_specs, operands = [], []
    for row, _, _ in specs:
        in_specs.append(
            pl.BlockSpec((tokens, BLK), lambda j, t, row=row: (0, 2 * t[row * steps + j] + t[core_at]))
        )
        operands.append(grad_own)
        in_specs.append(pl.BlockSpec((tokens, BLK), lambda j, t, row=row: (0, t[row * steps + j])))
        operands.append(grad_rec)
    for value in (out_own, out_rec):
        in_specs.append(pl.BlockSpec(value.shape, lambda j, t: (0, 0)))
        operands.append(value)
    for _, _, arrived in specs:
        for value, row in arrived:
            in_specs.append(
                pl.BlockSpec((BLK, COLS), lambda j, t, row=row: (t[row * steps + j], 0))
            )
            operands.append(value)
    count = len(specs)

    def kernel(table_ref, *refs):
        ins, results = refs[: len(operands)], refs[len(operands) :]
        own_ref, rec_ref = ins[2 * count], ins[2 * count + 1]
        at = 2 * count + 2
        for n, (_, col, arrived) in enumerate(specs):
            total = lax.dot_general(
                ins[2 * n][...],
                own_ref[:, col : col + COLS],
                TN,
                preferred_element_type=jnp.float32,
            )
            total = total + lax.dot_general(
                ins[2 * n + 1][...],
                rec_ref[:, col : col + COLS],
                TN,
                preferred_element_type=jnp.float32,
            )
            for _ in arrived:
                total = total + ins[at][...].astype(jnp.float32)
                at += 1
            if joined:
                results[0][:, col : col + COLS] = total.astype(dtype)
            else:
                results[n][...] = total.astype(dtype)

    if joined:
        out_specs = [pl.BlockSpec((BLK, count * COLS), lambda j, t: (j, 0))]
        out_shape = [jax.ShapeDtypeStruct((steps * BLK, count * COLS), dtype)]
    else:
        out_specs = [pl.BlockSpec((BLK, COLS), lambda j, t: (j, 0))] * count
        out_shape = [jax.ShapeDtypeStruct((steps * BLK, COLS), dtype)] * count
    return pl.pallas_call(
        kernel,
        grid_spec=pltpu.PrefetchScalarGridSpec(
            num_scalar_prefetch=1, grid=(steps,), in_specs=in_specs, out_specs=out_specs
        ),
        out_shape=out_shape,
        compiler_params=pltpu.CompilerParams(vmem_limit_bytes=32 * MIB),
        cost_estimate=pl.CostEstimate(
            flops=4 * count * steps * tokens * BLK * COLS,
            bytes_accessed=count * steps * (4 * tokens * BLK + 4 * BLK * COLS) + 4 * out_own.size,
            transcendentals=0,
        ),
        name=name,
    )(flat, *operands)


def weight_gradient(grad_rows, out_rows, x, y, core):
    grads = (grad_rows, swap_cores(other_half(grad_rows, core)))
    outs = (out_rows, swap_cores(out_rows))
    four = range(SIDE)
    xa, xb, ya, yb = 0, COLS, 2 * COLS, 3 * COLS

    def along(dx):
        return [((x + dx) % SIDE) * SIDE + j for j in four]

    def across(dy):
        return [j * SIDE + (y + dy) % SIDE for j in four]

    def make(name, table, specs, steps):
        return pieces(table, core, grads, outs, specs, steps, jnp.bfloat16, name=name)

    far = make(
        "far",
        [along(2), across(2)],
        [(0, xa, []), (0, xb, []), (1, ya, []), (1, yb, [])],
        SIDE,
    )
    far = [hop(v, w) for v, w in zip(far, (XP, XM, YP, YM))]
    sides = [along(1), along(-1), across(1), across(-1)]
    near = make("near", sides, [(0, xb, []), (1, xa, []), (2, yb, []), (3, ya, [])], SIDE)
    near = [hop(v, w) for v, w in zip(near, (XP, XM, YP, YM))]
    both = make(
        "both",
        sides + [list(four)],
        [
            (0, xa, [(far[0], 4)]),
            (1, xb, [(far[1], 4)]),
            (2, ya, [(far[2], 4)]),
            (3, yb, [(far[3], 4)]),
        ],
        SIDE,
    )
    both = [hop(v, w) for v, w in zip(both, (XP, XM, YP, YM))]
    got_xa = lambda row: [(both[0], row), (near[1], row)]
    got_xb = lambda row: [(near[0], row), (both[1], row)]
    got_ya = lambda row: [(both[2], row), (near[3], row)]
    got_yb = lambda row: [(near[2], row), (both[3], row)]

    def block(dx, dy):
        return ((x + dx) % SIDE) * SIDE + (y + dy) % SIDE

    y2, y1, y3 = (y + 2) % SIDE, (y + 1) % SIDE, (y + 3) % SIDE
    x2, x1, x3 = (x + 2) % SIDE, (x + 1) % SIDE, (x + 3) % SIDE
    sends = make(
        "sends",
        [[v] for v in (block(0, 2), block(2, 0), block(0, 1), block(0, 3), block(1, 0), block(3, 0))]
        + [[v] for v in (y2, x2, y1, y3, x1, x3)],
        [
            (0, xa, got_xa(6)),
            (0, xb, got_xb(6)),
            (1, ya, got_ya(7)),
            (1, yb, got_yb(7)),
            (2, xb, got_xb(8)),
            (3, xa, got_xa(9)),
            (4, yb, got_yb(10)),
            (5, ya, got_ya(11)),
        ],
        1,
    )
    sends = [hop(v, w) for v, w in zip(sends, (YP, YM, XP, XM) * 2)]
    last = make(
        "last",
        [[v] for v in (block(0, 1), block(0, 3), block(1, 0), block(3, 0), y1, y3, x1, x3)] + [[0]],
        [
            (0, xa, got_xa(4) + [(sends[0], 8)]),
            (1, xb, got_xb(5) + [(sends[1], 8)]),
            (2, ya, got_ya(6) + [(sends[2], 8)]),
            (3, yb, got_yb(7) + [(sends[3], 8)]),
        ],
        1,
    )
    last = [hop(v, w) for v, w in zip(last, (YP, YM, XP, XM))]
    return pieces(
        [[block(0, 0)], [y], [x], [0]],
        core,
        grads,
        outs,
        [
            (0, xa, got_xa(1) + [(last[0], 3), (sends[5], 3)]),
            (0, xb, got_xb(1) + [(last[1], 3), (sends[4], 3)]),
            (0, ya, got_ya(2) + [(last[2], 3), (sends[7], 3)]),
            (0, yb, got_yb(2) + [(last[3], 3), (sends[6], 3)]),
        ],
        1,
        jnp.float32,
        joined=True,
        name="total",
    )[0]


def attend_kernel(
    low_ref, pos_ref, q_ref, g_ref, o_ref, key_ref, val_ref,
    kv4, kv3, kv2, kv1,
    packed_ref, own_ref, back4, back3, back2, back1,
    bias, keys, keys_t, vals, dkey, dval,
):
    head = pl.program_id(0)
    scale = 1.0 / math.sqrt(HEAD)
    window = bias.shape[0]

    @pl.when(head == 0)
    def _():
        row = lax.broadcasted_iota(jnp.int32, bias.shape, 0)
        col = lax.broadcasted_iota(jnp.int32, bias.shape, 1)
        seen = (row >= low_ref[...]) & (row <= col + BACK * RUN)
        bias[...] = jnp.where(seen, 0.0, NEG)
        for n, ref in enumerate((kv4, kv3, kv2, kv1)):
            keys[n * RUN : (n + 1) * RUN, :] = ref[:, :HEAD]
            vals[n * RUN : (n + 1) * RUN, :] = ref[:, HEAD:]
        keys[BACK * RUN :, :] = key_ref[...]
        vals[BACK * RUN :, :] = val_ref[...]
        keys_t[...] = keys[...].T
        dkey[...] = jnp.zeros_like(dkey)
        dval[...] = jnp.zeros_like(dval)

    q = q_ref[...]
    g = g_ref[...]
    prod = g.astype(jnp.float32) * o_ref[...].astype(jnp.float32)
    row_dot = jnp.sum(prod.T, axis=0, keepdims=True)
    scores = lax.dot_general(keys[...], q, NT, preferred_element_type=jnp.float32)
    scores = scores * (scale * math.log2(math.e)) + bias[...]
    top = jnp.max(scores, axis=0, keepdims=True)
    probs = jnp.exp2(scores - top)
    probs = probs * (1.0 / jnp.sum(probs, axis=0, keepdims=True))
    dval[...] += jnp.dot(probs.astype(jnp.bfloat16), g, preferred_element_type=jnp.float32)
    prob_grad = lax.dot_general(vals[...], g, NT, preferred_element_type=jnp.float32)
    score_grad = (probs * (prob_grad - row_dot)).astype(jnp.bfloat16)
    dkey[...] += jnp.dot(score_grad, q, preferred_element_type=jnp.float32)
    dq_t = jnp.dot(keys_t[...], score_grad, preferred_element_type=jnp.float32) * scale
    dq = dq_t.T.astype(jnp.bfloat16)
    slots = lax.broadcasted_iota(jnp.int32, (packed_ref.shape[0], RUN), 0)
    select = (slots == pos_ref[...]).astype(jnp.bfloat16)
    packed_ref[...] = jnp.dot(select, dq, preferred_element_type=jnp.float32).astype(jnp.bfloat16)

    @pl.when(head == pl.num_programs(0) - 1)
    def _():
        for n, ref in enumerate((back4, back3, back2, back1)):
            rows = slice(n * RUN, (n + 1) * RUN)
            ref[:, :HEAD] = (dkey[rows, :] * scale).astype(jnp.bfloat16)
            ref[:, HEAD:] = dval[rows, :].astype(jnp.bfloat16)
        own_ref[:, :HEAD] = dkey[BACK * RUN :, :] * scale
        own_ref[:, HEAD:] = dval[BACK * RUN :, :]


def attend(low, pos, query, grad, out, key, value, earlier, slots):
    heads = query.shape[1] // HEAD
    window = (BACK + 1) * RUN
    whole = lambda shape: pl.BlockSpec(shape, lambda h: (0, 0))
    by_head = lambda rows: pl.BlockSpec((rows, HEAD), lambda h: (0, h))
    pair = (RUN, 2 * HEAD)
    return pl.pallas_call(
        attend_kernel,
        grid=(heads,),
        in_specs=[whole((1, RUN))] * 2
        + [by_head(RUN)] * 3
        + [whole((RUN, HEAD))] * 2
        + [whole(pair)] * BACK,
        out_specs=[by_head(slots), whole(pair)] + [whole(pair)] * BACK,
        out_shape=[
            jax.ShapeDtypeStruct((slots, query.shape[1]), jnp.bfloat16),
            jax.ShapeDtypeStruct(pair, jnp.float32),
        ]
        + [jax.ShapeDtypeStruct(pair, jnp.bfloat16)] * BACK,
        scratch_shapes=[
            pltpu.VMEM((window, RUN), jnp.float32),
            pltpu.VMEM((window, HEAD), jnp.bfloat16),
            pltpu.VMEM((HEAD, window), jnp.bfloat16),
            pltpu.VMEM((window, HEAD), jnp.bfloat16),
            pltpu.VMEM((window, HEAD), jnp.float32),
            pltpu.VMEM((window, HEAD), jnp.float32),
        ],
        compiler_params=pltpu.CompilerParams(vmem_limit_bytes=40 * MIB),
        cost_estimate=pl.CostEstimate(
            flops=10 * heads * RUN * window * HEAD,
            bytes_accessed=8 * MIB,
            transcendentals=heads * RUN * window,
        ),
        name="attend",
    )(low, pos, query, grad, out, key, value, *earlier)


def route_rows(slot_blocks, own_index, parties, block_rows):
    total = slot_blocks.shape[0]
    ids = jnp.arange(total, dtype=jnp.int32)
    slot_of_block = jnp.sum(
        jnp.where(slot_blocks[None, :] == ids[:, None], ids[None, :], 0), axis=1
    )
    local = jnp.arange(parties, dtype=jnp.int32)

    def place(peer, order):
        earlier = (peer[:, None] == peer[None, :]) & (order[None, :] < order[:, None])
        return peer * CAP + jnp.sum(earlier, axis=1).astype(jnp.int32)

    dest_slot = lax.dynamic_slice_in_dim(slot_of_block, own_index * parties, parties, 0)
    held = lax.dynamic_slice_in_dim(slot_blocks, own_index * parties, parties, 0)
    rows = jnp.arange(block_rows, dtype=jnp.int32)

    def spread(at):
        return (at[:, None] * block_rows + rows[None, :]).reshape(-1)

    return spread(place(dest_slot // parties, dest_slot)), spread(place(held // parties, local))


def on_device(
    grad_out, out_weight, query_states, key_states, value_tensor, attn_out, doc_ids, block_order
):
    parties = lax.axis_size("ctx")
    own_index = lax.axis_index("ctx")
    core = lax.axis_index("dp")
    x, y = own_index // SIDE, own_index % SIDE
    grad_rows, out_rows = grad_out[0], attn_out[0]
    doc_row = doc_ids[0]
    key, value = key_states[0], value_tensor[0]

    both = jnp.concatenate([key, value], axis=1)
    earlier = [lax.ppermute(both, "ctx", run_shift(k, parties)) for k in range(BACK, 0, -1)]

    weight_grad = weight_gradient(grad_rows, out_rows, x, y, core)

    attn_grad = jnp.dot(grad_rows, out_weight, preferred_element_type=jnp.float32).astype(
        jnp.bfloat16
    )
    own_docs = lax.dynamic_slice_in_dim(doc_row, own_index * RUN, RUN, 0)
    first = jnp.sum((doc_row[:, None] < own_docs[None, :]).astype(jnp.int32), axis=0)
    low = (first - (own_index - BACK) * RUN).reshape(1, RUN)
    send_rows, held_rows = route_rows(block_order[0], own_index, parties, RUN // parties)
    slots = CAP * RUN
    packed, own_kv, *back = attend(
        low,
        send_rows.reshape(1, RUN),
        query_states[0],
        attn_grad,
        out_rows,
        key,
        value,
        earlier,
        slots,
    )
    got = lax.all_to_all(
        packed.reshape(parties, slots // parties, -1), "ctx", 0, 0, tiled=True
    ).reshape(slots, -1)
    held_select = (
        held_rows[:, None] == jnp.arange(slots, dtype=jnp.int32)[None, :]
    ).astype(jnp.bfloat16)
    query_grad = jnp.dot(held_select, got, preferred_element_type=jnp.float32).astype(jnp.bfloat16)
    returned = [
        lax.ppermute(v, "ctx", run_shift(-k, parties)) for v, k in zip(back, range(BACK, 0, -1))
    ]
    kv_sum = own_kv
    for v in returned:
        kv_sum = kv_sum + v.astype(jnp.float32)
    kv_sum = kv_sum.astype(jnp.bfloat16)
    return (
        query_grad[None],
        kv_sum[None, :, :HEAD],
        kv_sum[None, :, HEAD:],
        weight_grad,
    )


def solution(mesh):
    heads = P("dp", "ctx", "tp")
    in_specs = (
        P("dp", "ctx", None),
        P(None, "tp"),
        heads,
        heads,
        heads,
        heads,
        P("dp", None),
        P("dp", None),
    )
    out_specs = (heads, heads, heads, P(("ctx", "dp"), "tp"))
    return jax.shard_map(
        on_device, mesh=mesh, in_specs=in_specs, out_specs=out_specs, check_vma=False
    )
```

time: 558 us -> 160 us (0.29)
  waiting for transfers between devices: 285 us -> 15.6 us
  matrix products: 125 us -> 14.8 us
  Pallas kernels: 0 us -> 51.8 us
  local copies, waits for them, and re-layouts: 69.1 us -> 17.5 us
  starting transfers between devices: 15.8 us -> 53.7 us
  other arithmetic: 35.1 us -> 4.51 us
  between operations: 14 us -> 0.87 us
  loops' own time: 11.7 us -> 0 us
    reduce_scatter x3 -> x0, waiting for transfers between devices: 248 us -> none  [the longest x1 117 us: on_device(): lax.psum_scatter(lax.dot_general(grad_rows, out_rows, (((0,), (0,)), ((),...]
    dot_general x55 -> x1, matrix products: 113 us -> 2.5 us  [on_device(): jnp.dot(held_select, got, preferred_element_type=jnp.float32)]
    gather x17 -> x0, local copies, waits for them, and re-layouts: 52 us -> none  [the longest x16 50.3 us: pair_mask(): key_doc = jnp.take(doc_row, jnp.clip(key_pos, 0, doc_row.shape[0] - 1))]
    pallas_call x0 -> x8, Pallas kernels: none -> 51.8 us  [the longest x6 25.1 us: pieces(): pl.pallas_call(kernel, grid_spec=pltpu.PrefetchScalarGridSpec(num_scalar_...]
    ppermute x0 -> x34, starting transfers between devices: none -> 49.4 us  [the longest x24 34.5 us: hop(): return lax.ppermute(value, 'ctx', grid_shift(*way))]
    all_to_all x3 -> x1, waiting for transfers between devices: 35.3 us -> 0.01 us  [on_device(): lax.all_to_all(packed.reshape(parties, slots // parties, -1), 'ctx', 0, 0...]
    ppermute x0 -> x34, waiting for transfers between devices: none -> 15.6 us  [the longest x4 6.72 us: on_device(): lax.ppermute(both, 'ctx', run_shift(k, parties))]
    unnamed x15 -> x42, local copies, waits for them, and re-layouts: 1.03 us -> 16.1 us
  transfers between devices with their start and end apart: 8 -> 35, of which waited for: 6 -> 8; matrix products, arithmetic and copies ran while one was open for 19% -> 13% of each run, Pallas kernels for 0% -> 24%
where the time goes in v1:
time: 160 us; the launch traced here: 159 us
  starting transfers between devices  53.7 us (34%)
  Pallas kernels  51.8 us (32%)
  local copies, waits for them, and re-layouts  17.5 us (11%)
  waiting for transfers between devices  15.6 us (10%)
  matrix products  14.8 us (9%)
  other arithmetic  4.51 us (3%)
    ppermute x24, starting transfers between devices, hop(): return lax.ppermute(value, 'ctx', grid_shift(*way))  34.5 us
    pallas_call x6, Pallas kernels, pieces(): pl.pallas_call(kernel, grid_spec=pltpu.PrefetchScalarGridSpec(num_scalar_...  25.1 us
    pallas_call x1, Pallas kernels, attend(): pl.pallas_call(attend_kernel, grid=(heads,), in_specs=[whole((1, RUN))] *...  17 us
    unnamed x42, local copies, waits for them, and re-layouts  16.1 us
    dot_general x1, matrix products, on_device(): jnp.dot(grad_rows, out_weight, preferred_element_type=jnp.float32)  12.3 us
    pallas_call x1, Pallas kernels, other_half(): pl.pallas_call(pick_kernel, grid_spec=pltpu.PrefetchScalarGridSpec(num_sc...  9.7 us
    ppermute x4, starting transfers between devices, on_device(): lax.ppermute(v, 'ctx', run_shift(-k, parties))  8.94 us
    ppermute x4, waiting for transfers between devices, on_device(): lax.ppermute(both, 'ctx', run_shift(k, parties))  6.72 us
  transfers between devices with their start and end apart: 35, of which 8 were waited for; matrix products, arithmetic and copies ran while one was open for 13% of the time, Pallas kernels for 24%

profile of v1, /device:TPU:0, one launch (start us, length us, event | category | flops | bytes accessed | tf_op | source)
XLA Modules:
  0.0 158.9 jit_solution(1102561406965933378)
XLA Ops:
  0.7 9.7 %other_half.1 = bf16[256,4096]{1,0:T(8,128)(2,1)} custom-call(s32[1]{0:T(128)} %bitcast.19.core_ref, bf16[256,8192]{1,0:T(8,128)(2,1)} %bitcast.69), custom_call_target="tpu_custom_call" | custom-call | bytes 4194304 | tf_op jit(solution)/shard_map/other_half/pallas_call | solution.py:52
  12.6 3.0 %collective-permute-start.1 = (bf16[256,256]{1,0:T(8,128)(2,1)}, bf16[256,256]{1,0:T(8,128)(2,1)}, u32[]{:S(2)}, u32[]{:S(2)}) collective-permute-start(bf16[256,256]{1,0:T(8,128)(2,1)} %pad_maximum_fusion), channel_id=1, source_target_pairs={{0,24},{8,32},{16,40},{24,48},{32,56},{40,64},{48,72},{56,80},{64,... | collective-permute-start | bytes 393224 | tf_op jit(solution)/shard_map/ppermute | solution.py:360
  15.6 12.3 %convolution_convert_fusion.1.g_ref = bf16[256,1024]{1,0:T(8,128)(2,1)} fusion(bf16[8192,1024]{1,0:T(8,128)(2,1)} %param.9, bf16[1,256,8192]{2,1,0:T(8,128)(2,1)} %param.8), kind=kOutput, calls=%fused_computation.2 | convolution fusion | flops 4295229440 | bytes 21495808 | tf_op jit(solution)/shard_map/dot_general | solution.py:364
  32.3 4.3 %far.1 = (bf16[1024,256]{1,0:T(8,128)(2,1)}, bf16[1024,256]{1,0:T(8,128)(2,1)}, bf16[1024,256]{1,0:T(8,128)(2,1)}, bf16[1024,256]{1,0:T(8,128)(2,1)}) custom-call(s32[9]{0:T(128)S(1)} %concatenate.24.table_ref, bf16[256,8192]{1,0:T(8,128)(2,1)S(1)} %bitcast.70, ...), custom_call_target="tpu_custom_call" | custom-call | flops 1073741824 | bytes 9437184 | tf_op jit(solution)/shard_map/far/pallas_call | solution.py:125
  40.2 3.2 %collective-permute-start.13 = (bf16[1024,256]{1,0:T(8,128)(2,1)}, bf16[1024,256]{1,0:T(8,128)(2,1)}, u32[]{:S(2)}, u32[]{:S(2)}) collective-permute-start(bf16[1024,256]{1,0:T(8,128)(2,1)} %get-tuple-element.43), channel_id=1, source_target_pairs={{0,24},{8,0},{16,8},{24,16},{32,56},{40,32},{48,40},{56,48},{64,88... | collective-permute-start | bytes 1572872 | tf_op jit(solution)/shard_map/ppermute | solution.py:39
  45.7 4.4 %near.1 = (bf16[1024,256]{1,0:T(8,128)(2,1)}, bf16[1024,256]{1,0:T(8,128)(2,1)}, bf16[1024,256]{1,0:T(8,128)(2,1)}, bf16[1024,256]{1,0:T(8,128)(2,1)}) custom-call(s32[17]{0:T(128)S(1)} %concatenate.25.table_ref, bf16[256,8192]{1,0:T(8,128)(2,1)S(1)} %bitcast.74, ...), custom_call_target="tpu_custom_call" | custom-call | flops 1073741824 | bytes 9437184 | tf_op jit(solution)/shard_map/near/pallas_call | solution.py:125
  57.1 2.2 %copy-done.2 = bf16[1,256,8192]{2,1,0:T(8,128)(2,1)S(1)} copy-done((bf16[1,256,8192]{2,1,0:T(8,128)(2,1)S(1)}, bf16[1,256,8192]{2,1,0:T(8,128)(2,1)}, u32[]{:S(2)}) %copy-start.2) | copy-done | bytes 4194328
  59.3 5.9 %both.1 = (bf16[1024,256]{1,0:T(8,128)(2,1)}, bf16[1024,256]{1,0:T(8,128)(2,1)}, bf16[1024,256]{1,0:T(8,128)(2,1)}, bf16[1024,256]{1,0:T(8,128)(2,1)}) custom-call(s32[21]{0:T(128)S(1)} %concatenate.23.table_ref, bf16[256,8192]{1,0:T(8,128)(2,1)S(1)} %bitcast.78, ...), custom_call_target="tpu_custom_call" | custom-call | flops 1073741824 | bytes 9437184 | tf_op jit(solution)/shard_map/both/pallas_call | solution.py:125
  65.2 6.6 %collective-permute-done.2.kv2 = bf16[256,256]{1,0:T(8,128)(2,1)S(1)} collective-permute-done((bf16[256,256]{1,0:T(8,128)(2,1)}, bf16[256,256]{1,0:T(8,128)(2,1)S(1)}, u32[]{:S(2)}, u32[]{:S(2)}) %collective-permute-start.2) | collective-permute-done | bytes 131104 | tf_op jit(solution)/shard_map/ppermute | solution.py:360
  74.2 3.2 %collective-permute-start.17 = (bf16[1024,256]{1,0:T(8,128)(2,1)}, bf16[1024,256]{1,0:T(8,128)(2,1)}, u32[]{:S(2)}, u32[]{:S(2)}) collective-permute-start(bf16[1024,256]{1,0:T(8,128)(2,1)} %get-tuple-element.47), channel_id=1, source_target_pairs={{0,96},{8,104},{16,112},{24,120},{32,0},{40,8},{48,16},{56,24},{64... | collective-permute-start | bytes 1572872 | tf_op jit(solution)/shard_map/ppermute | solution.py:39
  77.5 3.2 %collective-permute-start.21 = (bf16[1024,256]{1,0:T(8,128)(2,1)}, bf16[1024,256]{1,0:T(8,128)(2,1)}, u32[]{:S(2)}, u32[]{:S(2)}) collective-permute-start(bf16[1024,256]{1,0:T(8,128)(2,1)} %get-tuple-element.51), channel_id=1, source_target_pairs={{0,24},{8,0},{16,8},{24,16},{32,56},{40,32},{48,40},{56,48},{64,88... | collective-permute-start | bytes 1572872 | tf_op jit(solution)/shard_map/ppermute | solution.py:39
  81.6 17.0 %attend.1 = (bf16[512,1024]{1,0:T(8,128)(2,1)S(1)}, f32[256,256]{1,0:T(8,128)S(1)}, bf16[256,256]{1,0:T(8,128)(2,1)S(1)}, bf16[256,256]{1,0:T(8,128)(2,1)S(1)}, ...) custom-call(s32[1,256]{1,0:T(1,128)S(1)} %bitcast.111, s32[1,256]{1,0:T(1,128)S(1)} %add.300.pos_ref, ...), custom_call_target="tpu_custom_call" | custom-call | flops 3355443200 | bytes 8388608 | tf_op jit(solution)/shard_map/attend/pallas_call | solution.py:295
  102.2 4.3 %all-to-all-start = ((bf16[16,32,1024]{2,1,0:T(8,128)(2,1)}), bf16[16,32,1024]{2,1,0:T(8,128)(2,1)}, u32[]{:S(2)}, u32[]{:S(2)}) async-start(bf16[16,32,1024]{2,1,0:T(8,128)(2,1)} %bitcast.106), calls=%async_computation | async-start | bytes 2097152 | tf_op jit(solution)/shard_map/all_to_all | solution.py:383
  106.6 3.1 %collective-permute-start.4 = (bf16[256,256]{1,0:T(8,128)(2,1)}, bf16[256,256]{1,0:T(8,128)(2,1)}, u32[]{:S(2)}, u32[]{:S(2)}) collective-permute-start(bf16[256,256]{1,0:T(8,128)(2,1)} %copy-done.15), channel_id=1, source_target_pairs={{0,96},{8,104},{16,112},{24,120},{32,0},{40,8},{48,16},{56,24},{64... | collective-permute-start | bytes 393224 | tf_op jit(solution)/shard_map/ppermute | solution.py:391
  111.5 2.7 %collective-permute-start.6 = (bf16[256,256]{1,0:T(8,128)(2,1)}, bf16[256,256]{1,0:T(8,128)(2,1)}, u32[]{:S(2)}, u32[]{:S(2)}) collective-permute-start(bf16[256,256]{1,0:T(8,128)(2,1)} %copy-done.13), channel_id=1, source_target_pairs={{0,112},{8,120},{16,0},{24,8},{32,16},{40,24},{48,32},{56,40},{64,... | collective-permute-start | bytes 393224 | tf_op jit(solution)/shard_map/ppermute | solution.py:391
  118.2 3.7 %sends.1 = (bf16[256,256]{1,0:T(8,128)(2,1)S(1)}, bf16[256,256]{1,0:T(8,128)(2,1)S(1)}, bf16[256,256]{1,0:T(8,128)(2,1)S(1)}, bf16[256,256]{1,0:T(8,128)(2,1)S(1...) custom-call(s32[13]{0:T(128)S(1)} %concatenate.27.table_ref, ...), custom_call_target="tpu_custom_call" | custom-call | flops 536870912 | bytes 5242880 | tf_op jit(solution)/shard_map/sends/pallas_call | solution.py:125
  122.5 2.4 %collective-permute-done.4 = bf16[256,256]{1,0:T(8,128)(2,1)} collective-permute-done((bf16[256,256]{1,0:T(8,128)(2,1)}, bf16[256,256]{1,0:T(8,128)(2,1)}, u32[]{:S(2)}, u32[]{:S(2)}) %collective-permute-start.4) | collective-permute-done | bytes 131104 | tf_op jit(solution)/shard_map/ppermute | solution.py:391
  126.1 2.2 %collective-permute-done.6 = bf16[256,256]{1,0:T(8,128)(2,1)} collective-permute-done((bf16[256,256]{1,0:T(8,128)(2,1)}, bf16[256,256]{1,0:T(8,128)(2,1)}, u32[]{:S(2)}, u32[]{:S(2)}) %collective-permute-start.6) | collective-permute-done | bytes 131104 | tf_op jit(solution)/shard_map/ppermute | solution.py:391
  132.8 4.4 %collective-permute-start.27 = (bf16[256,256]{1,0:T(8,128)(2,1)S(1)}, bf16[256,256]{1,0:T(8,128)(2,1)S(1)}, u32[]{:S(2)}, u32[]{:S(2)}) collective-permute-start(bf16[256,256]{1,0:T(8,128)(2,1)S(1)} %get-tuple-element.57), channel_id=1, source_target_pairs={{0,24},{8,0},{16,8},{24,16},{32,56},{40,32},{48,40},{56,48},{64,88... | collective-permute-start | bytes 393224 | tf_op jit(solution)/shard_map/ppermute | solution.py:39
  140.0 3.2 %last.1 = (bf16[256,256]{1,0:T(8,128)(2,1)}, bf16[256,256]{1,0:T(8,128)(2,1)}, bf16[256,256]{1,0:T(8,128)(2,1)}, bf16[256,256]{1,0:T(8,128)(2,1)}) custom-call(s32[10]{0:T(128)S(1)} %concatenate.26.table_ref, bf16[256,8192]{1,0:T(8,128)(2,1)S(1)} %bitcast.90, ...), custom_call_target="tpu_custom_call" | custom-call | flops 268435456 | bytes 3145728 | tf_op jit(solution)/shard_map/last/pallas_call | solution.py:125
  143.2 3.2 %collective-permute-start.28 = (bf16[256,256]{1,0:T(8,128)(2,1)}, bf16[256,256]{1,0:T(8,128)(2,1)}, u32[]{:S(2)}, u32[]{:S(2)}) collective-permute-start(bf16[256,256]{1,0:T(8,128)(2,1)} %get-tuple-element.58), channel_id=1, source_target_pairs={{0,24},{8,0},{16,8},{24,16},{32,56},{40,32},{48,40},{56,48},{64,88... | collective-permute-start | bytes 393224 | tf_op jit(solution)/shard_map/ppermute | solution.py:39
  146.6 3.1 %collective-permute-start.32 = (bf16[256,256]{1,0:T(8,128)(2,1)}, bf16[256,256]{1,0:T(8,128)(2,1)}, u32[]{:S(2)}, u32[]{:S(2)}) collective-permute-start(bf16[256,256]{1,0:T(8,128)(2,1)} %get-tuple-element.62), channel_id=1, source_target_pairs={{0,96},{8,104},{16,112},{24,120},{32,0},{40,8},{48,16},{56,24},{64... | collective-permute-start | bytes 393224 | tf_op jit(solution)/shard_map/ppermute | solution.py:39
  149.7 2.5 %fusion = bf16[1,256,1024]{2,1,0:T(8,128)(2,1)} fusion(bf16[512,1024]{1,0:T(8,128)(2,1)} %bitcast.12, s32[256]{0:T(256)S(1)} %add.295), kind=kOutput, calls=%fused_computation.3 | convolution fusion | flops 268828672 | bytes 1573888 | tf_op jit(solution)/shard_map/dot_general | solution.py:389
  155.1 3.7 %total.1 = f32[256,1024]{1,0:T(8,128)} custom-call(s32[5]{0:T(128)S(1)} %concatenate.22.table_ref, bf16[256,8192]{1,0:T(8,128)(2,1)S(1)} %bitcast.94, bf16[256,4096]{1,0:T(8,128)(2,1)S(1)} %collective-permute-done.8.refs_1_.refs_3_.refs_5_.refs_7_.refs_9_.refs_11_.refs_13_.refs_15_, bf16[256,8192]{1,0:T(8,128)(2,1)S(1)} %bitcast.95, ...), custom_call_target="tpu_custom_call" | custom-call | flops 268435456 | bytes 3145728 | tf_op jit(solution)/shard_map/total/pallas_call | solution.py:125
  (122 shorter events, 44.4 us)
Async XLA Ops:
  10.4 19.7 %collective-permute-start.8 = (bf16[256,4096]{1,0:T(8,128)(2,1)}, bf16[256,4096]{1,0:T(8,128)(2,1)S(1)}, u32[]{:S(2)}, u32[]{:S(2)}) collective-permute-start(bf16[256,4096]{1,0:T(8,128)(2,1)} %other_half.1), channel_id=1, source_target_pairs={{0,1},{1,0},{2,3},{3,2},{4,5},{5,4},{6,7},{7,6},{8,9},{9,8},{10,11... | collective-permute-start | bytes 6291464 | tf_op jit(solution)/shard_map/ppermute | solution.py:43
  11.0 29.1 %collective-permute-start = (bf16[256,256]{1,0:T(8,128)(2,1)}, bf16[256,256]{1,0:T(8,128)(2,1)S(1)}, u32[]{:S(2)}, u32[]{:S(2)}) collective-permute-start(bf16[256,256]{1,0:T(8,128)(2,1)} %pad_maximum_fusion), channel_id=1, source_target_pairs={{0,32},{8,40},{16,48},{24,56},{32,64},{40,72},{48,80},{56,88},{64,... | collective-permute-start | bytes 393224 | tf_op jit(solution)/shard_map/ppermute | solution.py:360
  12.6 37.4 %collective-permute-start.1 = (bf16[256,256]{1,0:T(8,128)(2,1)}, bf16[256,256]{1,0:T(8,128)(2,1)}, u32[]{:S(2)}, u32[]{:S(2)}) collective-permute-start(bf16[256,256]{1,0:T(8,128)(2,1)} %pad_maximum_fusion), channel_id=1, source_target_pairs={{0,24},{8,32},{16,40},{24,48},{32,56},{40,64},{48,72},{56,80},{64,... | collective-permute-start | bytes 393224 | tf_op jit(solution)/shard_map/ppermute | solution.py:360
  15.6 14.5 %collective-permute-start.9 = (bf16[256,1024]{1,0:T(8,128)(2,1)S(1)}, bf16[256,1024]{1,0:T(8,128)(2,1)S(1)}, u32[]{:S(2)}, u32[]{:S(2)}) collective-permute-start(bf16[256,1024]{1,0:T(8,128)(2,1)S(1)} %bitcast.98), channel_id=1, source_target_pairs={{0,1},{1,0},{2,3},{3,2},{4,5},{5,4},{6,7},{7,6},{8,9},{9,8},{10,11... | collective-permute-start | bytes 1572872 | tf_op jit(solution)/shard_map/ppermute | solution.py:43
  36.6 15.9 %collective-permute-start.10 = (bf16[1024,256]{1,0:T(8,128)(2,1)}, bf16[1024,256]{1,0:T(8,128)(2,1)}, u32[]{:S(2)}, u32[]{:S(2)}) collective-permute-start(bf16[1024,256]{1,0:T(8,128)(2,1)} %get-tuple-element.40), channel_id=1, source_target_pairs={{0,32},{8,40},{16,48},{24,56},{32,64},{40,72},{48,80},{56,88},{64,... | collective-permute-start | bytes 1572872 | tf_op jit(solution)/shard_map/ppermute | solution.py:39
  38.0 14.6 %collective-permute-start.11 = (bf16[1024,256]{1,0:T(8,128)(2,1)}, bf16[1024,256]{1,0:T(8,128)(2,1)}, u32[]{:S(2)}, u32[]{:S(2)}) collective-permute-start(bf16[1024,256]{1,0:T(8,128)(2,1)} %get-tuple-element.41), channel_id=1, source_target_pairs={{0,96},{8,104},{16,112},{24,120},{32,0},{40,8},{48,16},{56,24},{64... | collective-permute-start | bytes 1572872 | tf_op jit(solution)/shard_map/ppermute | solution.py:39
  40.1 15.4 %collective-permute-start.12 = (bf16[1024,256]{1,0:T(8,128)(2,1)}, bf16[1024,256]{1,0:T(8,128)(2,1)}, u32[]{:S(2)}, u32[]{:S(2)}) collective-permute-start(bf16[1024,256]{1,0:T(8,128)(2,1)} %get-tuple-element.42), channel_id=1, source_target_pairs={{0,8},{8,16},{16,24},{24,0},{32,40},{40,48},{48,56},{56,32},{64,72... | collective-permute-start | bytes 1572872 | tf_op jit(solution)/shard_map/ppermute | solution.py:39
  40.2 15.6 %collective-permute-start.13 = (bf16[1024,256]{1,0:T(8,128)(2,1)}, bf16[1024,256]{1,0:T(8,128)(2,1)}, u32[]{:S(2)}, u32[]{:S(2)}) collective-permute-start(bf16[1024,256]{1,0:T(8,128)(2,1)} %get-tuple-element.43), channel_id=1, source_target_pairs={{0,24},{8,0},{16,8},{24,16},{32,56},{40,32},{48,40},{56,48},{64,88... | collective-permute-start | bytes 1572872 | tf_op jit(solution)/shard_map/ppermute | solution.py:39
  50.0 24.2 %collective-permute-start.15 = (bf16[1024,256]{1,0:T(8,128)(2,1)}, bf16[1024,256]{1,0:T(8,128)(2,1)}, u32[]{:S(2)}, u32[]{:S(2)}) collective-permute-start(bf16[1024,256]{1,0:T(8,128)(2,1)} %get-tuple-element.45), channel_id=1, source_target_pairs={{0,96},{8,104},{16,112},{24,120},{32,0},{40,8},{48,16},{56,24},{64... | collective-permute-start | bytes 1572872 | tf_op jit(solution)/shard_map/ppermute | solution.py:39
  52.4 25.0 %collective-permute-start.16 = (bf16[1024,256]{1,0:T(8,128)(2,1)}, bf16[1024,256]{1,0:T(8,128)(2,1)}, u32[]{:S(2)}, u32[]{:S(2)}) collective-permute-start(bf16[1024,256]{1,0:T(8,128)(2,1)} %get-tuple-element.46), channel_id=1, source_target_pairs={{0,32},{8,40},{16,48},{24,56},{32,64},{40,72},{48,80},{56,88},{64,... | collective-permute-start | bytes 1572872 | tf_op jit(solution)/shard_map/ppermute | solution.py:39
  52.7 24.8 %collective-permute-start.19 = (bf16[1024,256]{1,0:T(8,128)(2,1)}, bf16[1024,256]{1,0:T(8,128)(2,1)}, u32[]{:S(2)}, u32[]{:S(2)}) collective-permute-start(bf16[1024,256]{1,0:T(8,128)(2,1)} %get-tuple-element.49), channel_id=1, source_target_pairs={{0,24},{8,0},{16,8},{24,16},{32,56},{40,32},{48,40},{56,48},{64,88... | collective-permute-start | bytes 1572872 | tf_op jit(solution)/shard_map/ppermute | solution.py:39
  55.4 16.4 %collective-permute-start.2 = (bf16[256,256]{1,0:T(8,128)(2,1)}, bf16[256,256]{1,0:T(8,128)(2,1)S(1)}, u32[]{:S(2)}, u32[]{:S(2)}) collective-permute-start(bf16[256,256]{1,0:T(8,128)(2,1)} %pad_maximum_fusion), channel_id=1, source_target_pairs={{0,16},{8,24},{16,32},{24,40},{32,48},{40,56},{48,64},{56,72},{64,... | collective-permute-start | bytes 393224 | tf_op jit(solution)/shard_map/ppermute | solution.py:360
  55.8 18.4 %collective-permute-start.3 = (bf16[256,256]{1,0:T(8,128)(2,1)}, bf16[256,256]{1,0:T(8,128)(2,1)}, u32[]{:S(2)}, u32[]{:S(2)}) collective-permute-start(bf16[256,256]{1,0:T(8,128)(2,1)} %pad_maximum_fusion), channel_id=1, source_target_pairs={{0,8},{8,16},{16,24},{24,32},{32,40},{40,48},{48,56},{56,64},{64,7... | collective-permute-start | bytes 393224 | tf_op jit(solution)/shard_map/ppermute | solution.py:360
  72.4 34.2 %collective-permute-start.20 = (bf16[1024,256]{1,0:T(8,128)(2,1)}, bf16[1024,256]{1,0:T(8,128)(2,1)}, u32[]{:S(2)}, u32[]{:S(2)}) collective-permute-start(bf16[1024,256]{1,0:T(8,128)(2,1)} %get-tuple-element.50), channel_id=1, source_target_pairs={{0,8},{8,16},{16,24},{24,0},{32,40},{40,48},{48,56},{56,32},{64,72... | collective-permute-start | bytes 1572872 | tf_op jit(solution)/shard_map/ppermute | solution.py:39
  74.2 35.5 %collective-permute-start.14 = (bf16[1024,256]{1,0:T(8,128)(2,1)}, bf16[1024,256]{1,0:T(8,128)(2,1)}, u32[]{:S(2)}, u32[]{:S(2)}) collective-permute-start(bf16[1024,256]{1,0:T(8,128)(2,1)} %get-tuple-element.44), channel_id=1, source_target_pairs={{0,32},{8,40},{16,48},{24,56},{32,64},{40,72},{48,80},{56,88},{64,... | collective-permute-start | bytes 1572872 | tf_op jit(solution)/shard_map/ppermute | solution.py:39
  74.2 37.2 %collective-permute-start.17 = (bf16[1024,256]{1,0:T(8,128)(2,1)}, bf16[1024,256]{1,0:T(8,128)(2,1)}, u32[]{:S(2)}, u32[]{:S(2)}) collective-permute-start(bf16[1024,256]{1,0:T(8,128)(2,1)} %get-tuple-element.47), channel_id=1, source_target_pairs={{0,96},{8,104},{16,112},{24,120},{32,0},{40,8},{48,16},{56,24},{64... | collective-permute-start | bytes 1572872 | tf_op jit(solution)/shard_map/ppermute | solution.py:39
  77.5 36.7 %collective-permute-start.18 = (bf16[1024,256]{1,0:T(8,128)(2,1)}, bf16[1024,256]{1,0:T(8,128)(2,1)}, u32[]{:S(2)}, u32[]{:S(2)}) collective-permute-start(bf16[1024,256]{1,0:T(8,128)(2,1)} %get-tuple-element.48), channel_id=1, source_target_pairs={{0,8},{8,16},{16,24},{24,0},{32,40},{40,48},{48,56},{56,32},{64,72... | collective-permute-start | bytes 1572872 | tf_op jit(solution)/shard_map/ppermute | solution.py:39
  77.5 38.5 %collective-permute-start.21 = (bf16[1024,256]{1,0:T(8,128)(2,1)}, bf16[1024,256]{1,0:T(8,128)(2,1)}, u32[]{:S(2)}, u32[]{:S(2)}) collective-permute-start(bf16[1024,256]{1,0:T(8,128)(2,1)} %get-tuple-element.51), channel_id=1, source_target_pairs={{0,24},{8,0},{16,8},{24,16},{32,56},{40,32},{48,40},{56,48},{64,88... | collective-permute-start | bytes 1572872 | tf_op jit(solution)/shard_map/ppermute | solution.py:39
  102.2 47.4 %all-to-all-start = ((bf16[16,32,1024]{2,1,0:T(8,128)(2,1)}), bf16[16,32,1024]{2,1,0:T(8,128)(2,1)}, u32[]{:S(2)}, u32[]{:S(2)}) async-start(bf16[16,32,1024]{2,1,0:T(8,128)(2,1)} %bitcast.106), calls=%async_computation | async-start | bytes 2097152 | tf_op jit(solution)/shard_map/all_to_all | solution.py:383
  106.6 18.2 %collective-permute-start.4 = (bf16[256,256]{1,0:T(8,128)(2,1)}, bf16[256,256]{1,0:T(8,128)(2,1)}, u32[]{:S(2)}, u32[]{:S(2)}) collective-permute-start(bf16[256,256]{1,0:T(8,128)(2,1)} %copy-done.15), channel_id=1, source_target_pairs={{0,96},{8,104},{16,112},{24,120},{32,0},{40,8},{48,16},{56,24},{64... | collective-permute-start | bytes 393224 | tf_op jit(solution)/shard_map/ppermute | solution.py:391
  109.7 16.4 %collective-permute-start.5 = (bf16[256,256]{1,0:T(8,128)(2,1)}, bf16[256,256]{1,0:T(8,128)(2,1)}, u32[]{:S(2)}, u32[]{:S(2)}) collective-permute-start(bf16[256,256]{1,0:T(8,128)(2,1)} %copy-done.14), channel_id=1, source_target_pairs={{0,104},{8,112},{16,120},{24,0},{32,8},{40,16},{48,24},{56,32},{64... | collective-permute-start | bytes 393224 | tf_op jit(solution)/shard_map/ppermute | solution.py:391
  111.5 16.9 %collective-permute-start.6 = (bf16[256,256]{1,0:T(8,128)(2,1)}, bf16[256,256]{1,0:T(8,128)(2,1)}, u32[]{:S(2)}, u32[]{:S(2)}) collective-permute-start(bf16[256,256]{1,0:T(8,128)(2,1)} %copy-done.13), channel_id=1, source_target_pairs={{0,112},{8,120},{16,0},{24,8},{32,16},{40,24},{48,32},{56,40},{64,... | collective-permute-start | bytes 393224 | tf_op jit(solution)/shard_map/ppermute | solution.py:391
  114.1 14.2 %collective-permute-start.7 = (bf16[256,256]{1,0:T(8,128)(2,1)}, bf16[256,256]{1,0:T(8,128)(2,1)}, u32[]{:S(2)}, u32[]{:S(2)}) collective-permute-start(bf16[256,256]{1,0:T(8,128)(2,1)} %copy-done.12), channel_id=1, source_target_pairs={{0,120},{8,0},{16,8},{24,16},{32,24},{40,32},{48,40},{56,48},{64,5... | collective-permute-start | bytes 393224 | tf_op jit(solution)/shard_map/ppermute | solution.py:391
  121.9 15.3 %collective-permute-start.22 = (bf16[256,256]{1,0:T(8,128)(2,1)S(1)}, bf16[256,256]{1,0:T(8,128)(2,1)S(1)}, u32[]{:S(2)}, u32[]{:S(2)}) collective-permute-start(bf16[256,256]{1,0:T(8,128)(2,1)S(1)} %get-tuple-element.52), channel_id=1, source_target_pairs={{0,8},{8,16},{16,24},{24,0},{32,40},{40,48},{48,56},{56,32},{64,72... | collective-permute-start | bytes 393224 | tf_op jit(solution)/shard_map/ppermute | solution.py:39
  (32 other events, 253.5 us)

commit v2 on v1

v2 whole, which is shorter than its diff:
```python
import math

import jax
import jax.numpy as jnp
from jax import lax
from jax.experimental import pallas as pl
from jax.experimental.pallas import tpu as pltpu
from jax.sharding import PartitionSpec as P

HEAD = 128
CAP = 2
SIDE = 4
BACK = 4
RUN = 256
BLK = 256
TILE = 128
SEEN = BACK * RUN + TILE
CHUNK = 384
STACK = 2
VMEM = 56 * 1024 * 1024
WIDE = 512
NEG = -1e30
MIB = 1024 * 1024
NT = (((1,), (1,)), ((), ()))
TN = (((0,), (0,)), ((), ()))


def run_shift(k, parties):
    return [(i, (i + k) % parties) for i in range(parties)]


def axis_shift(k, second):
    pairs = []
    for x in range(SIDE):
        for y in range(SIDE):
            for core in range(2):
                along_x = (core == 0) != second
                to_x, to_y = ((x + k) % SIDE, y) if along_x else (x, (y + k) % SIDE)
                pairs.append(((x * SIDE + y) * 2 + core, (to_x * SIDE + to_y) * 2 + core))
    return pairs


def hop(value, k, second=False):
    return lax.ppermute(value, ("ctx", "dp"), axis_shift(k, second))


def swap_cores(value):
    return lax.ppermute(value, "dp", [(0, 1), (1, 0)])


def params():
    return pltpu.CompilerParams(vmem_limit_bytes=VMEM)


def cost(flops, moved, exps=0):
    return pl.CostEstimate(flops=flops, bytes_accessed=moved, transcendentals=exps)


def pick_kernel(core_ref, in_ref, out_ref, sems):
    other = 1 - core_ref[0]
    copies = []
    for i in range(out_ref.shape[1] // BLK):
        start = pl.multiple_of((2 * i + other) * BLK, BLK)
        copies.append(
            pltpu.make_async_copy(
                in_ref.at[:, pl.ds(start, BLK)], out_ref.at[:, i * BLK : (i + 1) * BLK], sems.at[i]
            )
        )
    for copy in copies:
        copy.start()
    for copy in copies:
        copy.wait()


def other_half(grad_rows, core):
    tokens, width = grad_rows.shape
    return pl.pallas_call(
        pick_kernel,
        in_specs=[pl.BlockSpec(memory_space=pltpu.SMEM), pl.BlockSpec(memory_space=pl.ANY)],
        out_specs=pl.BlockSpec(memory_space=pltpu.VMEM),
        out_shape=jax.ShapeDtypeStruct((tokens, width // 2), grad_rows.dtype),
        scratch_shapes=[pltpu.SemaphoreType.DMA((width // (2 * BLK),))],
        compiler_params=params(),
        cost_estimate=cost(0, 2 * tokens * width),
        name="other_half",
    )(core.reshape(1), grad_rows)


def project_kernel(grad_ref, weight_ref, out_ref, grads, weights, grad_sems, weight_sems):
    slabs = grad_sems.shape[0]
    depth = weight_ref.shape[0] // slabs
    copies = []
    for i in range(slabs):
        part = slice(i * depth, (i + 1) * depth)
        copies.append(
            (
                pltpu.make_async_copy(grad_ref.at[:, part], grads.at[:, part], grad_sems.at[i]),
                pltpu.make_async_copy(weight_ref.at[part], weights.at[part], weight_sems.at[i]),
            )
        )
    for pair in copies:
        for copy in pair:
            copy.start()
    total = None
    for i, pair in enumerate(copies):
        for copy in pair:
            copy.wait()
        part = slice(i * depth, (i + 1) * depth)
        addend = jnp.dot(grads[:, part], weights[part, :], preferred_element_type=jnp.float32)
        total = addend if total is None else total + addend
    out_ref[...] = total.astype(out_ref.dtype)


def project(grad_rows, weight):
    rows, depth = grad_rows.shape
    cols = weight.shape[1]
    slabs = 8
    return pl.pallas_call(
        project_kernel,
        in_specs=[pl.BlockSpec(memory_space=pl.ANY)] * 2,
        out_specs=pl.BlockSpec(memory_space=pltpu.VMEM),
        out_shape=jax.ShapeDtypeStruct((rows, cols), jnp.bfloat16),
        scratch_shapes=[
            pltpu.VMEM(grad_rows.shape, grad_rows.dtype),
            pltpu.VMEM(weight.shape, weight.dtype),
            pltpu.SemaphoreType.DMA((slabs,)),
            pltpu.SemaphoreType.DMA((slabs,)),
        ],
        compiler_params=params(),
        cost_estimate=cost(2 * rows * depth * cols, 2 * depth * (rows + cols)),
        name="project",
    )(grad_rows, weight)


def block_table(x, y, core):
    first, second = jnp.where(core == 0, x, y), jnp.where(core == 0, y, x)
    step_first, step_second = jnp.where(core == 0, SIDE, 1), jnp.where(core == 0, 1, SIDE)
    offsets = jnp.arange(SIDE, dtype=jnp.int32)
    blocks = ((first + offsets[:, None]) % SIDE) * step_first + offsets[None, :] * step_second
    order = (second + jnp.array([2, 1, 3, 0], jnp.int32)) % SIDE
    table = jnp.concatenate([blocks.reshape(-1), order, core.reshape(1)])
    return table.astype(jnp.int32)


ORDER, CORE = SIDE * SIDE, SIDE * SIDE + SIDE


def piece_kernel(plan, arrived_count, out_count, blocks, *refs):
    grad_own, grad_rec, out_own, out_rec = refs[:4]
    arrived_refs = refs[4 : 4 + arrived_count]
    refs = refs[-(out_count + 6) :] if arrived_count else refs[-(out_count + 5) :]
    results = refs[:out_count]
    if arrived_count:
        outs, grads, held, sent, in_sems, out_sems = refs[out_count:]
    else:
        outs, grads, sent, in_sems, out_sems = refs[out_count:]
    tokens = out_own.shape[0]
    core = blocks[CORE]
    taken = 0

    def load(source, target):
        nonlocal taken
        copy = pltpu.make_async_copy(source, target, in_sems.at[taken])
        taken += 1
        copy.start()
        return copy

    shared = [load(out_own, outs.at[:tokens]), load(out_rec, outs.at[tokens:])]
    loads, slot = [], 0
    for n, (at, parts) in enumerate(plan):
        block = blocks[at] if isinstance(at, int) else blocks[blocks[at[0]]]
        own = pl.multiple_of((2 * block + core) * BLK, BLK)
        rec = pl.multiple_of(block * BLK, BLK)
        copies = [
            load(grad_own.at[:, pl.ds(own, BLK)], grads.at[n, :tokens]),
            load(grad_rec.at[:, pl.ds(rec, BLK)], grads.at[n, tokens:]),
        ]
        slots = []
        for _, arrived, _, _, _ in parts:
            mine = []
            for which, row, col in arrived:
                first = row if isinstance(row, int) else blocks[row[0]]
                source = arrived_refs[which].at[
                    pl.ds(pl.multiple_of(first * BLK, BLK), BLK), col : col + WIDE
                ]
                copies.append(load(source, held.at[slot]))
                mine.append(slot)
                slot += 1
            slots.append(mine)
        loads.append((copies, slots))
    for copy in shared:
        copy.wait()
    stores = []
    for n, (_, parts) in enumerate(plan):
        copies, slots = loads[n]
        for copy in copies:
            copy.wait()
        for (col, _, out, row, out_col), mine in zip(parts, slots):
            total = lax.dot_general(
                grads[n], outs[:, col : col + WIDE], TN, preferred_element_type=jnp.float32
            )
            for k in mine:
                total = total + held[k].astype(jnp.float32)
            k = len(stores)
            sent[k] = total.astype(sent.dtype)
            copy = pltpu.make_async_copy(
                sent.at[k],
                results[out].at[row : row + BLK, out_col : out_col + WIDE],
                out_sems.at[k],
            )
            copy.start()
            stores.append(copy)
    for copy in stores:
        copy.wait()


def pieces(name, table, grads, outs, plan, arrived, out_shapes, after=()):
    tokens, cols = outs[0].shape
    parts = [part for _, each in plan for part in each]
    held = sum(len(part[1]) for part in parts)
    scratch = [
        pltpu.VMEM((2 * tokens, cols), jnp.bfloat16),
        pltpu.VMEM((len(plan), 2 * tokens, BLK), jnp.bfloat16),
    ]
    if held:
        scratch.append(pltpu.VMEM((held, BLK, WIDE), jnp.bfloat16))
    scratch += [
        pltpu.VMEM((len(parts), BLK, WIDE), jnp.bfloat16),
        pltpu.SemaphoreType.DMA((2 + 2 * len(plan) + held,)),
        pltpu.SemaphoreType.DMA((len(parts),)),
    ]
    operands = [*grads, *outs, *arrived, *after]
    return pl.pallas_call(
        lambda *refs: piece_kernel(plan, len(arrived), len(out_shapes), *refs),
        in_specs=[pl.BlockSpec(memory_space=pltpu.SMEM)]
        + [pl.BlockSpec(memory_space=pl.ANY)] * len(operands),
        out_specs=[pl.BlockSpec(memory_space=pl.ANY)] * len(out_shapes),
        out_shape=[jax.ShapeDtypeStruct(shape, jnp.bfloat16) for shape in out_shapes],
        scratch_shapes=scratch,
        compiler_params=params(),
        cost_estimate=cost(
            4 * tokens * BLK * WIDE * len(parts),
            2 * (2 * tokens * (cols + len(plan) * BLK) + (held + len(parts)) * BLK * WIDE),
        ),
        name=name,
    )(table, *operands)


def swap_halves(grad_rows, out_rows, core):
    grads = [grad_rows, swap_cores(other_half(grad_rows, core))]
    outs = [out_rows, swap_cores(out_rows)]
    return grads, outs


def first_stage(table, grads, outs, after):
    cols = outs[0].shape[1]
    plan = []
    for j in range(SIDE):
        row = j * BLK
        plan.append((SIDE * 2 + j, [(0, [], 0, row, 0), (WIDE, [], 1, row, 0)]))
        plan.append((SIDE * 1 + j, [(WIDE, [], 0, row, WIDE)]))
        plan.append((SIDE * 3 + j, [(0, [], 1, row, WIDE)]))
    plus, minus = pieces(
        "first_pieces", table, grads, outs, plan, [], [(SIDE * BLK, cols)] * 2, after
    )
    return hop(plus, 1), hop(minus, -1)


def second_stage(table, grads, outs, near, after):
    plan = []
    for j in range(SIDE):
        row = j * BLK
        plan.append((SIDE * 1 + j, [(0, [(0, j, 0)], 0, row, 0)]))
        plan.append((SIDE * 3 + j, [(WIDE, [(1, j, 0)], 1, row, 0)]))
    up, down = pieces(
        "second_pieces", table, grads, outs, plan, near, [(SIDE * BLK, WIDE)] * 2, after
    )
    return hop(up, 1), hop(down, -1)


def third_stage(table, grads, outs, near, far):
    plan = []
    for n in range(SIDE):
        at = (ORDER + n,)
        plan.append(
            (
                at,
                [
                    (0, [(2, at, 0), (1, at, WIDE)], n, 0, 0),
                    (WIDE, [(0, at, WIDE), (3, at, 0)], n, 0, WIDE),
                ],
            )
        )
    two, one, three, mine = pieces(
        "third_pieces", table, grads, outs, plan, [*near, *far], [(BLK, 2 * WIDE)] * SIDE
    )
    return mine, hop(two, 2, True), hop(one, 1, True), hop(three, -1, True)


def attend_kernel(
    low_ref, pos_ref, q_ref, g_ref, o_ref, key_ref, val_ref,
    kv4, kv3, kv2, kv1,
    packed_ref, own_ref, back4, back3, back2, back1,
    bias, held, keys, keys_t, vals, dkey, dval,
):
    step = pl.program_id(0)
    scale = 1.0 / math.sqrt(HEAD)
    tiles = RUN // TILE

    @pl.when(step == 0)
    def _():
        for t in range(tiles):
            row = lax.broadcasted_iota(jnp.int32, (SEEN, TILE), 0)
            col = lax.broadcasted_iota(jnp.int32, (SEEN, TILE), 1)
            low = low_ref[:, t * TILE : (t + 1) * TILE] - t * TILE
            one = jnp.where((row >= low) & (row <= col + BACK * RUN), 0.0, NEG)
            for h in range(STACK):
                bias[t, :, h * TILE : (h + 1) * TILE] = one
        for n, ref in enumerate((kv4, kv3, kv2, kv1)):
            keys[n * RUN : (n + 1) * RUN, :] = ref[:, :HEAD]
            vals[n * RUN : (n + 1) * RUN, :] = ref[:, HEAD:]
        keys[BACK * RUN :, :] = key_ref[...]
        vals[BACK * RUN :, :] = val_ref[...]
        keys_t[...] = keys[...].T
        dkey[...] = jnp.zeros_like(dkey)
        dval[...] = jnp.zeros_like(dval)

    def begin(t):
        rows = slice(t * TILE, (t + 1) * TILE)

        def stack(ref):
            return jnp.concatenate(
                [ref[rows, h * HEAD : (h + 1) * HEAD] for h in range(STACK)], axis=0
            )

        q, g = stack(q_ref), stack(g_ref)
        prod = g.astype(jnp.float32) * stack(o_ref).astype(jnp.float32)
        row_dot = jnp.sum(prod.T, axis=0, keepdims=True)
        top = jnp.full((1, STACK * TILE), 2 * NEG, jnp.float32)
        for at in range(0, SEEN, CHUNK):
            seen = slice(t * TILE + at, t * TILE + at + CHUNK)
            scores = lax.dot_general(keys[seen, :], q, NT, preferred_element_type=jnp.float32)
            scores = scores * (scale * math.log2(math.e)) + bias[t, at : at + CHUNK, :]
            held[t, at : at + CHUNK, :] = scores
            top = jnp.maximum(top, jnp.max(scores, axis=0, keepdims=True))
        return q, g, row_dot, top

    def exponents(t, top):
        total = jnp.zeros_like(top)
        for at in range(0, SEEN, CHUNK):
            probs = jnp.exp2(held[t, at : at + CHUNK, :] - top)
            held[t, at : at + CHUNK, :] = probs
            total = total + jnp.sum(probs, axis=0, keepdims=True)
        return 1.0 / total

    def finish(t, q, g, row_dot, inverse):
        dq_t = jnp.zeros((HEAD, STACK * TILE), jnp.float32)
        for at in range(0, SEEN, CHUNK):
            seen = slice(t * TILE + at, t * TILE + at + CHUNK)
            probs = held[t, at : at + CHUNK, :] * inverse
            dval[seen, :] += jnp.dot(
                probs.astype(jnp.bfloat16), g, preferred_element_type=jnp.float32
            )
            prob_grad = lax.dot_general(vals[seen, :], g, NT, preferred_element_type=jnp.float32)
            score_grad = (probs * (prob_grad - row_dot)).astype(jnp.bfloat16)
            dkey[seen, :] += jnp.dot(score_grad, q, preferred_element_type=jnp.float32)
            dq_t += jnp.dot(keys_t[:, seen], score_grad, preferred_element_type=jnp.float32)
        return (dq_t * scale).T.astype(jnp.bfloat16)

    grads = []
    unit = begin(0)
    for t in range(tiles):
        q, g, row_dot, top = unit
        inverse = exponents(t, top)
        if t + 1 < tiles:
            unit = begin(t + 1)
        grads.append(finish(t, q, g, row_dot, inverse))
    slots = lax.broadcasted_iota(jnp.int32, (packed_ref.shape[0], RUN), 0)
    select = (slots == pos_ref[...]).astype(jnp.bfloat16)
    dq = jnp.concatenate(
        [
            jnp.concatenate([part[h * TILE : (h + 1) * TILE, :] for part in grads], axis=0)
            for h in range(STACK)
        ],
        axis=1,
    )
    packed_ref[...] = jnp.dot(select, dq, preferred_element_type=jnp.float32).astype(jnp.bfloat16)

    @pl.when(step == pl.num_programs(0) - 1)
    def _():
        for n, ref in enumerate((back4, back3, back2, back1)):
            rows = slice(n * RUN, (n + 1) * RUN)
            ref[:, :HEAD] = (dkey[rows, :] * scale).astype(jnp.bfloat16)
            ref[:, HEAD:] = dval[rows, :].astype(jnp.bfloat16)
        own_ref[:, :HEAD] = dkey[BACK * RUN :, :] * scale
        own_ref[:, HEAD:] = dval[BACK * RUN :, :]


def attend(low, pos, query, grad, out, key, value, earlier, slots):
    heads = query.shape[1] // HEAD
    window = (BACK + 1) * RUN
    whole = lambda shape: pl.BlockSpec(shape, lambda h: (0, 0))
    by_heads = lambda rows: pl.BlockSpec((rows, STACK * HEAD), lambda h: (0, h))
    pair = (RUN, 2 * HEAD)
    return pl.pallas_call(
        attend_kernel,
        grid=(heads // STACK,),
        in_specs=[whole((1, RUN))] * 2
        + [by_heads(RUN)] * 3
        + [whole((RUN, HEAD))] * 2
        + [whole(pair)] * BACK,
        out_specs=[by_heads(slots), whole(pair)] + [whole(pair)] * BACK,
        out_shape=[
            jax.ShapeDtypeStruct((slots, query.shape[1]), jnp.bfloat16),
            jax.ShapeDtypeStruct(pair, jnp.float32),
        ]
        + [jax.ShapeDtypeStruct(pair, jnp.bfloat16)] * BACK,
        scratch_shapes=[
            pltpu.VMEM((RUN // TILE, SEEN, STACK * TILE), jnp.float32),
            pltpu.VMEM((RUN // TILE, SEEN, STACK * TILE), jnp.float32),
            pltpu.VMEM((window, HEAD), jnp.bfloat16),
            pltpu.VMEM((HEAD, window), jnp.bfloat16),
            pltpu.VMEM((window, HEAD), jnp.bfloat16),
            pltpu.VMEM((window, HEAD), jnp.float32),
            pltpu.VMEM((window, HEAD), jnp.float32),
        ],
        compiler_params=params(),
        cost_estimate=cost(10 * heads * RUN * window * HEAD, 8 * MIB, heads * RUN * window),
        name="attend",
    )(low, pos, query, grad, out, key, value, *earlier)


def route_rows(slot_blocks, own_index, parties, block_rows):
    total = slot_blocks.shape[0]
    ids = jnp.arange(total, dtype=jnp.int32)
    slot_of_block = jnp.sum(
        jnp.where(slot_blocks[None, :] == ids[:, None], ids[None, :], 0), axis=1
    )
    local = jnp.arange(parties, dtype=jnp.int32)

    def place(peer, order):
        earlier = (peer[:, None] == peer[None, :]) & (order[None, :] < order[:, None])
        return peer * CAP + jnp.sum(earlier, axis=1).astype(jnp.int32)

    dest_slot = lax.dynamic_slice_in_dim(slot_of_block, own_index * parties, parties, 0)
    held = lax.dynamic_slice_in_dim(slot_blocks, own_index * parties, parties, 0)
    rows = jnp.arange(block_rows, dtype=jnp.int32)

    def spread(at):
        return (at[:, None] * block_rows + rows[None, :]).reshape(-1)

    return spread(place(dest_slot // parties, dest_slot)), spread(place(held // parties, local))


def on_device(
    grad_out, out_weight, query_states, key_states, value_tensor, attn_out, doc_ids, block_order
):
    parties = lax.axis_size("ctx")
    own_index = lax.axis_index("ctx")
    core = lax.axis_index("dp")
    x, y = own_index // SIDE, own_index % SIDE
    grad_rows, out_rows = grad_out[0], attn_out[0]
    doc_row = doc_ids[0]
    key, value = key_states[0], value_tensor[0]

    both = jnp.concatenate([key, value], axis=1)
    earlier = [lax.ppermute(both, "ctx", run_shift(k, parties)) for k in range(BACK, 0, -1)]

    table = block_table(x, y, core)
    grads, outs = swap_halves(grad_rows, out_rows, core)
    near = first_stage(table, grads, outs, earlier)

    attn_grad = project(grad_rows, out_weight)
    own_docs = lax.dynamic_slice_in_dim(doc_row, own_index * RUN, RUN, 0)
    start = jnp.maximum(own_index - BACK, 0) * RUN
    seen_docs = lax.dynamic_slice_in_dim(doc_row, start, (BACK + 1) * RUN, 0)
    first = start + jnp.sum((seen_docs[:, None] < own_docs[None, :]).astype(jnp.int32), axis=0)
    low = (first - (own_index - BACK) * RUN).reshape(1, RUN)
    send_rows, held_rows = route_rows(block_order[0], own_index, parties, RUN // parties)
    slots = CAP * RUN
    packed, own_kv, *back = attend(
        low,
        send_rows.reshape(1, RUN),
        query_states[0],
        attn_grad,
        out_rows,
        key,
        value,
        earlier,
        slots,
    )
    far = second_stage(table, grads, outs, near, [own_kv])
    got = lax.all_to_all(
        packed.reshape(parties, slots // parties, -1), "ctx", 0, 0, tiled=True
    ).reshape(slots, -1)
    held_select = (
        held_rows[:, None] == jnp.arange(slots, dtype=jnp.int32)[None, :]
    ).astype(jnp.bfloat16)
    query_grad = jnp.dot(held_select, got, preferred_element_type=jnp.float32).astype(jnp.bfloat16)
    returned = [
        lax.ppermute(v, "ctx", run_shift(-k, parties)) for v, k in zip(back, range(BACK, 0, -1))
    ]
    kv_sum = own_kv
    for v in returned:
        kv_sum = kv_sum + v.astype(jnp.float32)
    kv_sum = kv_sum.astype(jnp.bfloat16)
    mine, *others = third_stage(table, grads, outs, near, far)
    weight_grad = mine.astype(jnp.float32)
    for v in others:
        weight_grad = weight_grad + v.astype(jnp.float32)
    return (
        query_grad[None],
        kv_sum[None, :, :HEAD],
        kv_sum[None, :, HEAD:],
        weight_grad,
    )


def solution(mesh):
    heads = P("dp", "ctx", "tp")
    in_specs = (
        P("dp", "ctx", None),
        P(None, "tp"),
        heads,
        heads,
        heads,
        heads,
        P("dp", None),
        P("dp", None),
    )
    out_specs = (heads, heads, heads, P(("ctx", "dp"), "tp"))
    return jax.shard_map(
        on_device, mesh=mesh, in_specs=in_specs, out_specs=out_specs, check_vma=False
    )
```

time: 160 us -> 119 us (0.74)
  starting transfers between devices: 53.7 us -> 31.3 us
  matrix products: 14.8 us -> 1.89 us
  waiting for transfers between devices: 15.6 us -> 27 us
  local copies, waits for them, and re-layouts: 17.5 us -> 7.37 us
  Pallas kernels: 51.8 us -> 43.8 us
    ppermute x24 -> x7, starting transfers between devices: 34.5 us -> 10.1 us  [hop(): return lax.ppermute(value, ('ctx', 'dp'), axis_shift(k, second))]
    dot_general x1 -> x0, matrix products: 12.3 us -> none  [on_device(): jnp.dot(grad_rows, out_weight, preferred_element_type=jnp.float32)]
    unnamed x42 -> x28, local copies, waits for them, and re-layouts: 16.1 us -> 4.64 us
    pallas_call x8 -> x6, Pallas kernels: 51.8 us -> 43.8 us  [the longest x3 18.5 us: pieces(): pl.pallas_call(lambda *refs: piece_kernel(plan, len(arrived), len(out_sha...]
    ppermute x24 -> x7, waiting for transfers between devices: 3.35 us -> 9.27 us  [hop(): return lax.ppermute(value, ('ctx', 'dp'), axis_shift(k, second))]
    ppermute x4, waiting for transfers between devices: 5.56 us -> 8.35 us  [on_device(): lax.ppermute(v, 'ctx', run_shift(-k, parties))]
    ppermute x4, waiting for transfers between devices: 6.72 us -> 9.36 us  [on_device(): lax.ppermute(both, 'ctx', run_shift(k, parties))]
    add x2, local copies, waits for them, and re-layouts: 0.16 us -> 1.95 us  [spread(): return (at[:, None] * block_rows + rows[None, :]).reshape(-1)]
  transfers between devices with their start and end apart: 35 -> 18, of which waited for: 8 -> 11; matrix products, arithmetic and copies ran while one was open for 13% -> 7% of each run, Pallas kernels for 24% -> 23%
where the time goes in v2:
time: 119 us; the launch traced here: 117 us
  Pallas kernels  43.8 us (37%)
  starting transfers between devices  31.3 us (26%)
  waiting for transfers between devices  27 us (23%)
  local copies, waits for them, and re-layouts  7.37 us (6%)
  other arithmetic  5.22 us (4%)
  matrix products  1.89 us (2%)
    pallas_call x3, Pallas kernels, pieces(): pl.pallas_call(lambda *refs: piece_kernel(plan, len(arrived), len(out_sha...  18.5 us
    pallas_call x1, Pallas kernels, attend(): pl.pallas_call(attend_kernel, grid=(heads // STACK,), in_specs=[whole((1,...  13.4 us
    ppermute x7, starting transfers between devices, hop(): return lax.ppermute(value, ('ctx', 'dp'), axis_shift(k, second))  10.1 us
    ppermute x4, starting transfers between devices, on_device(): lax.ppermute(v, 'ctx', run_shift(-k, parties))  10.1 us
    ppermute x4, waiting for transfers between devices, on_device(): lax.ppermute(both, 'ctx', run_shift(k, parties))  9.36 us
    ppermute x7, waiting for transfers between devices, hop(): return lax.ppermute(value, ('ctx', 'dp'), axis_shift(k, second))  9.27 us
    pallas_call x1, Pallas kernels, project(): pl.pallas_call(project_kernel, in_specs=[pl.BlockSpec(memory_space=pl.ANY...  8.73 us
    ppermute x4, waiting for transfers between devices, on_device(): lax.ppermute(v, 'ctx', run_shift(-k, parties))  8.35 us
  transfers between devices with their start and end apart: 18, of which 11 were waited for; matrix products, arithmetic and copies ran while one was open for 7% of the time, Pallas kernels for 23%

profile of v2, /device:TPU:0, one launch (start us, length us, event | category | flops | bytes accessed | tf_op | source)
XLA Modules:
  0.0 117.3 jit_solution(534162324307672892)
XLA Ops:
  0.7 3.2 %other_half.1 = bf16[256,4096]{1,0:T(8,128)(2,1)} custom-call(s32[1]{0:T(128)} %bitcast.15.core_ref, bf16[256,8192]{1,0:T(8,128)(2,1)} %bitcast.28), custom_call_target="tpu_custom_call" | custom-call | bytes 4194304 | tf_op jit(solution)/shard_map/other_half/pallas_call | solution.py:77
  4.0 1.7 %collective-permute-start.3 = (bf16[256,256]{1,0:T(8,128)(2,1)S(1)}, bf16[256,256]{1,0:T(8,128)(2,1)S(1)}, u32[]{:S(2)}, u32[]{:S(2)}) collective-permute-start(bf16[256,256]{1,0:T(8,128)(2,1)S(1)} %pad_maximum_fusion), channel_id=1, source_target_pairs={{0,8},{8,16},{16,24},{24,32},{32,40},{40,48},{48,56},{56,64},{64,7... | collective-permute-start | bytes 393224 | tf_op jit(solution)/shard_map/ppermute | solution.py:467
  5.7 2.9 %collective-permute-start.2 = (bf16[256,256]{1,0:T(8,128)(2,1)S(1)}, bf16[256,256]{1,0:T(8,128)(2,1)}, u32[]{:S(2)}, u32[]{:S(2)}) collective-permute-start(bf16[256,256]{1,0:T(8,128)(2,1)S(1)} %pad_maximum_fusion), channel_id=1, source_target_pairs={{0,16},{8,24},{16,32},{24,40},{32,48},{40,56},{48,64},{56,72},{64,... | collective-permute-start | bytes 393224 | tf_op jit(solution)/shard_map/ppermute | solution.py:467
  8.6 2.3 %collective-permute-start.1 = (bf16[256,256]{1,0:T(8,128)(2,1)S(1)}, bf16[256,256]{1,0:T(8,128)(2,1)}, u32[]{:S(2)}, u32[]{:S(2)}) collective-permute-start(bf16[256,256]{1,0:T(8,128)(2,1)S(1)} %pad_maximum_fusion), channel_id=1, source_target_pairs={{0,24},{8,32},{16,40},{24,48},{32,56},{40,64},{48,72},{56,80},{64,... | collective-permute-start | bytes 393224 | tf_op jit(solution)/shard_map/ppermute | solution.py:467
  11.0 3.9 %collective-permute-done.3.kv1.refs_8_ = bf16[256,256]{1,0:T(8,128)(2,1)S(1)} collective-permute-done((bf16[256,256]{1,0:T(8,128)(2,1)S(1)}, bf16[256,256]{1,0:T(8,128)(2,1)S(1)}, u32[]{:S(2)}, u32[]{:S(2)}) %collective-permute-start.3) | collective-permute-done | bytes 131104 | tf_op jit(solution)/shard_map/ppermute | solution.py:467
  16.8 4.4 %collective-permute-done.kv4.refs_5_ = bf16[256,256]{1,0:T(8,128)(2,1)} collective-permute-done((bf16[256,256]{1,0:T(8,128)(2,1)S(1)}, bf16[256,256]{1,0:T(8,128)(2,1)}, u32[]{:S(2)}, u32[]{:S(2)}) %collective-permute-start) | collective-permute-done | bytes 131104 | tf_op jit(solution)/shard_map/ppermute | solution.py:467
  22.1 1.3 %copy-done.1 = bf16[256,4096]{1,0:T(8,128)(2,1)} copy-done((bf16[256,4096]{1,0:T(8,128)(2,1)}, bf16[256,4096]{1,0:T(8,128)(2,1)S(1)}, u32[]{:S(2)}) %copy-start.1) | copy-done | bytes 2097176
  23.4 7.6 %first_pieces.1 = (bf16[1024,1024]{1,0:T(8,128)(2,1)}, bf16[1024,1024]{1,0:T(8,128)(2,1)}) custom-call(s32[21]{0:T(128)} %pad_add_fusion.refs_0_, bf16[256,8192]{1,0:T(8,128)(2,1)} %bitcast.29, bf16[256,4096]{1,0:T(8,128)(2,1)} %copy-done.1, bf16[256,1024]{1,0:T(8,128)(2,1)} %bitcast.34, bf16[256,1024]{1,0:T(8,128)(2,1)} %copy-done.4, ...), custom_call_target="tpu_custom_call" | custom-call | flops 2147483648 | bytes 8388608 | tf_op jit(solution)/shard_map/first_pieces/pallas_call | solution.py:233
  31.0 3.2 %collective-permute-start.11 = (bf16[1024,1024]{1,0:T(8,128)(2,1)}, bf16[1024,1024]{1,0:T(8,128)(2,1)}, u32[]{:S(2)}, u32[]{:S(2)}) collective-permute-start(bf16[1024,1024]{1,0:T(8,128)(2,1)} %get-tuple-element.25), channel_id=1, source_target_pairs={{0,96},{1,25},{8,104},{9,1},{16,112},{17,9},{24,120},{25,17},{32,0... | collective-permute-start | bytes 6291464 | tf_op jit(solution)/shard_map/ppermute | solution.py:44
  36.3 8.7 %project.1.g_ref = bf16[256,1024]{1,0:T(8,128)(2,1)} custom-call(bf16[256,8192]{1,0:T(8,128)(2,1)} %bitcast.30, bf16[8192,1024]{1,0:T(8,128)(2,1)} %weight_ref.1), custom_call_target="tpu_custom_call" | custom-call | flops 4294967296 | bytes 20971520 | tf_op jit(solution)/shard_map/project/pallas_call | solution.py:118
  45.0 13.4 %attend.1 = (bf16[512,1024]{1,0:T(8,128)(2,1)}, f32[256,256]{1,0:T(8,128)}, bf16[256,256]{1,0:T(8,128)(2,1)}, bf16[256,256]{1,0:T(8,128)(2,1)}, bf16[256,256]{1,0:T(8,128)(2,1)}, /*index=5*/bf16[256,256]{1,0:T(8,128)(2,1)}) custom-call(s32[1,256]{1,0:T(1,128)} %bitcast.45, s32[1,256]{1,0:T(1,128)} %add.173.pos_ref, bf16[256,1024]{1,0:T(8,128)(2,1)} %bitcast.46, ...), custom_call_target="tpu_custom_call" | custom-call | flops 3355443200 | bytes 8388608 | tf_op jit(solution)/shard_map/attend/pallas_call | solution.py:405
  58.5 1.3 %copy-done.2 = bf16[1024,1024]{1,0:T(8,128)(2,1)} copy-done((bf16[1024,1024]{1,0:T(8,128)(2,1)}, bf16[1024,1024]{1,0:T(8,128)(2,1)S(1)}, u32[]{:S(2)}) %copy-start.2) | copy-done | bytes 2097176
  59.8 5.7 %second_pieces.1 = (bf16[1024,512]{1,0:T(8,128)(2,1)}, bf16[1024,512]{1,0:T(8,128)(2,1)}) custom-call(s32[21]{0:T(128)} %pad_add_fusion.refs_0_, bf16[256,8192]{1,0:T(8,128)(2,1)} %bitcast.31, bf16[256,4096]{1,0:T(8,128)(2,1)} %copy-done.1, bf16[256,1024]{1,0:T(8,128)(2,1)} %bitcast.36, bf16[256,1024]{1,0:T(8,128)(2,1)} %copy-done.4, ...), custom_call_target="tpu_custom_call" | custom-call | flops 1073741824 | bytes 7340032 | tf_op jit(solution)/shard_map/second_pieces/pallas_call | solution.py:233
  65.6 3.2 %collective-permute-start.13 = (bf16[1024,512]{1,0:T(8,128)(2,1)}, bf16[1024,512]{1,0:T(8,128)(2,1)S(1)}, u32[]{:S(2)}, u32[]{:S(2)}) collective-permute-start(bf16[1024,512]{1,0:T(8,128)(2,1)} %get-tuple-element.27), channel_id=1, source_target_pairs={{0,96},{1,25},{8,104},{9,1},{16,112},{17,9},{24,120},{25,17},{32,0... | collective-permute-start | bytes 3145736 | tf_op jit(solution)/shard_map/ppermute | solution.py:44
  69.1 3.9 %all-to-all-start = ((bf16[16,32,1024]{2,1,0:T(8,128)(2,1)}), bf16[16,32,1024]{2,1,0:T(8,128)(2,1)S(1)}, u32[]{:S(2)}, u32[]{:S(2)}) async-start(bf16[16,32,1024]{2,1,0:T(8,128)(2,1)} %bitcast.10), calls=%async_computation | async-start | bytes 2097152 | tf_op jit(solution)/shard_map/all_to_all | solution.py:493
  73.0 3.2 %collective-permute-start.4 = (bf16[256,256]{1,0:T(8,128)(2,1)}, bf16[256,256]{1,0:T(8,128)(2,1)S(1)}, u32[]{:S(2)}, u32[]{:S(2)}) collective-permute-start(bf16[256,256]{1,0:T(8,128)(2,1)} %get-tuple-element.20), channel_id=1, source_target_pairs={{0,96},{8,104},{16,112},{24,120},{32,0},{40,8},{48,16},{56,24},{64... | collective-permute-start | bytes 393224 | tf_op jit(solution)/shard_map/ppermute | solution.py:501
  76.2 1.8 %collective-permute-start.5 = (bf16[256,256]{1,0:T(8,128)(2,1)}, bf16[256,256]{1,0:T(8,128)(2,1)S(1)}, u32[]{:S(2)}, u32[]{:S(2)}) collective-permute-start(bf16[256,256]{1,0:T(8,128)(2,1)} %get-tuple-element.21), channel_id=1, source_target_pairs={{0,104},{8,112},{16,120},{24,0},{32,8},{40,16},{48,24},{56,32},{64... | collective-permute-start | bytes 393224 | tf_op jit(solution)/shard_map/ppermute | solution.py:501
  77.9 2.7 %collective-permute-start.6 = (bf16[256,256]{1,0:T(8,128)(2,1)}, bf16[256,256]{1,0:T(8,128)(2,1)S(1)}, u32[]{:S(2)}, u32[]{:S(2)}) collective-permute-start(bf16[256,256]{1,0:T(8,128)(2,1)} %get-tuple-element.22), channel_id=1, source_target_pairs={{0,112},{8,120},{16,0},{24,8},{32,16},{40,24},{48,32},{56,40},{64,... | collective-permute-start | bytes 393224 | tf_op jit(solution)/shard_map/ppermute | solution.py:501
  80.6 6.8 %collective-permute-done.12.refs_7_ = bf16[1024,512]{1,0:T(8,128)(2,1)S(1)} collective-permute-done((bf16[1024,512]{1,0:T(8,128)(2,1)}, bf16[1024,512]{1,0:T(8,128)(2,1)S(1)}, u32[]{:S(2)}, u32[]{:S(2)}) %collective-permute-start.12) | collective-permute-done | bytes 1048608 | tf_op jit(solution)/shard_map/ppermute | solution.py:44
  87.4 2.5 %collective-permute-start.7 = (bf16[256,256]{1,0:T(8,128)(2,1)}, bf16[256,256]{1,0:T(8,128)(2,1)}, u32[]{:S(2)}, u32[]{:S(2)}) collective-permute-start(bf16[256,256]{1,0:T(8,128)(2,1)} %get-tuple-element.23), channel_id=1, source_target_pairs={{0,120},{8,0},{16,8},{24,16},{32,24},{40,32},{48,40},{56,48},{64,5... | collective-permute-start | bytes 393224 | tf_op jit(solution)/shard_map/ppermute | solution.py:501
  94.2 5.2 %third_pieces.1 = (bf16[256,1024]{1,0:T(8,128)(2,1)}, bf16[256,1024]{1,0:T(8,128)(2,1)}, bf16[256,1024]{1,0:T(8,128)(2,1)}, bf16[256,1024]{1,0:T(8,128)(2,1)}) custom-call(s32[21]{0:T(128)} %pad_add_fusion.refs_0_, bf16[256,8192]{1,0:T(8,128)(2,1)} %bitcast.32, bf16[256,4096]{1,0:T(8,128)(2,1)} %copy-done.1, bf16[256,1024]{1,0:T(8,128)(2,1)} %bitcast.37, ...), custom_call_target="tpu_custom_call" | custom-call | flops 1073741824 | bytes 8388608 | tf_op jit(solution)/shard_map/third_pieces/pallas_call | solution.py:233
  101.4 2.2 %collective-permute-start.16 = (bf16[256,1024]{1,0:T(8,128)(2,1)}, bf16[256,1024]{1,0:T(8,128)(2,1)S(1)}, u32[]{:S(2)}, u32[]{:S(2)}) collective-permute-start(bf16[256,1024]{1,0:T(8,128)(2,1)} %get-tuple-element.31), channel_id=1, source_target_pairs={{0,24},{1,97},{8,0},{9,105},{16,8},{17,113},{24,16},{25,121},{32,5... | collective-permute-start | bytes 1572872 | tf_op jit(solution)/shard_map/ppermute | solution.py:44
  104.6 6.7 %collective-permute-done.7 = bf16[256,256]{1,0:T(8,128)(2,1)} collective-permute-done((bf16[256,256]{1,0:T(8,128)(2,1)}, bf16[256,256]{1,0:T(8,128)(2,1)}, u32[]{:S(2)}, u32[]{:S(2)}) %collective-permute-start.7) | collective-permute-done | bytes 131104 | tf_op jit(solution)/shard_map/ppermute | solution.py:501
  113.0 1.9 %fusion = bf16[1,256,1024]{2,1,0:T(8,128)(2,1)} fusion(bf16[512,1024]{1,0:T(8,128)(2,1)S(1)} %bitcast.33, s32[256]{0:T(256)} %add.165), kind=kOutput, calls=%fused_computation.2 | convolution fusion | flops 268828672 | bytes 1573888 | tf_op jit(solution)/shard_map/dot_general | solution.py:499
  (71 shorter events, 16.8 us)
Async XLA Ops:
  0.6 34.8 %copy-start = (s32[1,4096]{1,0:T(1,128)S(1)}, s32[1,4096]{1,0:T(1,128)}, u32[]{:S(2)}) copy-start(s32[1,4096]{1,0:T(1,128)} %param.15) | copy-start | bytes 49156
  0.7 10.2 %copy-start.3 = (bf16[1,256,1024]{2,1,0:T(8,128)(2,1)S(1)}, bf16[1,256,1024]{2,1,0:T(8,128)(2,1)}, u32[]{:S(2)}) copy-start(bf16[1,256,1024]{2,1,0:T(8,128)(2,1)} %param.14) | copy-start | bytes 1572868
  0.7 14.3 %copy-start.13 = (s32[4]{0:T(128)S(1)}, s32[4]{0:T(128)}, u32[]{:S(2)}) copy-start(s32[4]{0:T(128)} %constant.87.clone) | copy-start | bytes 52
  3.9 17.3 %collective-permute-start.8 = (bf16[256,4096]{1,0:T(8,128)(2,1)}, bf16[256,4096]{1,0:T(8,128)(2,1)S(1)}, u32[]{:S(2)}, u32[]{:S(2)}) collective-permute-start(bf16[256,4096]{1,0:T(8,128)(2,1)} %other_half.1), channel_id=1, source_target_pairs={{0,1},{1,0},{2,3},{3,2},{4,5},{5,4},{6,7},{7,6},{8,9},{9,8},{10,11... | collective-permute-start | bytes 6291464 | tf_op jit(solution)/shard_map/ppermute | solution.py:48
  4.0 10.9 %collective-permute-start.3 = (bf16[256,256]{1,0:T(8,128)(2,1)S(1)}, bf16[256,256]{1,0:T(8,128)(2,1)S(1)}, u32[]{:S(2)}, u32[]{:S(2)}) collective-permute-start(bf16[256,256]{1,0:T(8,128)(2,1)S(1)} %pad_maximum_fusion), channel_id=1, source_target_pairs={{0,8},{8,16},{16,24},{24,32},{32,40},{40,48},{48,56},{56,64},{64,7... | collective-permute-start | bytes 393224 | tf_op jit(solution)/shard_map/ppermute | solution.py:467
  5.7 10.7 %collective-permute-start.2 = (bf16[256,256]{1,0:T(8,128)(2,1)S(1)}, bf16[256,256]{1,0:T(8,128)(2,1)}, u32[]{:S(2)}, u32[]{:S(2)}) collective-permute-start(bf16[256,256]{1,0:T(8,128)(2,1)S(1)} %pad_maximum_fusion), channel_id=1, source_target_pairs={{0,16},{8,24},{16,32},{24,40},{32,48},{40,56},{48,64},{56,72},{64,... | collective-permute-start | bytes 393224 | tf_op jit(solution)/shard_map/ppermute | solution.py:467
  8.6 8.1 %collective-permute-start.1 = (bf16[256,256]{1,0:T(8,128)(2,1)S(1)}, bf16[256,256]{1,0:T(8,128)(2,1)}, u32[]{:S(2)}, u32[]{:S(2)}) collective-permute-start(bf16[256,256]{1,0:T(8,128)(2,1)S(1)} %pad_maximum_fusion), channel_id=1, source_target_pairs={{0,24},{8,32},{16,40},{24,48},{32,56},{40,64},{48,72},{56,80},{64,... | collective-permute-start | bytes 393224 | tf_op jit(solution)/shard_map/ppermute | solution.py:467
  10.9 10.3 %collective-permute-start.9 = (bf16[256,1024]{1,0:T(8,128)(2,1)S(1)}, bf16[256,1024]{1,0:T(8,128)(2,1)S(1)}, u32[]{:S(2)}, u32[]{:S(2)}) collective-permute-start(bf16[256,1024]{1,0:T(8,128)(2,1)S(1)} %bitcast.38), channel_id=1, source_target_pairs={{0,1},{1,0},{2,3},{3,2},{4,5},{5,4},{6,7},{7,6},{8,9},{9,8},{10,11... | collective-permute-start | bytes 1572872 | tf_op jit(solution)/shard_map/ppermute | solution.py:48
  14.9 6.3 %collective-permute-start = (bf16[256,256]{1,0:T(8,128)(2,1)S(1)}, bf16[256,256]{1,0:T(8,128)(2,1)}, u32[]{:S(2)}, u32[]{:S(2)}) collective-permute-start(bf16[256,256]{1,0:T(8,128)(2,1)S(1)} %pad_maximum_fusion), channel_id=1, source_target_pairs={{0,32},{8,40},{16,48},{24,56},{32,64},{40,72},{48,80},{56,88},{64,... | collective-permute-start | bytes 393224 | tf_op jit(solution)/shard_map/ppermute | solution.py:467
  15.7 18.5 %copy-start.11 = (s32[1,256]{1,0:T(1,128)S(1)}, s32[1,256]{1,0:T(1,128)}, u32[]{:S(2)}) copy-start(s32[1,256]{1,0:T(1,128)} %param.16) | copy-start | bytes 3076
  31.0 27.5 %collective-permute-start.10 = (bf16[1024,1024]{1,0:T(8,128)(2,1)}, bf16[1024,1024]{1,0:T(8,128)(2,1)S(1)}, u32[]{:S(2)}, u32[]{:S(2)}) collective-permute-start(bf16[1024,1024]{1,0:T(8,128)(2,1)} %get-tuple-element.24), channel_id=1, source_target_pairs={{0,32},{1,9},{8,40},{9,17},{16,48},{17,25},{24,56},{25,1},{32,64},... | collective-permute-start | bytes 6291464 | tf_op jit(solution)/shard_map/ppermute | solution.py:44
  31.0 27.4 %collective-permute-start.11 = (bf16[1024,1024]{1,0:T(8,128)(2,1)}, bf16[1024,1024]{1,0:T(8,128)(2,1)}, u32[]{:S(2)}, u32[]{:S(2)}) collective-permute-start(bf16[1024,1024]{1,0:T(8,128)(2,1)} %get-tuple-element.25), channel_id=1, source_target_pairs={{0,96},{1,25},{8,104},{9,1},{16,112},{17,9},{24,120},{25,17},{32,0... | collective-permute-start | bytes 6291464 | tf_op jit(solution)/shard_map/ppermute | solution.py:44
  65.5 21.9 %collective-permute-start.12 = (bf16[1024,512]{1,0:T(8,128)(2,1)}, bf16[1024,512]{1,0:T(8,128)(2,1)S(1)}, u32[]{:S(2)}, u32[]{:S(2)}) collective-permute-start(bf16[1024,512]{1,0:T(8,128)(2,1)} %get-tuple-element.26), channel_id=1, source_target_pairs={{0,32},{1,9},{8,40},{9,17},{16,48},{17,25},{24,56},{25,1},{32,64},... | collective-permute-start | bytes 3145736 | tf_op jit(solution)/shard_map/ppermute | solution.py:44
  65.6 27.5 %collective-permute-start.13 = (bf16[1024,512]{1,0:T(8,128)(2,1)}, bf16[1024,512]{1,0:T(8,128)(2,1)S(1)}, u32[]{:S(2)}, u32[]{:S(2)}) collective-permute-start(bf16[1024,512]{1,0:T(8,128)(2,1)} %get-tuple-element.27), channel_id=1, source_target_pairs={{0,96},{1,25},{8,104},{9,1},{16,112},{17,9},{24,120},{25,17},{32,0... | collective-permute-start | bytes 3145736 | tf_op jit(solution)/shard_map/ppermute | solution.py:44
  69.1 43.9 %all-to-all-start = ((bf16[16,32,1024]{2,1,0:T(8,128)(2,1)}), bf16[16,32,1024]{2,1,0:T(8,128)(2,1)S(1)}, u32[]{:S(2)}, u32[]{:S(2)}) async-start(bf16[16,32,1024]{2,1,0:T(8,128)(2,1)} %bitcast.10), calls=%async_computation | async-start | bytes 2097152 | tf_op jit(solution)/shard_map/all_to_all | solution.py:493
  73.0 27.3 %collective-permute-start.4 = (bf16[256,256]{1,0:T(8,128)(2,1)}, bf16[256,256]{1,0:T(8,128)(2,1)S(1)}, u32[]{:S(2)}, u32[]{:S(2)}) collective-permute-start(bf16[256,256]{1,0:T(8,128)(2,1)} %get-tuple-element.20), channel_id=1, source_target_pairs={{0,96},{8,104},{16,112},{24,120},{32,0},{40,8},{48,16},{56,24},{64... | collective-permute-start | bytes 393224 | tf_op jit(solution)/shard_map/ppermute | solution.py:501
  76.2 25.2 %collective-permute-start.5 = (bf16[256,256]{1,0:T(8,128)(2,1)}, bf16[256,256]{1,0:T(8,128)(2,1)S(1)}, u32[]{:S(2)}, u32[]{:S(2)}) collective-permute-start(bf16[256,256]{1,0:T(8,128)(2,1)} %get-tuple-element.21), channel_id=1, source_target_pairs={{0,104},{8,112},{16,120},{24,0},{32,8},{40,16},{48,24},{56,32},{64... | collective-permute-start | bytes 393224 | tf_op jit(solution)/shard_map/ppermute | solution.py:501
  77.9 26.7 %collective-permute-start.6 = (bf16[256,256]{1,0:T(8,128)(2,1)}, bf16[256,256]{1,0:T(8,128)(2,1)S(1)}, u32[]{:S(2)}, u32[]{:S(2)}) collective-permute-start(bf16[256,256]{1,0:T(8,128)(2,1)} %get-tuple-element.22), channel_id=1, source_target_pairs={{0,112},{8,120},{16,0},{24,8},{32,16},{40,24},{48,32},{56,40},{64,... | collective-permute-start | bytes 393224 | tf_op jit(solution)/shard_map/ppermute | solution.py:501
  87.4 23.9 %collective-permute-start.7 = (bf16[256,256]{1,0:T(8,128)(2,1)}, bf16[256,256]{1,0:T(8,128)(2,1)}, u32[]{:S(2)}, u32[]{:S(2)}) collective-permute-start(bf16[256,256]{1,0:T(8,128)(2,1)} %get-tuple-element.23), channel_id=1, source_target_pairs={{0,120},{8,0},{16,8},{24,16},{32,24},{40,32},{48,40},{56,48},{64,5... | collective-permute-start | bytes 393224 | tf_op jit(solution)/shard_map/ppermute | solution.py:501
  91.9 19.5 %copy-start.5 = (f32[256,256]{1,0:T(8,128)S(1)}, f32[256,256]{1,0:T(8,128)}, u32[]{:S(2)}) copy-start(f32[256,256]{1,0:T(8,128)} %get-tuple-element.19.refs_7_) | copy-start | bytes 786436
  99.4 16.6 %copy-start.8 = (bf16[256,1024]{1,0:T(8,128)(2,1)S(1)}, bf16[256,1024]{1,0:T(8,128)(2,1)}, u32[]{:S(2)}) copy-start(bf16[256,1024]{1,0:T(8,128)(2,1)} %get-tuple-element.28) | copy-start | bytes 1572868
  99.4 15.4 %collective-permute-start.14 = (bf16[256,1024]{1,0:T(8,128)(2,1)}, bf16[256,1024]{1,0:T(8,128)(2,1)S(1)}, u32[]{:S(2)}, u32[]{:S(2)}) collective-permute-start(bf16[256,1024]{1,0:T(8,128)(2,1)} %get-tuple-element.29), channel_id=1, source_target_pairs={{0,16},{1,65},{8,24},{9,73},{16,0},{17,81},{24,8},{25,89},{32,48},... | collective-permute-start | bytes 1572872 | tf_op jit(solution)/shard_map/ppermute | solution.py:44
  100.3 15.7 %collective-permute-start.15 = (bf16[256,1024]{1,0:T(8,128)(2,1)}, bf16[256,1024]{1,0:T(8,128)(2,1)S(1)}, u32[]{:S(2)}, u32[]{:S(2)}) collective-permute-start(bf16[256,1024]{1,0:T(8,128)(2,1)} %get-tuple-element.30), channel_id=1, source_target_pairs={{0,8},{1,33},{8,16},{9,41},{16,24},{17,49},{24,0},{25,57},{32,40},... | collective-permute-start | bytes 1572872 | tf_op jit(solution)/shard_map/ppermute | solution.py:44
  101.4 14.7 %collective-permute-start.16 = (bf16[256,1024]{1,0:T(8,128)(2,1)}, bf16[256,1024]{1,0:T(8,128)(2,1)S(1)}, u32[]{:S(2)}, u32[]{:S(2)}) collective-permute-start(bf16[256,1024]{1,0:T(8,128)(2,1)} %get-tuple-element.31), channel_id=1, source_target_pairs={{0,24},{1,97},{8,0},{9,105},{16,8},{17,113},{24,16},{25,121},{32,5... | collective-permute-start | bytes 1572872 | tf_op jit(solution)/shard_map/ppermute | solution.py:44
  (8 other events, 23.2 us)

commit v3 on v2

v3 whole, which is shorter than its diff:
```python
import math

import jax
import jax.numpy as jnp
from jax import lax
from jax.experimental import pallas as pl
from jax.experimental.pallas import tpu as pltpu
from jax.sharding import PartitionSpec as P

HEAD = 128
CAP = 2
SIDE = 4
BACK = 4
RUN = 256
BLK = 256
TILE = 128
SEEN = BACK * RUN + TILE
CHUNK = 384
PIECES_MIB = 24
WIDE = 512
NEG = -1e30
MIB = 1024 * 1024
NT = (((1,), (1,)), ((), ()))
TN = (((0,), (0,)), ((), ()))


def run_shift(k, parties):
    return [(i, (i + k) % parties) for i in range(parties)]


def axis_shift(k, second):
    pairs = []
    for x in range(SIDE):
        for y in range(SIDE):
            for core in range(2):
                along_x = (core == 0) != second
                to_x, to_y = ((x + k) % SIDE, y) if along_x else (x, (y + k) % SIDE)
                pairs.append(((x * SIDE + y) * 2 + core, (to_x * SIDE + to_y) * 2 + core))
    return pairs


def hop(value, k, second=False):
    return lax.ppermute(value, ("ctx", "dp"), axis_shift(k, second))


def swap_cores(value):
    return lax.ppermute(value, "dp", [(0, 1), (1, 0)])


def params(mib):
    return pltpu.CompilerParams(vmem_limit_bytes=mib * MIB)


def hbm(values):
    return [pltpu.with_memory_space_constraint(v, pltpu.HBM) for v in values]


def cost(flops, moved, exps=0):
    return pl.CostEstimate(flops=flops, bytes_accessed=moved, transcendentals=exps)


def project_kernel(grad_ref, weight_ref, after_ref, out_ref, grads, weights, grad_sems, weight_sems):
    slabs = grad_sems.shape[0]
    depth = weight_ref.shape[0] // slabs
    copies = []
    for i in range(slabs):
        part = slice(i * depth, (i + 1) * depth)
        copies.append(
            (
                pltpu.make_async_copy(grad_ref.at[:, part], grads.at[:, part], grad_sems.at[i]),
                pltpu.make_async_copy(weight_ref.at[part], weights.at[part], weight_sems.at[i]),
            )
        )
    for pair in copies:
        for copy in pair:
            copy.start()
    total = None
    for i, pair in enumerate(copies):
        for copy in pair:
            copy.wait()
        part = slice(i * depth, (i + 1) * depth)
        addend = jnp.dot(grads[:, part], weights[part, :], preferred_element_type=jnp.float32)
        total = addend if total is None else total + addend
    out_ref[...] = total.astype(out_ref.dtype)


def project(grad_rows, weight, after):
    rows, depth = grad_rows.shape
    cols = weight.shape[1]
    slabs = 8
    return pl.pallas_call(
        project_kernel,
        in_specs=[pl.BlockSpec(memory_space=pl.ANY)] * 3,
        out_specs=pl.BlockSpec(memory_space=pltpu.VMEM),
        out_shape=jax.ShapeDtypeStruct((rows, cols), jnp.bfloat16),
        scratch_shapes=[
            pltpu.VMEM(grad_rows.shape, grad_rows.dtype),
            pltpu.VMEM(weight.shape, weight.dtype),
            pltpu.SemaphoreType.DMA((slabs,)),
            pltpu.SemaphoreType.DMA((slabs,)),
        ],
        compiler_params=params(32),
        cost_estimate=cost(2 * rows * depth * cols, 2 * depth * (rows + cols)),
        name="project",
    )(*hbm([grad_rows, weight]), after)


def block_table(x, y, core):
    first, second = jnp.where(core == 0, x, y), jnp.where(core == 0, y, x)
    step_first, step_second = jnp.where(core == 0, SIDE, 1), jnp.where(core == 0, 1, SIDE)
    offsets = jnp.arange(SIDE, dtype=jnp.int32)
    blocks = ((first + offsets[:, None]) % SIDE) * step_first + offsets[None, :] * step_second
    order = (second + jnp.stack([jnp.int32(v) for v in (2, 1, 3, 0)])) % SIDE
    table = jnp.concatenate([blocks.reshape(-1), order, core.reshape(1)])
    return table.astype(jnp.int32)


ORDER, CORE = SIDE * SIDE, SIDE * SIDE + SIDE


def turn_kernel(*refs):
    refs[-1][...] = refs[0][...].T


def turn(value, after):
    rows, cols = value.shape
    return pl.pallas_call(
        turn_kernel,
        in_specs=[pl.BlockSpec(memory_space=pltpu.VMEM), pl.BlockSpec(memory_space=pl.ANY)],
        out_specs=pl.BlockSpec(memory_space=pltpu.VMEM),
        out_shape=jax.ShapeDtypeStruct((cols, rows), value.dtype),
        compiler_params=params(8),
        cost_estimate=cost(0, 4 * rows * cols),
        name="turn",
    )(value, after)


def piece_kernel(plan, arrived_count, out_count, extra, blocks, *refs):
    grad_refs, out_refs = refs[:2], refs[2:4]
    arrived_refs = refs[4 : 4 + arrived_count]
    refs = refs[4 + arrived_count + extra :]
    results, refs = refs[:out_count], refs[out_count:]
    if arrived_count:
        outs, grads, held, sent, in_sems, out_sems = refs
    else:
        outs, grads, sent, in_sems, out_sems = refs
    tokens = out_refs[0].shape[1]
    core = blocks[CORE]
    taken = 0

    def load(source, target):
        nonlocal taken
        copy = pltpu.make_async_copy(source, target, in_sems.at[taken])
        taken += 1
        copy.start()
        return copy

    def number(at):
        return blocks[at] if isinstance(at, int) else blocks[blocks[at[0]]]

    shared = [
        load(ref, outs.at[:, n * tokens : (n + 1) * tokens]) for n, ref in enumerate(out_refs)
    ]

    def fetch(n, slot):
        at, parts = plan[n]
        copies = []
        for j, place in enumerate(at):
            first = pl.multiple_of((2 * number(place) + core) * BLK, BLK)
            for k, ref in enumerate(grad_refs):
                copies.append(
                    load(
                        ref.at[:, pl.ds(first, BLK)],
                        grads.at[n, k * tokens : (k + 1) * tokens, j * BLK : (j + 1) * BLK],
                    )
                )
        slots = []
        for _, arrived, _ in parts:
            mine = []
            for which, row, places in arrived:
                rows = arrived_refs[which].at[row : row + WIDE]
                if places is None:
                    copies.append(load(rows, held.at[slot]))
                else:
                    for j, place in enumerate(places):
                        first = pl.multiple_of(blocks[place] * BLK, BLK)
                        copies.append(
                            load(
                                rows.at[:, pl.ds(first, BLK)],
                                held.at[slot, :, j * BLK : (j + 1) * BLK],
                            )
                        )
                mine.append(slot)
                slot += 1
            slots.append(mine)
        return copies, slots, slot

    ahead = fetch(0, 0)
    for copy in shared:
        copy.wait()
    stores, done = [], 0
    for n, (_, parts) in enumerate(plan):
        copies, slots, slot = ahead
        if n + 1 < len(plan):
            ahead = fetch(n + 1, slot)
        for copy in copies:
            copy.wait()
        for (col, _, targets), mine in zip(parts, slots):
            total = jnp.dot(
                outs[col : col + WIDE, :], grads[n], preferred_element_type=jnp.float32
            )
            for k in mine:
                total = total + held[k].astype(jnp.float32)
            sent[done] = total.astype(sent.dtype)
            for out, row, first, count in targets:
                copy = pltpu.make_async_copy(
                    sent.at[done, :, first : first + count],
                    results[out].at[row : row + WIDE],
                    out_sems.at[len(stores)],
                )
                copy.start()
                stores.append(copy)
            done += 1
    for copy in stores:
        copy.wait()


def pieces(name, table, grads, outs, plan, arrived, out_shapes, after=()):
    cols, tokens = outs[0].shape
    parts = [part for _, each in plan for part in each]
    terms = [term for part in parts for term in part[1]]
    loads = 2 + 2 * sum(len(at) for at, _ in plan)
    loads += sum(1 if term[2] is None else len(term[2]) for term in terms)
    rows = SIDE * BLK
    scratch = [
        pltpu.VMEM((cols, 2 * tokens), jnp.bfloat16),
        pltpu.VMEM((len(plan), 2 * tokens, rows), jnp.bfloat16),
    ]
    if terms:
        scratch.append(pltpu.VMEM((len(terms), WIDE, rows), jnp.bfloat16))
    scratch += [
        pltpu.VMEM((len(parts), WIDE, rows), jnp.bfloat16),
        pltpu.SemaphoreType.DMA((loads,)),
        pltpu.SemaphoreType.DMA((sum(len(part[2]) for part in parts),)),
    ]
    operands = [*grads, *outs, *arrived, *after]
    return pl.pallas_call(
        lambda *refs: piece_kernel(plan, len(arrived), len(out_shapes), len(after), *refs),
        in_specs=[pl.BlockSpec(memory_space=pltpu.SMEM)]
        + [pl.BlockSpec(memory_space=pl.ANY)] * len(operands),
        out_specs=[pl.BlockSpec(memory_space=pl.ANY)] * len(out_shapes),
        out_shape=[pltpu.HBM(shape, jnp.bfloat16) for shape in out_shapes],
        scratch_shapes=scratch,
        compiler_params=params(PIECES_MIB),
        cost_estimate=cost(
            4 * tokens * rows * WIDE * len(parts),
            2 * (2 * tokens * (cols + len(plan) * rows) + (len(terms) + len(parts)) * rows * WIDE),
        ),
        name=name,
    )(table, *hbm(operands[:1]), *operands[1:])


def chunk(k):
    return [SIDE * k + j for j in range(SIDE)]


def far_stage(table, grads, outs, after):
    rows = SIDE * BLK
    plan = [(chunk(2), [(0, [], [(0, 0, 0, rows)]), (WIDE, [], [(1, 0, 0, rows)])])]
    plus, minus = pieces("far_pieces", table, grads, outs, plan, [], [(WIDE, rows)] * 2, after)
    return hop(plus, 1), hop(minus, -1)


def near_stage(table, grads, outs, after):
    rows = SIDE * BLK
    plan = [
        (chunk(1), [(WIDE, [], [(0, 0, 0, rows)])]),
        (chunk(3), [(0, [], [(1, 0, 0, rows)])]),
    ]
    plus, minus = pieces("near_pieces", table, grads, outs, plan, [], [(WIDE, rows)] * 2, after)
    return [hop(plus, 1), hop(minus, -1)], [plus, minus]


def join_stage(table, grads, outs, far, after):
    rows = SIDE * BLK
    plan = [
        (chunk(1), [(0, [(0, 0, None)], [(0, 0, 0, rows)])]),
        (chunk(3), [(WIDE, [(1, 0, None)], [(1, 0, 0, rows)])]),
    ]
    up, down = pieces("join_pieces", table, grads, outs, plan, far, [(WIDE, rows)] * 2, after)
    return [hop(up, 1), hop(down, -1)], [up, down]


def block_stage(table, grads, outs, near, joined):
    places = [ORDER + n for n in range(SIDE)]
    left = [(n, 0, n * BLK, BLK) for n in range(SIDE)]
    right = [(n, WIDE, n * BLK, BLK) for n in range(SIDE)]
    plan = [
        (
            [(place,) for place in places],
            [
                (0, [(2, 0, places), (1, 0, places)], left),
                (WIDE, [(0, 0, places), (3, 0, places)], right),
            ],
        )
    ]
    two, one, three, mine = pieces(
        "block_pieces", table, grads, outs, plan, [*near, *joined], [(2 * WIDE, BLK)] * SIDE
    )
    return mine, hop(two, 2, True), hop(one, 1, True), hop(three, -1, True)


def total_kernel(*refs):
    total = refs[0][...].astype(jnp.float32)
    for ref in refs[1:-1]:
        total = total + ref[...].astype(jnp.float32)
    refs[-1][...] = total.T


def total_gradient(terms):
    cols, rows = terms[0].shape
    return pl.pallas_call(
        total_kernel,
        in_specs=[pl.BlockSpec(memory_space=pltpu.VMEM)] * len(terms),
        out_specs=pl.BlockSpec(memory_space=pltpu.VMEM),
        out_shape=jax.ShapeDtypeStruct((rows, cols), jnp.float32),
        compiler_params=params(16),
        cost_estimate=cost(4 * rows * cols, 12 * rows * cols),
        name="total_gradient",
    )(*hbm(terms[:1]), *terms[1:])


def attend_kernel(
    low_ref, pos_ref, q_ref, g_ref, o_ref, key_ref, val_ref,
    kv4, kv3, kv2, kv1, after_plus, after_minus,
    packed_ref, own_ref, back4, back3, back2, back1,
    bias, held, keys, keys_t, vals, dkey, dval,
):
    tile = pl.program_id(0)
    scale = 1.0 / math.sqrt(HEAD)
    heads = q_ref.shape[1] // HEAD
    width = heads * TILE
    first = pl.multiple_of(tile * TILE, TILE)

    @pl.when(tile == 0)
    def _():
        for n, ref in enumerate((kv4, kv3, kv2, kv1)):
            keys[n * RUN : (n + 1) * RUN, :] = ref[:, :HEAD]
            vals[n * RUN : (n + 1) * RUN, :] = ref[:, HEAD:]
        keys[BACK * RUN :, :] = key_ref[...]
        vals[BACK * RUN :, :] = val_ref[...]
        keys_t[...] = keys[...].T
        dkey[...] = jnp.zeros_like(dkey)
        dval[...] = jnp.zeros_like(dval)

    row = lax.broadcasted_iota(jnp.int32, (SEEN, TILE), 0)
    col = lax.broadcasted_iota(jnp.int32, (SEEN, TILE), 1)
    low = low_ref[...] - first
    bias[...] = jnp.where((row >= low) & (row <= col + BACK * RUN), 0.0, NEG)

    def stack(ref):
        return jnp.concatenate([ref[:, h * HEAD : (h + 1) * HEAD] for h in range(heads)], axis=0)

    q, g = stack(q_ref), stack(g_ref)
    dots = []
    for h in range(heads):
        part = slice(h * HEAD, (h + 1) * HEAD)
        prod = g_ref[:, part].astype(jnp.float32) * o_ref[:, part].astype(jnp.float32)
        dots.append(jnp.sum(prod.T, axis=0, keepdims=True))
    row_dot = jnp.concatenate(dots, axis=1)
    top = jnp.full((1, width), 2 * NEG, jnp.float32)
    for at in range(0, SEEN, CHUNK):
        rows = pl.ds(pl.multiple_of(first + at, TILE), CHUNK)
        scores = lax.dot_general(keys[rows, :], q, NT, preferred_element_type=jnp.float32)
        mask = jnp.concatenate([bias[at : at + CHUNK, :]] * heads, axis=1)
        scores = scores * (scale * math.log2(math.e)) + mask
        held[at : at + CHUNK, :] = scores
        top = jnp.maximum(top, jnp.max(scores, axis=0, keepdims=True))
    total = jnp.zeros((1, width), jnp.float32)
    for at in range(0, SEEN, CHUNK):
        probs = jnp.exp2(held[at : at + CHUNK, :] - top)
        held[at : at + CHUNK, :] = probs
        total = total + jnp.sum(probs, axis=0, keepdims=True)
    inverse = 1.0 / total
    dq_t = jnp.zeros((HEAD, width), jnp.float32)
    for at in range(0, SEEN, CHUNK):
        rows = pl.ds(pl.multiple_of(first + at, TILE), CHUNK)
        probs = held[at : at + CHUNK, :] * inverse
        dval[rows, :] += jnp.dot(probs.astype(jnp.bfloat16), g, preferred_element_type=jnp.float32)
        prob_grad = lax.dot_general(vals[rows, :], g, NT, preferred_element_type=jnp.float32)
        score_grad = (probs * (prob_grad - row_dot)).astype(jnp.bfloat16)
        dkey[rows, :] += jnp.dot(score_grad, q, preferred_element_type=jnp.float32)
        dq_t += jnp.dot(keys_t[:, rows], score_grad, preferred_element_type=jnp.float32)
    dq_t = dq_t * scale
    dq = jnp.concatenate(
        [dq_t[:, h * TILE : (h + 1) * TILE].T for h in range(heads)], axis=1
    ).astype(jnp.bfloat16)
    slots = lax.broadcasted_iota(jnp.int32, (packed_ref.shape[0], TILE), 0)
    select = (slots == pos_ref[...]).astype(jnp.bfloat16)
    placed = jnp.dot(select, dq, preferred_element_type=jnp.float32).astype(jnp.bfloat16)

    @pl.when(tile == 0)
    def _():
        packed_ref[...] = placed

    @pl.when(tile > 0)
    def _():
        packed_ref[...] += placed

    @pl.when(tile == pl.num_programs(0) - 1)
    def _():
        for n, ref in enumerate((back4, back3, back2, back1)):
            rows = slice(n * RUN, (n + 1) * RUN)
            ref[:, :HEAD] = (dkey[rows, :] * scale).astype(jnp.bfloat16)
            ref[:, HEAD:] = dval[rows, :].astype(jnp.bfloat16)
        own_ref[:, :HEAD] = dkey[BACK * RUN :, :] * scale
        own_ref[:, HEAD:] = dval[BACK * RUN :, :]


def attend(low, pos, query, grad, out, key, value, earlier, slots, after):
    cols = query.shape[1]
    heads = cols // HEAD
    window = (BACK + 1) * RUN
    whole = lambda shape: pl.BlockSpec(shape, lambda t: (0, 0))
    by_tile = pl.BlockSpec((TILE, cols), lambda t: (t, 0))
    pair = (RUN, 2 * HEAD)
    return pl.pallas_call(
        attend_kernel,
        grid=(RUN // TILE,),
        in_specs=[pl.BlockSpec((1, TILE), lambda t: (0, t))] * 2
        + [by_tile] * 3
        + [whole((RUN, HEAD))] * 2
        + [whole(pair)] * BACK
        + [pl.BlockSpec(memory_space=pl.ANY)] * len(after),
        out_specs=[whole((slots, cols)), whole(pair)] + [whole(pair)] * BACK,
        out_shape=[
            pltpu.HBM((slots, cols), jnp.bfloat16),
            pltpu.HBM(pair, jnp.float32),
        ]
        + [pltpu.HBM(pair, jnp.bfloat16)] * BACK,
        scratch_shapes=[
            pltpu.VMEM((SEEN, TILE), jnp.float32),
            pltpu.VMEM((SEEN, heads * TILE), jnp.float32),
            pltpu.VMEM((window, HEAD), jnp.bfloat16),
            pltpu.VMEM((HEAD, window), jnp.bfloat16),
            pltpu.VMEM((window, HEAD), jnp.bfloat16),
            pltpu.VMEM((window, HEAD), jnp.float32),
            pltpu.VMEM((window, HEAD), jnp.float32),
        ],
        compiler_params=params(32),
        cost_estimate=cost(10 * heads * RUN * window * HEAD, 8 * MIB, heads * RUN * window),
        name="attend",
    )(*hbm([low, pos, query]), grad, *hbm([out, key, value]), *earlier, *after)


def route_rows(slot_blocks, own_index, parties, block_rows):
    total = slot_blocks.shape[0]
    ids = jnp.arange(total, dtype=jnp.int32)
    slot_of_block = jnp.sum(
        jnp.where(slot_blocks[None, :] == ids[:, None], ids[None, :], 0), axis=1
    )
    local = jnp.arange(parties, dtype=jnp.int32)

    def place(peer, order):
        earlier = (peer[:, None] == peer[None, :]) & (order[None, :] < order[:, None])
        return peer * CAP + jnp.sum(earlier, axis=1).astype(jnp.int32)

    dest_slot = lax.dynamic_slice_in_dim(slot_of_block, own_index * parties, parties, 0)
    held = lax.dynamic_slice_in_dim(slot_blocks, own_index * parties, parties, 0)
    rows = jnp.arange(block_rows, dtype=jnp.int32)

    def spread(at):
        return (at[:, None] * block_rows + rows[None, :]).reshape(-1)

    return spread(place(dest_slot // parties, dest_slot)), spread(place(held // parties, local))


def on_device(
    grad_out, out_weight, query_states, key_states, value_tensor, attn_out, doc_ids, block_order
):
    parties = lax.axis_size("ctx")
    own_index = lax.axis_index("ctx")
    core = lax.axis_index("dp")
    x, y = own_index // SIDE, own_index % SIDE
    grad_rows, out_rows = grad_out[0], attn_out[0]
    doc_row = doc_ids[0]
    key, value = key_states[0], value_tensor[0]

    both = jnp.concatenate([key, value], axis=1)
    earlier = [lax.ppermute(both, "ctx", run_shift(k, parties)) for k in range(BACK, 0, -1)]

    table = block_table(x, y, core)
    grads = [grad_rows, swap_cores(grad_rows)]
    turned = turn(out_rows, grads[1])
    outs = [turned, swap_cores(turned)]
    attn_grad = project(grad_rows, out_weight, turned)
    far = far_stage(table, grads, outs, [*earlier, attn_grad])
    near, near_sent = near_stage(table, grads, outs, [attn_grad])
    joined, joined_sent = join_stage(table, grads, outs, far, hbm(near_sent))
    own_docs = lax.dynamic_slice_in_dim(doc_row, own_index * RUN, RUN, 0)
    start = jnp.maximum(own_index - BACK, 0) * RUN
    seen_docs = lax.dynamic_slice_in_dim(doc_row, start, (BACK + 1) * RUN, 0)
    first = start + jnp.sum((seen_docs[:, None] < own_docs[None, :]).astype(jnp.int32), axis=0)
    low = (first - (own_index - BACK) * RUN).reshape(1, RUN)
    send_rows, held_rows = route_rows(block_order[0], own_index, parties, RUN // parties)
    slots = CAP * RUN
    packed, own_kv, *back = attend(
        low,
        send_rows.reshape(1, RUN),
        query_states[0],
        attn_grad,
        out_rows,
        key,
        value,
        earlier,
        slots,
        hbm(joined_sent),
    )
    got = lax.all_to_all(
        packed.reshape(parties, slots // parties, -1), "ctx", 0, 0, tiled=True
    ).reshape(slots, -1)
    held_select = (
        held_rows[:, None] == jnp.arange(slots, dtype=jnp.int32)[None, :]
    ).astype(jnp.bfloat16)
    query_grad = jnp.dot(held_select, got, preferred_element_type=jnp.float32).astype(jnp.bfloat16)
    returned = [
        lax.ppermute(v, "ctx", run_shift(-k, parties)) for v, k in zip(back, range(BACK, 0, -1))
    ]
    kv_sum = own_kv
    for v in returned:
        kv_sum = kv_sum + v.astype(jnp.float32)
    kv_sum = kv_sum.astype(jnp.bfloat16)
    weight_grad = total_gradient(block_stage(table, grads, outs, near, joined))
    return (
        query_grad[None],
        kv_sum[None, :, :HEAD],
        kv_sum[None, :, HEAD:],
        weight_grad,
    )


def solution(mesh):
    heads = P("dp", "ctx", "tp")
    in_specs = (
        P("dp", "ctx", None),
        P(None, "tp"),
        heads,
        heads,
        heads,
        heads,
        P("dp", None),
        P("dp", None),
    )
    out_specs = (heads, heads, heads, P(("ctx", "dp"), "tp"))
    return jax.shard_map(
        on_device, mesh=mesh, in_specs=in_specs, out_specs=out_specs, check_vma=False
    )
```

time: 119 us -> 106 us (0.89)
  the two profiles are of different devices: /device:TPU:0 before, /device:TPU:1 now
where the time goes in v3:
time: 106 us; the launch traced here: 105 us
  Pallas kernels  41.5 us (39%)
  starting transfers between devices  34.2 us (32%)
  waiting for transfers between devices  21.1 us (20%)
  other arithmetic  2.77 us (3%)
  local copies, waits for them, and re-layouts  2.56 us (2%)
  matrix products  2.5 us (2%)
    pallas_call x4, Pallas kernels, pieces(): pl.pallas_call(lambda *refs: piece_kernel(plan, len(arrived), len(out_sha...  19.4 us
    ppermute x9, waiting for transfers between devices, hop(): return lax.ppermute(value, ('ctx', 'dp'), axis_shift(k, second))  15.6 us
    ppermute x9, starting transfers between devices, hop(): return lax.ppermute(value, ('ctx', 'dp'), axis_shift(k, second))  14.8 us
    pallas_call x1, Pallas kernels, attend(): pl.pallas_call(attend_kernel, grid=(RUN // TILE,), in_specs=[pl.BlockSpec...  11.6 us
    pallas_call x1, Pallas kernels, project(): pl.pallas_call(project_kernel, in_specs=[pl.BlockSpec(memory_space=pl.ANY...  7.94 us
    ppermute x4, starting transfers between devices, on_device(): lax.ppermute(v, 'ctx', run_shift(-k, parties))  6.33 us
    ppermute x4, starting transfers between devices, on_device(): lax.ppermute(both, 'ctx', run_shift(k, parties))  6.07 us
    ppermute x4, waiting for transfers between devices, on_device(): lax.ppermute(v, 'ctx', run_shift(-k, parties))  4.87 us
  transfers between devices with their start and end apart: 20, of which 6 were waited for; matrix products, arithmetic and copies ran while one was open for 6% of the time, Pallas kernels for 33%

profile of v3, /device:TPU:1, one launch (start us, length us, event | category | flops | bytes accessed | tf_op | source)
XLA Modules:
  0.0 105.4 jit_solution(4900138830834625702)
XLA Ops:
  0.7 1.5 %collective-permute-start = (bf16[256,8192]{1,0:T(8,128)(2,1)}, bf16[256,8192]{1,0:T(8,128)(2,1)}, u32[]{:S(2)}, u32[]{:S(2)}) collective-permute-start(bf16[256,8192]{1,0:T(8,128)(2,1)} %bitcast.30), channel_id=1, source_target_pairs={{0,1},{1,0},{2,3},{3,2},{4,5},{5,4},{6,7},{7,6},{8,9},{9,8},{10,11... | collective-permute-start | bytes 12582920 | tf_op jit(solution)/shard_map/ppermute | solution.py:47
  3.0 1.4 %collective-permute-start.1 = (bf16[256,256]{1,0:T(8,128)(2,1)S(1)}, bf16[256,256]{1,0:T(8,128)(2,1)S(1)}, u32[]{:S(2)}, u32[]{:S(2)}) collective-permute-start(bf16[256,256]{1,0:T(8,128)(2,1)S(1)} %pad_maximum_fusion), channel_id=1, source_target_pairs={{0,32},{8,40},{16,48},{24,56},{32,64},{40,72},{48,80},{56,88},{64,... | collective-permute-start | bytes 393224 | tf_op jit(solution)/shard_map/ppermute | solution.py:490
  4.4 2.7 %collective-permute-start.2 = (bf16[256,256]{1,0:T(8,128)(2,1)S(1)}, bf16[256,256]{1,0:T(8,128)(2,1)S(1)}, u32[]{:S(2)}, u32[]{:S(2)}) collective-permute-start(bf16[256,256]{1,0:T(8,128)(2,1)S(1)} %pad_maximum_fusion), channel_id=1, source_target_pairs={{0,24},{8,32},{16,40},{24,48},{32,56},{40,64},{48,72},{56,80},{64,... | collective-permute-start | bytes 393224 | tf_op jit(solution)/shard_map/ppermute | solution.py:490
  7.1 1.3 %collective-permute-start.3 = (bf16[256,256]{1,0:T(8,128)(2,1)S(1)}, bf16[256,256]{1,0:T(8,128)(2,1)S(1)}, u32[]{:S(2)}, u32[]{:S(2)}) collective-permute-start(bf16[256,256]{1,0:T(8,128)(2,1)S(1)} %pad_maximum_fusion), channel_id=1, source_target_pairs={{0,16},{8,24},{16,32},{24,40},{32,48},{40,56},{48,64},{56,72},{64,... | collective-permute-start | bytes 393224 | tf_op jit(solution)/shard_map/ppermute | solution.py:490
  10.5 1.1 %collective-permute-start.5 = (bf16[1024,256]{1,0:T(8,128)(2,1)S(1)}, bf16[1024,256]{1,0:T(8,128)(2,1)S(1)}, u32[]{:S(2)}, u32[]{:S(2)}) collective-permute-start(bf16[1024,256]{1,0:T(8,128)(2,1)S(1)} %turn.1.after_ref.refs_3_), channel_id=1, source_target_pairs={{0,1},{1,0},{2,3},{3,2},{4,5},{5,4},{6,7},{7,6},{8,9},{9,8},{10,11... | collective-permute-start | bytes 1572872 | tf_op jit(solution)/shard_map/ppermute | solution.py:47
  11.8 7.9 %project.1.refs_9_.refs_5_.g_ref = bf16[256,1024]{1,0:T(8,128)(2,1)S(1)} custom-call(bf16[256,8192]{1,0:T(8,128)(2,1)} %bitcast.31, bf16[8192,1024]{1,0:T(8,128)(2,1)} %weight_ref.1, bf16[1024,256]{1,0:T(8,128)(2,1)S(1)} %turn.1.after_ref.refs_3_), custom_call_target="tpu_custom_call" | custom-call | flops 4294967296 | bytes 20971520 | tf_op jit(solution)/shard_map/project/pallas_call | solution.py:91
  20.4 4.3 %far_pieces.1 = (bf16[512,1024]{1,0:T(8,128)(2,1)}, bf16[512,1024]{1,0:T(8,128)(2,1)}) custom-call(s32[21]{0:T(128)S(1)} %pad_add_fusion.refs_0_, bf16[256,8192]{1,0:T(8,128)(2,1)} %bitcast.32, bf16[256,8192]{1,0:T(8,128)(2,1)} %collective-permute-done.refs_1_.refs_2_, bf16[1024,256]{1,0:T(8,128)(2,1)S(1)} %turn.1.after_ref.refs_3_, ...), custom_call_target="tpu_custom_call" | custom-call | flops 1073741824 | bytes 4194304 | tf_op jit(solution)/shard_map/far_pieces/pallas_call | solution.py:247
  25.9 1.6 %collective-permute-start.7 = (bf16[512,1024]{1,0:T(8,128)(2,1)}, bf16[512,1024]{1,0:T(8,128)(2,1)}, u32[]{:S(2)}, u32[]{:S(2)}) collective-permute-start(bf16[512,1024]{1,0:T(8,128)(2,1)} %get-tuple-element.21), channel_id=1, source_target_pairs={{0,96},{1,25},{8,104},{9,1},{16,112},{17,9},{24,120},{25,17},{32,0... | collective-permute-start | bytes 3145736 | tf_op jit(solution)/shard_map/ppermute | solution.py:43
  28.0 4.5 %near_pieces.1 = (bf16[512,1024]{1,0:T(8,128)(2,1)}, bf16[512,1024]{1,0:T(8,128)(2,1)}) custom-call(s32[21]{0:T(128)S(1)} %pad_add_fusion.refs_0_, bf16[256,8192]{1,0:T(8,128)(2,1)} %bitcast.33, bf16[256,8192]{1,0:T(8,128)(2,1)} %collective-permute-done.refs_1_.refs_2_, bf16[1024,256]{1,0:T(8,128)(2,1)S(1)} %turn.1.after_ref.refs_3_, ...), custom_call_target="tpu_custom_call" | custom-call | flops 1073741824 | bytes 5242880 | tf_op jit(solution)/shard_map/near_pieces/pallas_call | solution.py:247
  32.6 2.7 %collective-permute-start.13 = (bf16[512,1024]{1,0:T(8,128)(2,1)}, bf16[512,1024]{1,0:T(8,128)(2,1)}, u32[]{:S(2)}, u32[]{:S(2)}) collective-permute-start(bf16[512,1024]{1,0:T(8,128)(2,1)} %get-tuple-element.23.refs_8_), channel_id=1, source_target_pairs={{0,96},{1,25},{8,104},{9,1},{16,112},{17,9},{24,120},{25,17},{32,0... | collective-permute-start | bytes 3145736 | tf_op jit(solution)/shard_map/ppermute | solution.py:43
  35.2 5.1 %collective-permute-done.6.refs_5_ = bf16[512,1024]{1,0:T(8,128)(2,1)} collective-permute-done((bf16[512,1024]{1,0:T(8,128)(2,1)}, bf16[512,1024]{1,0:T(8,128)(2,1)}, u32[]{:S(2)}, u32[]{:S(2)}) %collective-permute-start.6) | collective-permute-done | bytes 1048608 | tf_op jit(solution)/shard_map/ppermute | solution.py:43
  40.3 4.9 %join_pieces.1 = (bf16[512,1024]{1,0:T(8,128)(2,1)}, bf16[512,1024]{1,0:T(8,128)(2,1)}) custom-call(s32[21]{0:T(128)S(1)} %pad_add_fusion.refs_0_, bf16[256,8192]{1,0:T(8,128)(2,1)} %bitcast.34, bf16[256,8192]{1,0:T(8,128)(2,1)} %collective-permute-done.refs_1_.refs_2_, bf16[1024,256]{1,0:T(8,128)(2,1)S(1)} %turn.1.after_ref.refs_3_, ...), custom_call_target="tpu_custom_call" | custom-call | flops 1073741824 | bytes 7340032 | tf_op jit(solution)/shard_map/join_pieces/pallas_call | solution.py:247
  46.5 2.7 %collective-permute-start.15 = (bf16[512,1024]{1,0:T(8,128)(2,1)}, bf16[512,1024]{1,0:T(8,128)(2,1)}, u32[]{:S(2)}, u32[]{:S(2)}) collective-permute-start(bf16[512,1024]{1,0:T(8,128)(2,1)} %get-tuple-element.25.after_minus), channel_id=1, source_target_pairs={{0,96},{1,25},{8,104},{9,1},{16,112},{17,9},{24,120},{25,17},{32,0... | collective-permute-start | bytes 3145736 | tf_op jit(solution)/shard_map/ppermute | solution.py:43
  50.0 11.6 %attend.1 = (bf16[512,1024]{1,0:T(8,128)(2,1)}, f32[256,256]{1,0:T(8,128)}, bf16[256,256]{1,0:T(8,128)(2,1)}, bf16[256,256]{1,0:T(8,128)(2,1)}, bf16[256,256]{1,0:T(8,128)(2,1)}, /*index=5*/bf16[256,256]{1,0:T(8,128)(2,1)}) custom-call(s32[1,256]{1,0:T(1,128)} %bitcast.43, s32[1,256]{1,0:T(1,128)} %add.164.pos_ref, bf16[256,1024]{1,0:T(8,128)(2,1)} %bitcast.44, ...), custom_call_target="tpu_custom_call" | custom-call | flops 3355443200 | bytes 8388608 | tf_op jit(solution)/shard_map/attend/pallas_call | solution.py:427
  61.6 4.3 %all-to-all-start = ((bf16[16,32,1024]{2,1,0:T(8,128)(2,1)}), bf16[16,32,1024]{2,1,0:T(8,128)(2,1)}, u32[]{:S(2)}, u32[]{:S(2)}) async-start(bf16[16,32,1024]{2,1,0:T(8,128)(2,1)} %bitcast.36), calls=%async_computation | async-start | bytes 2097152 | tf_op jit(solution)/shard_map/all_to_all | solution.py:519
  65.9 4.7 %collective-permute-start.11 = (bf16[256,256]{1,0:T(8,128)(2,1)}, bf16[256,256]{1,0:T(8,128)(2,1)S(1)}, u32[]{:S(2)}, u32[]{:S(2)}) collective-permute-start(bf16[256,256]{1,0:T(8,128)(2,1)} %get-tuple-element.31), channel_id=1, source_target_pairs={{0,120},{8,0},{16,8},{24,16},{32,24},{40,32},{48,40},{56,48},{64,5... | collective-permute-start | bytes 393224 | tf_op jit(solution)/shard_map/ppermute | solution.py:527
  72.4 5.6 %block_pieces.1 = (bf16[1024,256]{1,0:T(8,128)(2,1)}, bf16[1024,256]{1,0:T(8,128)(2,1)}, bf16[1024,256]{1,0:T(8,128)(2,1)}, bf16[1024,256]{1,0:T(8,128)(2,1)}) custom-call(s32[21]{0:T(128)S(1)} %pad_add_fusion.refs_0_, bf16[256,8192]{1,0:T(8,128)(2,1)} %bitcast.35, bf16[256,8192]{1,0:T(8,128)(2,1)} %collective-permute-done.refs_1_.refs_2_, ...), custom_call_target="tpu_custom_call" | custom-call | flops 1073741824 | bytes 8388608 | tf_op jit(solution)/shard_map/block_pieces/pallas_call | solution.py:247
  78.1 2.5 %collective-permute-start.16 = (bf16[1024,256]{1,0:T(8,128)(2,1)}, bf16[1024,256]{1,0:T(8,128)(2,1)S(1)}, u32[]{:S(2)}, u32[]{:S(2)}) collective-permute-start(bf16[1024,256]{1,0:T(8,128)(2,1)} %get-tuple-element.33), channel_id=1, source_target_pairs={{0,16},{1,65},{8,24},{9,73},{16,0},{17,81},{24,8},{25,89},{32,48},... | collective-permute-start | bytes 1572872 | tf_op jit(solution)/shard_map/ppermute | solution.py:43
  80.6 2.9 %collective-permute-start.17 = (bf16[1024,256]{1,0:T(8,128)(2,1)}, bf16[1024,256]{1,0:T(8,128)(2,1)S(1)}, u32[]{:S(2)}, u32[]{:S(2)}) collective-permute-start(bf16[1024,256]{1,0:T(8,128)(2,1)} %get-tuple-element.34), channel_id=1, source_target_pairs={{0,8},{1,33},{8,16},{9,41},{16,24},{17,49},{24,0},{25,57},{32,40},... | collective-permute-start | bytes 1572872 | tf_op jit(solution)/shard_map/ppermute | solution.py:43
  83.5 4.9 %collective-permute-done.10 = bf16[256,256]{1,0:T(8,128)(2,1)S(1)} collective-permute-done((bf16[256,256]{1,0:T(8,128)(2,1)}, bf16[256,256]{1,0:T(8,128)(2,1)S(1)}, u32[]{:S(2)}, u32[]{:S(2)}) %collective-permute-start.10) | collective-permute-done | bytes 131104 | tf_op jit(solution)/shard_map/ppermute | solution.py:527
  90.0 2.5 %fusion = bf16[1,256,1024]{2,1,0:T(8,128)(2,1)} fusion(bf16[512,1024]{1,0:T(8,128)(2,1)} %bitcast.12, s32[256]{0:T(256)S(1)} %add.156), kind=kOutput, calls=%fused_computation.2 | convolution fusion | flops 268828672 | bytes 1573888 | tf_op jit(solution)/shard_map/dot_general | solution.py:525
  92.5 3.8 %collective-permute-done.17.refs_2_ = bf16[1024,256]{1,0:T(8,128)(2,1)S(1)} collective-permute-done((bf16[1024,256]{1,0:T(8,128)(2,1)}, bf16[1024,256]{1,0:T(8,128)(2,1)S(1)}, u32[]{:S(2)}, u32[]{:S(2)}) %collective-permute-start.17) | collective-permute-done | bytes 524320 | tf_op jit(solution)/shard_map/ppermute | solution.py:43
  96.3 6.7 %collective-permute-done.18.refs_3_ = bf16[1024,256]{1,0:T(8,128)(2,1)S(1)} collective-permute-done((bf16[1024,256]{1,0:T(8,128)(2,1)}, bf16[1024,256]{1,0:T(8,128)(2,1)S(1)}, u32[]{:S(2)}, u32[]{:S(2)}) %collective-permute-start.18) | collective-permute-done | bytes 524320 | tf_op jit(solution)/shard_map/ppermute | solution.py:43
  103.0 2.4 %total_gradient.1 = f32[256,1024]{1,0:T(8,128)} custom-call(bf16[1024,256]{1,0:T(8,128)(2,1)} %get-tuple-element.32.refs_0_, bf16[1024,256]{1,0:T(8,128)(2,1)S(1)} %collective-permute-done.16.refs_1_, bf16[1024,256]{1,0:T(8,128)(2,1)S(1)} %collective-permute-done.17.refs_2_, bf16[1024,256]{1,0:T(8,128)(2,1)S(1)} %collective-permute-done.18.refs_3_), custom_call_target="tpu_custom_call" | custom-call | flops 1048576 | bytes 3145728 | tf_op jit(solution)/shard_map/total_gradient/pallas_call | solution.py:322
  (58 shorter events, 10.9 us)
Async XLA Ops:
  0.6 26.9 %copy-start = (s32[1,4096]{1,0:T(1,128)S(1)}, s32[1,4096]{1,0:T(1,128)}, u32[]{:S(2)}) copy-start(s32[1,4096]{1,0:T(1,128)} %param.14) | copy-start | bytes 49156
  0.6 11.0 %copy-start.4 = (s32[4]{0:T(128)S(1)}, s32[4]{0:T(128)}, u32[]{:S(2)}) copy-start(s32[4]{0:T(128)} %constant.86.clone.1) | copy-start | bytes 52
  0.7 8.6 %collective-permute-start = (bf16[256,8192]{1,0:T(8,128)(2,1)}, bf16[256,8192]{1,0:T(8,128)(2,1)}, u32[]{:S(2)}, u32[]{:S(2)}) collective-permute-start(bf16[256,8192]{1,0:T(8,128)(2,1)} %bitcast.30), channel_id=1, source_target_pairs={{0,1},{1,0},{2,3},{3,2},{4,5},{5,4},{6,7},{7,6},{8,9},{9,8},{10,11... | collective-permute-start | bytes 12582920 | tf_op jit(solution)/shard_map/ppermute | solution.py:47
  3.0 16.7 %collective-permute-start.1 = (bf16[256,256]{1,0:T(8,128)(2,1)S(1)}, bf16[256,256]{1,0:T(8,128)(2,1)S(1)}, u32[]{:S(2)}, u32[]{:S(2)}) collective-permute-start(bf16[256,256]{1,0:T(8,128)(2,1)S(1)} %pad_maximum_fusion), channel_id=1, source_target_pairs={{0,32},{8,40},{16,48},{24,56},{32,64},{40,72},{48,80},{56,88},{64,... | collective-permute-start | bytes 393224 | tf_op jit(solution)/shard_map/ppermute | solution.py:490
  4.4 15.4 %collective-permute-start.2 = (bf16[256,256]{1,0:T(8,128)(2,1)S(1)}, bf16[256,256]{1,0:T(8,128)(2,1)S(1)}, u32[]{:S(2)}, u32[]{:S(2)}) collective-permute-start(bf16[256,256]{1,0:T(8,128)(2,1)S(1)} %pad_maximum_fusion), channel_id=1, source_target_pairs={{0,24},{8,32},{16,40},{24,48},{32,56},{40,64},{48,72},{56,80},{64,... | collective-permute-start | bytes 393224 | tf_op jit(solution)/shard_map/ppermute | solution.py:490
  7.1 12.7 %collective-permute-start.3 = (bf16[256,256]{1,0:T(8,128)(2,1)S(1)}, bf16[256,256]{1,0:T(8,128)(2,1)S(1)}, u32[]{:S(2)}, u32[]{:S(2)}) collective-permute-start(bf16[256,256]{1,0:T(8,128)(2,1)S(1)} %pad_maximum_fusion), channel_id=1, source_target_pairs={{0,16},{8,24},{16,32},{24,40},{32,48},{40,56},{48,64},{56,72},{64,... | collective-permute-start | bytes 393224 | tf_op jit(solution)/shard_map/ppermute | solution.py:490
  8.4 12.0 %collective-permute-start.4 = (bf16[256,256]{1,0:T(8,128)(2,1)S(1)}, bf16[256,256]{1,0:T(8,128)(2,1)S(1)}, u32[]{:S(2)}, u32[]{:S(2)}) collective-permute-start(bf16[256,256]{1,0:T(8,128)(2,1)S(1)} %pad_maximum_fusion), channel_id=1, source_target_pairs={{0,8},{8,16},{16,24},{24,32},{32,40},{40,48},{48,56},{56,64},{64,7... | collective-permute-start | bytes 393224 | tf_op jit(solution)/shard_map/ppermute | solution.py:490
  10.5 9.9 %collective-permute-start.5 = (bf16[1024,256]{1,0:T(8,128)(2,1)S(1)}, bf16[1024,256]{1,0:T(8,128)(2,1)S(1)}, u32[]{:S(2)}, u32[]{:S(2)}) collective-permute-start(bf16[1024,256]{1,0:T(8,128)(2,1)S(1)} %turn.1.after_ref.refs_3_), channel_id=1, source_target_pairs={{0,1},{1,0},{2,3},{3,2},{4,5},{5,4},{6,7},{7,6},{8,9},{9,8},{10,11... | collective-permute-start | bytes 1572872 | tf_op jit(solution)/shard_map/ppermute | solution.py:47
  19.8 7.7 %copy-start.3 = (s32[1,256]{1,0:T(1,128)S(1)}, s32[1,256]{1,0:T(1,128)}, u32[]{:S(2)}) copy-start(s32[1,256]{1,0:T(1,128)} %param.15) | copy-start | bytes 3076
  24.7 15.5 %collective-permute-start.6 = (bf16[512,1024]{1,0:T(8,128)(2,1)}, bf16[512,1024]{1,0:T(8,128)(2,1)}, u32[]{:S(2)}, u32[]{:S(2)}) collective-permute-start(bf16[512,1024]{1,0:T(8,128)(2,1)} %get-tuple-element.20), channel_id=1, source_target_pairs={{0,32},{1,9},{8,40},{9,17},{16,48},{17,25},{24,56},{25,1},{32,64},... | collective-permute-start | bytes 3145736 | tf_op jit(solution)/shard_map/ppermute | solution.py:43
  25.9 14.4 %collective-permute-start.7 = (bf16[512,1024]{1,0:T(8,128)(2,1)}, bf16[512,1024]{1,0:T(8,128)(2,1)}, u32[]{:S(2)}, u32[]{:S(2)}) collective-permute-start(bf16[512,1024]{1,0:T(8,128)(2,1)} %get-tuple-element.21), channel_id=1, source_target_pairs={{0,96},{1,25},{8,104},{9,1},{16,112},{17,9},{24,120},{25,17},{32,0... | collective-permute-start | bytes 3145736 | tf_op jit(solution)/shard_map/ppermute | solution.py:43
  32.5 38.1 %collective-permute-start.12 = (bf16[512,1024]{1,0:T(8,128)(2,1)}, bf16[512,1024]{1,0:T(8,128)(2,1)S(1)}, u32[]{:S(2)}, u32[]{:S(2)}) collective-permute-start(bf16[512,1024]{1,0:T(8,128)(2,1)} %get-tuple-element.22.refs_7_), channel_id=1, source_target_pairs={{0,32},{1,9},{8,40},{9,17},{16,48},{17,25},{24,56},{25,1},{32,64},... | collective-permute-start | bytes 3145736 | tf_op jit(solution)/shard_map/ppermute | solution.py:43
  32.6 38.6 %collective-permute-start.13 = (bf16[512,1024]{1,0:T(8,128)(2,1)}, bf16[512,1024]{1,0:T(8,128)(2,1)}, u32[]{:S(2)}, u32[]{:S(2)}) collective-permute-start(bf16[512,1024]{1,0:T(8,128)(2,1)} %get-tuple-element.23.refs_8_), channel_id=1, source_target_pairs={{0,96},{1,25},{8,104},{9,1},{16,112},{17,9},{24,120},{25,17},{32,0... | collective-permute-start | bytes 3145736 | tf_op jit(solution)/shard_map/ppermute | solution.py:43
  45.2 26.8 %collective-permute-start.14 = (bf16[512,1024]{1,0:T(8,128)(2,1)}, bf16[512,1024]{1,0:T(8,128)(2,1)}, u32[]{:S(2)}, u32[]{:S(2)}) collective-permute-start(bf16[512,1024]{1,0:T(8,128)(2,1)} %get-tuple-element.24.after_plus), channel_id=1, source_target_pairs={{0,32},{1,9},{8,40},{9,17},{16,48},{17,25},{24,56},{25,1},{32,64},... | collective-permute-start | bytes 3145736 | tf_op jit(solution)/shard_map/ppermute | solution.py:43
  46.5 25.9 %collective-permute-start.15 = (bf16[512,1024]{1,0:T(8,128)(2,1)}, bf16[512,1024]{1,0:T(8,128)(2,1)}, u32[]{:S(2)}, u32[]{:S(2)}) collective-permute-start(bf16[512,1024]{1,0:T(8,128)(2,1)} %get-tuple-element.25.after_minus), channel_id=1, source_target_pairs={{0,96},{1,25},{8,104},{9,1},{16,112},{17,9},{24,120},{25,17},{32,0... | collective-permute-start | bytes 3145736 | tf_op jit(solution)/shard_map/ppermute | solution.py:43
  61.6 28.4 %all-to-all-start = ((bf16[16,32,1024]{2,1,0:T(8,128)(2,1)}), bf16[16,32,1024]{2,1,0:T(8,128)(2,1)}, u32[]{:S(2)}, u32[]{:S(2)}) async-start(bf16[16,32,1024]{2,1,0:T(8,128)(2,1)} %bitcast.36), calls=%async_computation | async-start | bytes 2097152 | tf_op jit(solution)/shard_map/all_to_all | solution.py:519
  65.9 14.7 %collective-permute-start.11 = (bf16[256,256]{1,0:T(8,128)(2,1)}, bf16[256,256]{1,0:T(8,128)(2,1)S(1)}, u32[]{:S(2)}, u32[]{:S(2)}) collective-permute-start(bf16[256,256]{1,0:T(8,128)(2,1)} %get-tuple-element.31), channel_id=1, source_target_pairs={{0,120},{8,0},{16,8},{24,16},{32,24},{40,32},{48,40},{56,48},{64,5... | collective-permute-start | bytes 393224 | tf_op jit(solution)/shard_map/ppermute | solution.py:527
  70.6 17.8 %collective-permute-start.10 = (bf16[256,256]{1,0:T(8,128)(2,1)}, bf16[256,256]{1,0:T(8,128)(2,1)S(1)}, u32[]{:S(2)}, u32[]{:S(2)}) collective-permute-start(bf16[256,256]{1,0:T(8,128)(2,1)} %get-tuple-element.30), channel_id=1, source_target_pairs={{0,112},{8,120},{16,0},{24,8},{32,16},{40,24},{48,32},{56,40},{64,... | collective-permute-start | bytes 393224 | tf_op jit(solution)/shard_map/ppermute | solution.py:527
  71.2 18.1 %collective-permute-start.9 = (bf16[256,256]{1,0:T(8,128)(2,1)}, bf16[256,256]{1,0:T(8,128)(2,1)S(1)}, u32[]{:S(2)}, u32[]{:S(2)}) collective-permute-start(bf16[256,256]{1,0:T(8,128)(2,1)} %get-tuple-element.29), channel_id=1, source_target_pairs={{0,104},{8,112},{16,120},{24,0},{32,8},{40,16},{48,24},{56,32},{64... | collective-permute-start | bytes 393224 | tf_op jit(solution)/shard_map/ppermute | solution.py:527
  72.0 17.2 %collective-permute-start.8 = (bf16[256,256]{1,0:T(8,128)(2,1)}, bf16[256,256]{1,0:T(8,128)(2,1)S(1)}, u32[]{:S(2)}, u32[]{:S(2)}) collective-permute-start(bf16[256,256]{1,0:T(8,128)(2,1)} %get-tuple-element.28), channel_id=1, source_target_pairs={{0,96},{8,104},{16,112},{24,120},{32,0},{40,8},{48,16},{56,24},{64... | collective-permute-start | bytes 393224 | tf_op jit(solution)/shard_map/ppermute | solution.py:527
  72.4 16.8 %copy-start.2 = (f32[256,256]{1,0:T(8,128)S(1)}, f32[256,256]{1,0:T(8,128)}, u32[]{:S(2)}) copy-start(f32[256,256]{1,0:T(8,128)} %get-tuple-element.27) | copy-start | bytes 786436
  78.1 14.5 %collective-permute-start.16 = (bf16[1024,256]{1,0:T(8,128)(2,1)}, bf16[1024,256]{1,0:T(8,128)(2,1)S(1)}, u32[]{:S(2)}, u32[]{:S(2)}) collective-permute-start(bf16[1024,256]{1,0:T(8,128)(2,1)} %get-tuple-element.33), channel_id=1, source_target_pairs={{0,16},{1,65},{8,24},{9,73},{16,0},{17,81},{24,8},{25,89},{32,48},... | collective-permute-start | bytes 1572872 | tf_op jit(solution)/shard_map/ppermute | solution.py:43
  80.6 15.7 %collective-permute-start.17 = (bf16[1024,256]{1,0:T(8,128)(2,1)}, bf16[1024,256]{1,0:T(8,128)(2,1)S(1)}, u32[]{:S(2)}, u32[]{:S(2)}) collective-permute-start(bf16[1024,256]{1,0:T(8,128)(2,1)} %get-tuple-element.34), channel_id=1, source_target_pairs={{0,8},{1,33},{8,16},{9,41},{16,24},{17,49},{24,0},{25,57},{32,40},... | collective-permute-start | bytes 1572872 | tf_op jit(solution)/shard_map/ppermute | solution.py:43
  88.4 14.6 %collective-permute-start.18 = (bf16[1024,256]{1,0:T(8,128)(2,1)}, bf16[1024,256]{1,0:T(8,128)(2,1)S(1)}, u32[]{:S(2)}, u32[]{:S(2)}) collective-permute-start(bf16[1024,256]{1,0:T(8,128)(2,1)} %get-tuple-element.35), channel_id=1, source_target_pairs={{0,24},{1,97},{8,0},{9,105},{16,8},{17,113},{24,16},{25,121},{32,5... | collective-permute-start | bytes 1572872 | tf_op jit(solution)/shard_map/ppermute | solution.py:43
  (1 other events, 1.0 us)

commit v4 on v3

--- a/solution.py
+++ b/solution.py
@@ -15,9 +15,10 @@
 BLK = 256
 TILE = 128
 SEEN = BACK * RUN + TILE
-CHUNK = 384
+CHUNK = 1152
 PIECES_MIB = 24
 WIDE = 512
+PAIR = 2 * HEAD
 NEG = -1e30
 MIB = 1024 * 1024
 NT = (((1,), (1,)), ((), ()))
@@ -132,14 +133,14 @@
         compiler_params=params(8),
         cost_estimate=cost(0, 4 * rows * cols),
         name="turn",
-    )(value, after)
-
-
-def piece_kernel(plan, arrived_count, out_count, extra, blocks, *refs):
+    )(*hbm([value]), after)
+
+
+def piece_kernel(plan, arrived_count, out_count, extra, carried, blocks, *refs):
     grad_refs, out_refs = refs[:2], refs[2:4]
     arrived_refs = refs[4 : 4 + arrived_count]
     refs = refs[4 + arrived_count + extra :]
-    results, refs = refs[:out_count], refs[out_count:]
+    results, refs = refs[:out_count], refs[out_count + carried :]
     if arrived_count:
         outs, grads, held, sent, in_sems, out_sems = refs
     else:
@@ -225,7 +226,7 @@
         copy.wait()
 
 
-def pieces(name, table, grads, outs, plan, arrived, out_shapes, after=()):
+def pieces(name, table, grads, outs, plan, arrived, out_shapes, after=(), carried=()):
     cols, tokens = outs[0].shape
     parts = [part for _, each in plan for part in each]
     terms = [term for part in parts for term in part[1]]
@@ -244,12 +245,18 @@
         pltpu.SemaphoreType.DMA((sum(len(part[2]) for part in parts),)),
     ]
     operands = [*grads, *outs, *arrived, *after]
+    at, extra = 1 + len(operands), len(after) + len(carried)
+    operands += hbm(carried)
     return pl.pallas_call(
-        lambda *refs: piece_kernel(plan, len(arrived), len(out_shapes), len(after), *refs),
+        lambda *refs: piece_kernel(
+            plan, len(arrived), len(out_shapes), extra, len(carried), *refs
+        ),
         in_specs=[pl.BlockSpec(memory_space=pltpu.SMEM)]
         + [pl.BlockSpec(memory_space=pl.ANY)] * len(operands),
-        out_specs=[pl.BlockSpec(memory_space=pl.ANY)] * len(out_shapes),
-        out_shape=[pltpu.HBM(shape, jnp.bfloat16) for shape in out_shapes],
+        out_specs=[pl.BlockSpec(memory_space=pl.ANY)] * (len(out_shapes) + len(carried)),
+        out_shape=[pltpu.HBM(shape, jnp.bfloat16) for shape in out_shapes]
+        + [pltpu.HBM(v.shape, v.dtype) for v in carried],
+        input_output_aliases={at + n: len(out_shapes) + n for n in range(len(carried))},
         scratch_shapes=scratch,
         compiler_params=params(PIECES_MIB),
         cost_estimate=cost(
@@ -268,7 +275,7 @@
     rows = SIDE * BLK
     plan = [(chunk(2), [(0, [], [(0, 0, 0, rows)]), (WIDE, [], [(1, 0, 0, rows)])])]
     plus, minus = pieces("far_pieces", table, grads, outs, plan, [], [(WIDE, rows)] * 2, after)
-    return hop(plus, 1), hop(minus, -1)
+    return [hop(plus, 1), hop(minus, -1)], [plus, minus]
 
 
 def near_stage(table, grads, outs, after):
@@ -305,9 +312,15 @@
         )
     ]
     two, one, three, mine = pieces(
-        "block_pieces", table, grads, outs, plan, [*near, *joined], [(2 * WIDE, BLK)] * SIDE
+        "block_pieces",
+        table,
+        grads,
+        outs,
+        plan,
+        [*near, *joined],
+        [(2 * WIDE, BLK)] * SIDE,
     )
-    return mine, hop(two, 2, True), hop(one, 1, True), hop(three, -1, True)
+    return [mine, hop(two, 2, True), hop(one, 1, True), hop(three, -1, True)]
 
 
 def total_kernel(*refs):
@@ -333,7 +346,7 @@
 def attend_kernel(
     low_ref, pos_ref, q_ref, g_ref, o_ref, key_ref, val_ref,
     kv4, kv3, kv2, kv1, after_plus, after_minus,
-    packed_ref, own_ref, back4, back3, back2, back1,
+    packed_ref, own_ref, back4, back32, back1,
     bias, held, keys, keys_t, vals, dkey, dval,
 ):
     tile = pl.program_id(0)
@@ -409,10 +422,10 @@
 
     @pl.when(tile == pl.num_programs(0) - 1)
     def _():
-        for n, ref in enumerate((back4, back3, back2, back1)):
+        for n, (ref, at) in enumerate(((back4, 0), (back32, PAIR), (back32, 0), (back1, 0))):
             rows = slice(n * RUN, (n + 1) * RUN)
-            ref[:, :HEAD] = (dkey[rows, :] * scale).astype(jnp.bfloat16)
-            ref[:, HEAD:] = dval[rows, :].astype(jnp.bfloat16)
+            ref[:, at : at + HEAD] = (dkey[rows, :] * scale).astype(jnp.bfloat16)
+            ref[:, at + HEAD : at + PAIR] = dval[rows, :].astype(jnp.bfloat16)
         own_ref[:, :HEAD] = dkey[BACK * RUN :, :] * scale
         own_ref[:, HEAD:] = dval[BACK * RUN :, :]
 
@@ -423,7 +436,7 @@
     window = (BACK + 1) * RUN
     whole = lambda shape: pl.BlockSpec(shape, lambda t: (0, 0))
     by_tile = pl.BlockSpec((TILE, cols), lambda t: (t, 0))
-    pair = (RUN, 2 * HEAD)
+    pair, double = (RUN, PAIR), (RUN, 2 * PAIR)
     return pl.pallas_call(
         attend_kernel,
         grid=(RUN // TILE,),
@@ -432,12 +445,12 @@
         + [whole((RUN, HEAD))] * 2
         + [whole(pair)] * BACK
         + [pl.BlockSpec(memory_space=pl.ANY)] * len(after),
-        out_specs=[whole((slots, cols)), whole(pair)] + [whole(pair)] * BACK,
+        out_specs=[whole((slots, cols)), whole(pair), whole(pair), whole(double), whole(pair)],
         out_shape=[
             pltpu.HBM((slots, cols), jnp.bfloat16),
             pltpu.HBM(pair, jnp.float32),
         ]
-        + [pltpu.HBM(pair, jnp.bfloat16)] * BACK,
+        + [pltpu.HBM(shape, jnp.bfloat16) for shape in (pair, double, pair)],
         scratch_shapes=[
             pltpu.VMEM((SEEN, TILE), jnp.float32),
             pltpu.VMEM((SEEN, heads * TILE), jnp.float32),
@@ -493,10 +506,10 @@
     grads = [grad_rows, swap_cores(grad_rows)]
     turned = turn(out_rows, grads[1])
     outs = [turned, swap_cores(turned)]
-    attn_grad = project(grad_rows, out_weight, turned)
-    far = far_stage(table, grads, outs, [*earlier, attn_grad])
-    near, near_sent = near_stage(table, grads, outs, [attn_grad])
-    joined, joined_sent = join_stage(table, grads, outs, far, hbm(near_sent))
+    far, far_sent = far_stage(table, grads, outs, earlier)
+    near, near_sent = near_stage(table, grads, outs, hbm(far_sent))
+    attn_grad = project(grad_rows, out_weight, *hbm(near_sent[:1]))
+    joined, joined_sent = join_stage(table, grads, outs, far, [attn_grad])
     own_docs = lax.dynamic_slice_in_dim(doc_row, own_index * RUN, RUN, 0)
     start = jnp.maximum(own_index - BACK, 0) * RUN
     seen_docs = lax.dynamic_slice_in_dim(doc_row, start, (BACK + 1) * RUN, 0)
@@ -504,7 +517,7 @@
     low = (first - (own_index - BACK) * RUN).reshape(1, RUN)
     send_rows, held_rows = route_rows(block_order[0], own_index, parties, RUN // parties)
     slots = CAP * RUN
-    packed, own_kv, *back = attend(
+    packed, own_kv, back4, back32, back1 = attend(
         low,
         send_rows.reshape(1, RUN),
         query_states[0],
@@ -523,14 +536,17 @@
         held_rows[:, None] == jnp.arange(slots, dtype=jnp.int32)[None, :]
     ).astype(jnp.bfloat16)
     query_grad = jnp.dot(held_select, got, preferred_element_type=jnp.float32).astype(jnp.bfloat16)
-    returned = [
-        lax.ppermute(v, "ctx", run_shift(-k, parties)) for v, k in zip(back, range(BACK, 0, -1))
-    ]
+    terms = block_stage(table, grads, outs, near, joined)
+    back32 = lax.ppermute(back32, "ctx", run_shift(-2, parties))
+    back4 = lax.ppermute(back4, "ctx", run_shift(-4, parties))
+    joint = back1.astype(jnp.float32) + back32[:, PAIR:].astype(jnp.float32)
+    back1 = lax.ppermute(joint.astype(jnp.bfloat16), "ctx", run_shift(-1, parties))
+    returned = [back32[:, :PAIR], back4, back1]
     kv_sum = own_kv
     for v in returned:
         kv_sum = kv_sum + v.astype(jnp.float32)
     kv_sum = kv_sum.astype(jnp.bfloat16)
-    weight_grad = total_gradient(block_stage(table, grads, outs, near, joined))
+    weight_grad = total_gradient(terms)
     return (
         query_grad[None],
         kv_sum[None, :, :HEAD],

time: 106 us -> 104 us (0.981)
  the two profiles are of different devices: /device:TPU:1 before, /device:TPU:0 now
where the time goes in v4:
time: 104 us; the launch traced here: 103 us
  Pallas kernels  41.5 us (40%)
  starting transfers between devices  36.3 us (35%)
  waiting for transfers between devices  11.8 us (11%)
  other arithmetic  7.22 us (7%)
  local copies, waits for them, and re-layouts  2.63 us (3%)
  matrix products  2.51 us (2%)
    pallas_call x4, Pallas kernels, pieces(): pl.pallas_call(lambda *refs: piece_kernel(plan, len(arrived), len(out_sha...  18.7 us
    ppermute x9, starting transfers between devices, hop(): return lax.ppermute(value, ('ctx', 'dp'), axis_shift(k, second))  12.2 us
    pallas_call x1, Pallas kernels, attend(): pl.pallas_call(attend_kernel, grid=(RUN // TILE,), in_specs=[pl.BlockSpec...  11.3 us
    ppermute x9, waiting for transfers between devices, hop(): return lax.ppermute(value, ('ctx', 'dp'), axis_shift(k, second))  8.77 us
    ppermute x4, starting transfers between devices, on_device(): lax.ppermute(both, 'ctx', run_shift(k, parties))  8.4 us
    pallas_call x1, Pallas kernels, project(): pl.pallas_call(project_kernel, in_specs=[pl.BlockSpec(memory_space=pl.ANY...  7.94 us
    ppermute x1, starting transfers between devices, on_device(): lax.ppermute(joint.astype(jnp.bfloat16), 'ctx', run_shift(-1, parties))  5.87 us
    all_to_all x1, starting transfers between devices, on_device(): lax.all_to_all(packed.reshape(parties, slots // parties, -1), 'ctx', 0, 0...  4.54 us
  transfers between devices with their start and end apart: 19, of which 5 were waited for; matrix products, arithmetic and copies ran while one was open for 11% of the time, Pallas kernels for 34%

profile of v4, /device:TPU:0, one launch (start us, length us, event | category | flops | bytes accessed | tf_op | source)
XLA Modules:
  0.0 102.8 jit_solution(8527693211631834018)
XLA Ops:
  1.6 1.7 %collective-permute-start.5 = (bf16[256,256]{1,0:T(8,128)(2,1)S(1)}, bf16[256,256]{1,0:T(8,128)(2,1)S(1)}, u32[]{:S(2)}, u32[]{:S(2)}) collective-permute-start(bf16[256,256]{1,0:T(8,128)(2,1)S(1)} %pad_maximum_fusion), channel_id=1, source_target_pairs={{0,8},{8,16},{16,24},{24,32},{32,40},{40,48},{48,56},{56,64},{64,7... | collective-permute-start | bytes 393224 | tf_op jit(solution)/shard_map/ppermute | solution.py:503
  3.4 2.9 %collective-permute-start.4 = (bf16[256,256]{1,0:T(8,128)(2,1)S(1)}, bf16[256,256]{1,0:T(8,128)(2,1)S(1)}, u32[]{:S(2)}, u32[]{:S(2)}) collective-permute-start(bf16[256,256]{1,0:T(8,128)(2,1)S(1)} %pad_maximum_fusion), channel_id=1, source_target_pairs={{0,16},{8,24},{16,32},{24,40},{32,48},{40,56},{48,64},{56,72},{64,... | collective-permute-start | bytes 393224 | tf_op jit(solution)/shard_map/ppermute | solution.py:503
  6.3 2.3 %collective-permute-start.3 = (bf16[256,256]{1,0:T(8,128)(2,1)S(1)}, bf16[256,256]{1,0:T(8,128)(2,1)S(1)}, u32[]{:S(2)}, u32[]{:S(2)}) collective-permute-start(bf16[256,256]{1,0:T(8,128)(2,1)S(1)} %pad_maximum_fusion), channel_id=1, source_target_pairs={{0,24},{8,32},{16,40},{24,48},{32,56},{40,64},{48,72},{56,80},{64,... | collective-permute-start | bytes 393224 | tf_op jit(solution)/shard_map/ppermute | solution.py:503
  8.6 1.5 %collective-permute-start.2 = (bf16[256,256]{1,0:T(8,128)(2,1)S(1)}, bf16[256,256]{1,0:T(8,128)(2,1)S(1)}, u32[]{:S(2)}, u32[]{:S(2)}) collective-permute-start(bf16[256,256]{1,0:T(8,128)(2,1)S(1)} %pad_maximum_fusion), channel_id=1, source_target_pairs={{0,32},{8,40},{16,48},{24,56},{32,64},{40,72},{48,80},{56,88},{64,... | collective-permute-start | bytes 393224 | tf_op jit(solution)/shard_map/ppermute | solution.py:503
  15.7 4.3 %far_pieces.1 = (bf16[512,1024]{1,0:T(8,128)(2,1)}, bf16[512,1024]{1,0:T(8,128)(2,1)}) custom-call(s32[21]{0:T(128)S(1)} %pad_add_fusion.refs_0_, bf16[256,8192]{1,0:T(8,128)(2,1)} %bitcast.29, bf16[256,8192]{1,0:T(8,128)(2,1)} %collective-permute-done.refs_1_.refs_2_, bf16[1024,256]{1,0:T(8,128)(2,1)S(1)} %turn.1.refs_3_, ...), custom_call_target="tpu_custom_call" | custom-call | flops 1073741824 | bytes 4194304 | tf_op jit(solution)/shard_map/far_pieces/pallas_call | solution.py:250
  21.2 2.0 %collective-permute-start.7 = (bf16[512,1024]{1,0:T(8,128)(2,1)}, bf16[512,1024]{1,0:T(8,128)(2,1)S(1)}, u32[]{:S(2)}, u32[]{:S(2)}) collective-permute-start(bf16[512,1024]{1,0:T(8,128)(2,1)} %get-tuple-element.20.refs_6_), channel_id=1, source_target_pairs={{0,96},{1,25},{8,104},{9,1},{16,112},{17,9},{24,120},{25,17},{32,0... | collective-permute-start | bytes 3145736 | tf_op jit(solution)/shard_map/ppermute | solution.py:44
  24.2 4.5 %near_pieces.1 = (bf16[512,1024]{1,0:T(8,128)(2,1)}, bf16[512,1024]{1,0:T(8,128)(2,1)}) custom-call(s32[21]{0:T(128)S(1)} %pad_add_fusion.refs_0_, bf16[256,8192]{1,0:T(8,128)(2,1)} %bitcast.30, bf16[256,8192]{1,0:T(8,128)(2,1)} %collective-permute-done.refs_1_.refs_2_, bf16[1024,256]{1,0:T(8,128)(2,1)S(1)} %turn.1.refs_3_, ...), custom_call_target="tpu_custom_call" | custom-call | flops 1073741824 | bytes 5242880 | tf_op jit(solution)/shard_map/near_pieces/pallas_call | solution.py:250
  29.3 1.5 %collective-permute-start.11 = (bf16[512,1024]{1,0:T(8,128)(2,1)}, bf16[512,1024]{1,0:T(8,128)(2,1)S(1)}, u32[]{:S(2)}, u32[]{:S(2)}) collective-permute-start(bf16[512,1024]{1,0:T(8,128)(2,1)} %get-tuple-element.21.after_ref), channel_id=1, source_target_pairs={{0,32},{1,9},{8,40},{9,17},{16,48},{17,25},{24,56},{25,1},{32,64},... | collective-permute-start | bytes 3145736 | tf_op jit(solution)/shard_map/ppermute | solution.py:44
  30.8 7.9 %project.1.refs_7_.g_ref = bf16[256,1024]{1,0:T(8,128)(2,1)S(1)} custom-call(bf16[256,8192]{1,0:T(8,128)(2,1)} %bitcast.31, bf16[8192,1024]{1,0:T(8,128)(2,1)} %weight_ref.1, bf16[512,1024]{1,0:T(8,128)(2,1)} %get-tuple-element.21.after_ref), custom_call_target="tpu_custom_call" | custom-call | flops 4294967296 | bytes 20971520 | tf_op jit(solution)/shard_map/project/pallas_call | solution.py:92
  38.8 4.6 %join_pieces.1 = (bf16[512,1024]{1,0:T(8,128)(2,1)}, bf16[512,1024]{1,0:T(8,128)(2,1)}) custom-call(s32[21]{0:T(128)S(1)} %pad_add_fusion.refs_0_, bf16[256,8192]{1,0:T(8,128)(2,1)} %bitcast.32, bf16[256,8192]{1,0:T(8,128)(2,1)} %collective-permute-done.refs_1_.refs_2_, bf16[1024,256]{1,0:T(8,128)(2,1)S(1)} %turn.1.refs_3_, ...), custom_call_target="tpu_custom_call" | custom-call | flops 1073741824 | bytes 7340032 | tf_op jit(solution)/shard_map/join_pieces/pallas_call | solution.py:250
  43.4 3.2 %collective-permute-start.14 = (bf16[512,1024]{1,0:T(8,128)(2,1)}, bf16[512,1024]{1,0:T(8,128)(2,1)}, u32[]{:S(2)}, u32[]{:S(2)}) collective-permute-start(bf16[512,1024]{1,0:T(8,128)(2,1)} %get-tuple-element.23.after_minus), channel_id=1, source_target_pairs={{0,96},{1,25},{8,104},{9,1},{16,112},{17,9},{24,120},{25,17},{32,0... | collective-permute-start | bytes 3145736 | tf_op jit(solution)/shard_map/ppermute | solution.py:44
  46.6 11.3 %attend.1 = (bf16[512,1024]{1,0:T(8,128)(2,1)}, f32[256,256]{1,0:T(8,128)}, bf16[256,256]{1,0:T(8,128)(2,1)}, bf16[256,512]{1,0:T(8,128)(2,1)}, bf16[256,256]{1,0:T(8,128)(2,1)}) custom-call(s32[1,256]{1,0:T(1,128)} %bitcast.43, s32[1,256]{1,0:T(1,128)} %add.164.pos_ref, bf16[256,1024]{1,0:T(8,128)(2,1)} %bitcast.44, ...), custom_call_target="tpu_custom_call" | custom-call | flops 3355443200 | bytes 8388608 | tf_op jit(solution)/shard_map/attend/pallas_call | solution.py:440
  57.9 4.0 %collective-permute-start.8 = (bf16[256,512]{1,0:T(8,128)(2,1)}, bf16[256,512]{1,0:T(8,128)(2,1)S(1)}, u32[]{:S(2)}, u32[]{:S(2)}) collective-permute-start(bf16[256,512]{1,0:T(8,128)(2,1)} %get-tuple-element.26), channel_id=1, source_target_pairs={{0,112},{8,120},{16,0},{24,8},{32,16},{40,24},{48,32},{56,40},{64,... | collective-permute-start | bytes 786440 | tf_op jit(solution)/shard_map/ppermute | solution.py:540
  62.2 4.5 %all-to-all-start = ((bf16[16,32,1024]{2,1,0:T(8,128)(2,1)}), bf16[16,32,1024]{2,1,0:T(8,128)(2,1)}, u32[]{:S(2)}, u32[]{:S(2)}) async-start(bf16[16,32,1024]{2,1,0:T(8,128)(2,1)} %bitcast.34), calls=%async_computation | async-start | bytes 2097152 | tf_op jit(solution)/shard_map/all_to_all | solution.py:532
  66.7 2.1 %collective-permute-done.8 = bf16[256,512]{1,0:T(8,128)(2,1)S(1)} collective-permute-done((bf16[256,512]{1,0:T(8,128)(2,1)}, bf16[256,512]{1,0:T(8,128)(2,1)S(1)}, u32[]{:S(2)}, u32[]{:S(2)}) %collective-permute-start.8) | collective-permute-done | bytes 262176 | tf_op jit(solution)/shard_map/ppermute | solution.py:540
  69.9 1.6 %add_convert_fusion.1 = bf16[256,256]{1,0:T(8,128)(2,1)} fusion(bf16[256,256]{1,0:T(8,128)(2,1)} %get-tuple-element.28, bf16[256,512]{1,0:T(8,128)(2,1)S(1)} %collective-permute-done.8), kind=kLoop, calls=%fused_computation.5 | loop fusion | flops 262144 | bytes 393216 | tf_op jit(solution)/shard_map/convert_element_type | solution.py:543
  71.5 5.9 %collective-permute-start.10 = (bf16[256,256]{1,0:T(8,128)(2,1)}, bf16[256,256]{1,0:T(8,128)(2,1)}, u32[]{:S(2)}, u32[]{:S(2)}) collective-permute-start(bf16[256,256]{1,0:T(8,128)(2,1)} %add_convert_fusion.1), channel_id=1, source_target_pairs={{0,120},{8,0},{16,8},{24,16},{32,24},{40,32},{48,40},{56,48},{64,5... | collective-permute-start | bytes 393224 | tf_op jit(solution)/shard_map/ppermute | solution.py:543
  78.6 5.3 %block_pieces.1 = (bf16[1024,256]{1,0:T(8,128)(2,1)}, bf16[1024,256]{1,0:T(8,128)(2,1)}, bf16[1024,256]{1,0:T(8,128)(2,1)}, bf16[1024,256]{1,0:T(8,128)(2,1)}) custom-call(s32[21]{0:T(128)S(1)} %copy-done.4, bf16[256,8192]{1,0:T(8,128)(2,1)} %bitcast.33, bf16[256,8192]{1,0:T(8,128)(2,1)} %collective-permute-done.refs_1_.refs_2_, ...), custom_call_target="tpu_custom_call" | custom-call | flops 1073741824 | bytes 8388608 | tf_op jit(solution)/shard_map/block_pieces/pallas_call | solution.py:250
  84.2 1.4 %collective-permute-start.16 = (bf16[1024,256]{1,0:T(8,128)(2,1)}, bf16[1024,256]{1,0:T(8,128)(2,1)S(1)}, u32[]{:S(2)}, u32[]{:S(2)}) collective-permute-start(bf16[1024,256]{1,0:T(8,128)(2,1)} %get-tuple-element.32), channel_id=1, source_target_pairs={{0,8},{1,33},{8,16},{9,41},{16,24},{17,49},{24,0},{25,57},{32,40},... | collective-permute-start | bytes 1572872 | tf_op jit(solution)/shard_map/ppermute | solution.py:44
  85.6 1.8 %collective-permute-start.17 = (bf16[1024,256]{1,0:T(8,128)(2,1)}, bf16[1024,256]{1,0:T(8,128)(2,1)S(1)}, u32[]{:S(2)}, u32[]{:S(2)}) collective-permute-start(bf16[1024,256]{1,0:T(8,128)(2,1)} %get-tuple-element.33), channel_id=1, source_target_pairs={{0,24},{1,97},{8,0},{9,105},{16,8},{17,113},{24,16},{25,121},{32,5... | collective-permute-start | bytes 1572872 | tf_op jit(solution)/shard_map/ppermute | solution.py:44
  89.2 2.5 %fusion = bf16[1,256,1024]{2,1,0:T(8,128)(2,1)} fusion(bf16[512,1024]{1,0:T(8,128)(2,1)} %bitcast.12, s32[256]{0:T(256)} %add.156), kind=kOutput, calls=%fused_computation.2 | convolution fusion | flops 268828672 | bytes 1573888 | tf_op jit(solution)/shard_map/dot_general | solution.py:538
  91.7 3.4 %collective-permute-done.15.refs_1_ = bf16[1024,256]{1,0:T(8,128)(2,1)S(1)} collective-permute-done((bf16[1024,256]{1,0:T(8,128)(2,1)}, bf16[1024,256]{1,0:T(8,128)(2,1)S(1)}, u32[]{:S(2)}, u32[]{:S(2)}) %collective-permute-start.15) | collective-permute-done | bytes 524320 | tf_op jit(solution)/shard_map/ppermute | solution.py:44
  95.0 5.4 %collective-permute-done.16.refs_2_ = bf16[1024,256]{1,0:T(8,128)(2,1)S(1)} collective-permute-done((bf16[1024,256]{1,0:T(8,128)(2,1)}, bf16[1024,256]{1,0:T(8,128)(2,1)S(1)}, u32[]{:S(2)}, u32[]{:S(2)}) %collective-permute-start.16) | collective-permute-done | bytes 524320 | tf_op jit(solution)/shard_map/ppermute | solution.py:44
  100.4 2.4 %total_gradient.1 = f32[256,1024]{1,0:T(8,128)} custom-call(bf16[1024,256]{1,0:T(8,128)(2,1)} %get-tuple-element.30.refs_0_, bf16[1024,256]{1,0:T(8,128)(2,1)S(1)} %collective-permute-done.15.refs_1_, bf16[1024,256]{1,0:T(8,128)(2,1)S(1)} %collective-permute-done.16.refs_2_, bf16[1024,256]{1,0:T(8,128)(2,1)S(1)} %collective-permute-done.17.refs_3_), custom_call_target="tpu_custom_call" | custom-call | flops 1048576 | bytes 3145728 | tf_op jit(solution)/shard_map/total_gradient/pallas_call | solution.py:335
  (69 shorter events, 13.9 us)
Async XLA Ops:
  0.6 14.0 %copy-start = (s32[1,4096]{1,0:T(1,128)S(1)}, s32[1,4096]{1,0:T(1,128)}, u32[]{:S(2)}) copy-start(s32[1,4096]{1,0:T(1,128)} %param.14) | copy-start | bytes 49156
  0.6 13.2 %copy-start.10 = (s32[4]{0:T(128)S(1)}, s32[4]{0:T(128)}, u32[]{:S(2)}) copy-start(s32[4]{0:T(128)} %constant.86.clone.1) | copy-start | bytes 52
  0.7 11.8 %collective-permute-start = (bf16[256,8192]{1,0:T(8,128)(2,1)}, bf16[256,8192]{1,0:T(8,128)(2,1)}, u32[]{:S(2)}, u32[]{:S(2)}) collective-permute-start(bf16[256,8192]{1,0:T(8,128)(2,1)} %bitcast.28), channel_id=1, source_target_pairs={{0,1},{1,0},{2,3},{3,2},{4,5},{5,4},{6,7},{7,6},{8,9},{9,8},{10,11... | collective-permute-start | bytes 12582920 | tf_op jit(solution)/shard_map/ppermute | solution.py:48
  1.6 13.1 %collective-permute-start.5 = (bf16[256,256]{1,0:T(8,128)(2,1)S(1)}, bf16[256,256]{1,0:T(8,128)(2,1)S(1)}, u32[]{:S(2)}, u32[]{:S(2)}) collective-permute-start(bf16[256,256]{1,0:T(8,128)(2,1)S(1)} %pad_maximum_fusion), channel_id=1, source_target_pairs={{0,8},{8,16},{16,24},{24,32},{32,40},{40,48},{48,56},{56,64},{64,7... | collective-permute-start | bytes 393224 | tf_op jit(solution)/shard_map/ppermute | solution.py:503
  3.4 11.3 %collective-permute-start.4 = (bf16[256,256]{1,0:T(8,128)(2,1)S(1)}, bf16[256,256]{1,0:T(8,128)(2,1)S(1)}, u32[]{:S(2)}, u32[]{:S(2)}) collective-permute-start(bf16[256,256]{1,0:T(8,128)(2,1)S(1)} %pad_maximum_fusion), channel_id=1, source_target_pairs={{0,16},{8,24},{16,32},{24,40},{32,48},{40,56},{48,64},{56,72},{64,... | collective-permute-start | bytes 393224 | tf_op jit(solution)/shard_map/ppermute | solution.py:503
  6.3 8.5 %collective-permute-start.3 = (bf16[256,256]{1,0:T(8,128)(2,1)S(1)}, bf16[256,256]{1,0:T(8,128)(2,1)S(1)}, u32[]{:S(2)}, u32[]{:S(2)}) collective-permute-start(bf16[256,256]{1,0:T(8,128)(2,1)S(1)} %pad_maximum_fusion), channel_id=1, source_target_pairs={{0,24},{8,32},{16,40},{24,48},{32,56},{40,64},{48,72},{56,80},{64,... | collective-permute-start | bytes 393224 | tf_op jit(solution)/shard_map/ppermute | solution.py:503
  8.6 6.3 %collective-permute-start.2 = (bf16[256,256]{1,0:T(8,128)(2,1)S(1)}, bf16[256,256]{1,0:T(8,128)(2,1)S(1)}, u32[]{:S(2)}, u32[]{:S(2)}) collective-permute-start(bf16[256,256]{1,0:T(8,128)(2,1)S(1)} %pad_maximum_fusion), channel_id=1, source_target_pairs={{0,32},{8,40},{16,48},{24,56},{32,64},{40,72},{48,80},{56,88},{64,... | collective-permute-start | bytes 393224 | tf_op jit(solution)/shard_map/ppermute | solution.py:503
  13.7 2.0 %collective-permute-start.1 = (bf16[1024,256]{1,0:T(8,128)(2,1)S(1)}, bf16[1024,256]{1,0:T(8,128)(2,1)S(1)}, u32[]{:S(2)}, u32[]{:S(2)}) collective-permute-start(bf16[1024,256]{1,0:T(8,128)(2,1)S(1)} %turn.1.refs_3_), channel_id=1, source_target_pairs={{0,1},{1,0},{2,3},{3,2},{4,5},{5,4},{6,7},{7,6},{8,9},{9,8},{10,11... | collective-permute-start | bytes 1572872 | tf_op jit(solution)/shard_map/ppermute | solution.py:48
  14.7 24.1 %copy-start.3 = (s32[21]{0:T(128)}, s32[21]{0:T(128)S(1)}, u32[]{:S(2)}) copy-start(s32[21]{0:T(128)S(1)} %pad_add_fusion.refs_0_) | copy-start | bytes 256
  20.0 18.8 %collective-permute-start.6 = (bf16[512,1024]{1,0:T(8,128)(2,1)}, bf16[512,1024]{1,0:T(8,128)(2,1)S(1)}, u32[]{:S(2)}, u32[]{:S(2)}) collective-permute-start(bf16[512,1024]{1,0:T(8,128)(2,1)} %get-tuple-element.19.refs_5_), channel_id=1, source_target_pairs={{0,32},{1,9},{8,40},{9,17},{16,48},{17,25},{24,56},{25,1},{32,64},... | collective-permute-start | bytes 3145736 | tf_op jit(solution)/shard_map/ppermute | solution.py:44
  21.2 17.5 %collective-permute-start.7 = (bf16[512,1024]{1,0:T(8,128)(2,1)}, bf16[512,1024]{1,0:T(8,128)(2,1)S(1)}, u32[]{:S(2)}, u32[]{:S(2)}) collective-permute-start(bf16[512,1024]{1,0:T(8,128)(2,1)} %get-tuple-element.20.refs_6_), channel_id=1, source_target_pairs={{0,96},{1,25},{8,104},{9,1},{16,112},{17,9},{24,120},{25,17},{32,0... | collective-permute-start | bytes 3145736 | tf_op jit(solution)/shard_map/ppermute | solution.py:44
  28.7 42.8 %collective-permute-start.12 = (bf16[512,1024]{1,0:T(8,128)(2,1)}, bf16[512,1024]{1,0:T(8,128)(2,1)S(1)}, u32[]{:S(2)}, u32[]{:S(2)}) collective-permute-start(bf16[512,1024]{1,0:T(8,128)(2,1)} %get-tuple-element.29), channel_id=1, source_target_pairs={{0,96},{1,25},{8,104},{9,1},{16,112},{17,9},{24,120},{25,17},{32,0... | collective-permute-start | bytes 3145736 | tf_op jit(solution)/shard_map/ppermute | solution.py:44
  29.3 48.7 %collective-permute-start.11 = (bf16[512,1024]{1,0:T(8,128)(2,1)}, bf16[512,1024]{1,0:T(8,128)(2,1)S(1)}, u32[]{:S(2)}, u32[]{:S(2)}) collective-permute-start(bf16[512,1024]{1,0:T(8,128)(2,1)} %get-tuple-element.21.after_ref), channel_id=1, source_target_pairs={{0,32},{1,9},{8,40},{9,17},{16,48},{17,25},{24,56},{25,1},{32,64},... | collective-permute-start | bytes 3145736 | tf_op jit(solution)/shard_map/ppermute | solution.py:44
  43.3 34.7 %collective-permute-start.13 = (bf16[512,1024]{1,0:T(8,128)(2,1)}, bf16[512,1024]{1,0:T(8,128)(2,1)}, u32[]{:S(2)}, u32[]{:S(2)}) collective-permute-start(bf16[512,1024]{1,0:T(8,128)(2,1)} %get-tuple-element.22.after_plus), channel_id=1, source_target_pairs={{0,32},{1,9},{8,40},{9,17},{16,48},{17,25},{24,56},{25,1},{32,64},... | collective-permute-start | bytes 3145736 | tf_op jit(solution)/shard_map/ppermute | solution.py:44
  43.4 34.6 %collective-permute-start.14 = (bf16[512,1024]{1,0:T(8,128)(2,1)}, bf16[512,1024]{1,0:T(8,128)(2,1)}, u32[]{:S(2)}, u32[]{:S(2)}) collective-permute-start(bf16[512,1024]{1,0:T(8,128)(2,1)} %get-tuple-element.23.after_minus), channel_id=1, source_target_pairs={{0,96},{1,25},{8,104},{9,1},{16,112},{17,9},{24,120},{25,17},{32,0... | collective-permute-start | bytes 3145736 | tf_op jit(solution)/shard_map/ppermute | solution.py:44
  46.6 15.3 %copy-start.9 = (s32[16]{0:T(128)S(1)}, s32[16]{0:T(128)}, u32[]{:S(2)}) copy-start(s32[16]{0:T(128)} %get-tuple-element.38) | copy-start | bytes 196
  57.9 10.9 %collective-permute-start.8 = (bf16[256,512]{1,0:T(8,128)(2,1)}, bf16[256,512]{1,0:T(8,128)(2,1)S(1)}, u32[]{:S(2)}, u32[]{:S(2)}) collective-permute-start(bf16[256,512]{1,0:T(8,128)(2,1)} %get-tuple-element.26), channel_id=1, source_target_pairs={{0,112},{8,120},{16,0},{24,8},{32,16},{40,24},{48,32},{56,40},{64,... | collective-permute-start | bytes 786440 | tf_op jit(solution)/shard_map/ppermute | solution.py:540
  62.2 27.0 %all-to-all-start = ((bf16[16,32,1024]{2,1,0:T(8,128)(2,1)}), bf16[16,32,1024]{2,1,0:T(8,128)(2,1)}, u32[]{:S(2)}, u32[]{:S(2)}) async-start(bf16[16,32,1024]{2,1,0:T(8,128)(2,1)} %bitcast.34), calls=%async_computation | async-start | bytes 2097152 | tf_op jit(solution)/shard_map/all_to_all | solution.py:532
  68.8 9.2 %copy-start.6 = (bf16[256,512]{1,0:T(8,128)(2,1)}, bf16[256,512]{1,0:T(8,128)(2,1)S(1)}, u32[]{:S(2)}) copy-start(bf16[256,512]{1,0:T(8,128)(2,1)S(1)} %collective-permute-done.8) | copy-start | bytes 786436
  68.8 18.6 %collective-permute-start.9 = (bf16[256,256]{1,0:T(8,128)(2,1)}, bf16[256,256]{1,0:T(8,128)(2,1)}, u32[]{:S(2)}, u32[]{:S(2)}) collective-permute-start(bf16[256,256]{1,0:T(8,128)(2,1)} %get-tuple-element.27), channel_id=1, source_target_pairs={{0,96},{8,104},{16,112},{24,120},{32,0},{40,8},{48,16},{56,24},{64... | collective-permute-start | bytes 393224 | tf_op jit(solution)/shard_map/ppermute | solution.py:541
  71.5 16.0 %collective-permute-start.10 = (bf16[256,256]{1,0:T(8,128)(2,1)}, bf16[256,256]{1,0:T(8,128)(2,1)}, u32[]{:S(2)}, u32[]{:S(2)}) collective-permute-start(bf16[256,256]{1,0:T(8,128)(2,1)} %add_convert_fusion.1), channel_id=1, source_target_pairs={{0,120},{8,0},{16,8},{24,16},{32,24},{40,32},{48,40},{56,48},{64,5... | collective-permute-start | bytes 393224 | tf_op jit(solution)/shard_map/ppermute | solution.py:543
  84.0 11.1 %collective-permute-start.15 = (bf16[1024,256]{1,0:T(8,128)(2,1)}, bf16[1024,256]{1,0:T(8,128)(2,1)S(1)}, u32[]{:S(2)}, u32[]{:S(2)}) collective-permute-start(bf16[1024,256]{1,0:T(8,128)(2,1)} %get-tuple-element.31), channel_id=1, source_target_pairs={{0,16},{1,65},{8,24},{9,73},{16,0},{17,81},{24,8},{25,89},{32,48},... | collective-permute-start | bytes 1572872 | tf_op jit(solution)/shard_map/ppermute | solution.py:44
  84.2 16.2 %collective-permute-start.16 = (bf16[1024,256]{1,0:T(8,128)(2,1)}, bf16[1024,256]{1,0:T(8,128)(2,1)S(1)}, u32[]{:S(2)}, u32[]{:S(2)}) collective-permute-start(bf16[1024,256]{1,0:T(8,128)(2,1)} %get-tuple-element.32), channel_id=1, source_target_pairs={{0,8},{1,33},{8,16},{9,41},{16,24},{17,49},{24,0},{25,57},{32,40},... | collective-permute-start | bytes 1572872 | tf_op jit(solution)/shard_map/ppermute | solution.py:44
  85.6 14.8 %collective-permute-start.17 = (bf16[1024,256]{1,0:T(8,128)(2,1)}, bf16[1024,256]{1,0:T(8,128)(2,1)S(1)}, u32[]{:S(2)}, u32[]{:S(2)}) collective-permute-start(bf16[1024,256]{1,0:T(8,128)(2,1)} %get-tuple-element.33), channel_id=1, source_target_pairs={{0,24},{1,97},{8,0},{9,105},{16,8},{17,113},{24,16},{25,121},{32,5... | collective-permute-start | bytes 1572872 | tf_op jit(solution)/shard_map/ppermute | solution.py:44
  (6 other events, 39.8 us)

commit v5 on v4

--- a/solution.py
+++ b/solution.py
@@ -323,24 +323,34 @@
     return [mine, hop(two, 2, True), hop(one, 1, True), hop(three, -1, True)]
 
 
-def total_kernel(*refs):
+def partial_kernel(*refs):
     total = refs[0][...].astype(jnp.float32)
     for ref in refs[1:-1]:
         total = total + ref[...].astype(jnp.float32)
     refs[-1][...] = total.T
 
 
+def total_kernel(partial_ref, last_ref, out_ref):
+    out_ref[...] = partial_ref[...] + last_ref[...].astype(jnp.float32).T
+
+
+def summed(kernel, name, operands, shape):
+    return pl.pallas_call(
+        kernel,
+        in_specs=[pl.BlockSpec(memory_space=pltpu.VMEM)] * len(operands),
+        out_specs=pl.BlockSpec(memory_space=pltpu.VMEM),
+        out_shape=jax.ShapeDtypeStruct(shape, jnp.float32),
+        compiler_params=params(16),
+        cost_estimate=cost(4 * shape[0] * shape[1], 12 * shape[0] * shape[1]),
+        name=name,
+    )(*operands)
+
+
 def total_gradient(terms):
-    cols, rows = terms[0].shape
-    return pl.pallas_call(
-        total_kernel,
-        in_specs=[pl.BlockSpec(memory_space=pltpu.VMEM)] * len(terms),
-        out_specs=pl.BlockSpec(memory_space=pltpu.VMEM),
-        out_shape=jax.ShapeDtypeStruct((rows, cols), jnp.float32),
-        compiler_params=params(16),
-        cost_estimate=cost(4 * rows * cols, 12 * rows * cols),
-        name="total_gradient",
-    )(*hbm(terms[:1]), *terms[1:])
+    mine, two, one, three = terms
+    shape = mine.shape[::-1]
+    partial = summed(partial_kernel, "partial_gradient", [*hbm([mine]), two, three], shape)
+    return summed(total_kernel, "total_gradient", [partial, one], shape)
 
 
 def attend_kernel(

time: 104 us -> 103 us (level)
  starting transfers between devices: 36.3 us -> 35 us
    ppermute x9, starting transfers between devices: 12.2 us -> 11 us  [hop(): return lax.ppermute(value, ('ctx', 'dp'), axis_shift(k, second))]
    pallas_call x1 -> x2, Pallas kernels: 2.35 us -> 2.55 us  [summed(): pl.pallas_call(kernel, in_specs=[pl.BlockSpec(memory_space=pltpu.VMEM)] *...]
  transfers between devices with their start and end apart: 19 -> 19, of which waited for: 5 -> 7; matrix products, arithmetic and copies ran while one was open for 11% -> 12% of each run, Pallas kernels for 34% -> 36%
where the time goes in v5:
time: 103 us; the launch traced here: 102 us
  Pallas kernels  41.7 us (40%)
  starting transfers between devices  35 us (34%)
  waiting for transfers between devices  11.8 us (11%)
  other arithmetic  7.21 us (7%)
  local copies, waits for them, and re-layouts  2.63 us (3%)
  matrix products  2.51 us (2%)
    pallas_call x4, Pallas kernels, pieces(): pl.pallas_call(lambda *refs: piece_kernel(plan, len(arrived), len(out_sha...  18.7 us
    pallas_call x1, Pallas kernels, attend(): pl.pallas_call(attend_kernel, grid=(RUN // TILE,), in_specs=[pl.BlockSpec...  11.3 us
    ppermute x9, starting transfers between devices, hop(): return lax.ppermute(value, ('ctx', 'dp'), axis_shift(k, second))  11 us
    ppermute x4, starting transfers between devices, on_device(): lax.ppermute(both, 'ctx', run_shift(k, parties))  8.4 us
    ppermute x9, waiting for transfers between devices, hop(): return lax.ppermute(value, ('ctx', 'dp'), axis_shift(k, second))  8.36 us
    pallas_call x1, Pallas kernels, project(): pl.pallas_call(project_kernel, in_specs=[pl.BlockSpec(memory_space=pl.ANY...  7.94 us
    ppermute x1, starting transfers between devices, on_device(): lax.ppermute(joint.astype(jnp.bfloat16), 'ctx', run_shift(-1, parties))  5.87 us
    all_to_all x1, starting transfers between devices, on_device(): lax.all_to_all(packed.reshape(parties, slots // parties, -1), 'ctx', 0, 0...  4.54 us
  transfers between devices with their start and end apart: 19, of which 7 were waited for; matrix products, arithmetic and copies ran while one was open for 12% of the time, Pallas kernels for 36%

profile of v5, /device:TPU:0, one launch (start us, length us, event | category | flops | bytes accessed | tf_op | source)
XLA Modules:
  0.0 101.7 jit_solution(3675394230242171908)
XLA Ops:
  1.6 1.7 %collective-permute-start.5 = (bf16[256,256]{1,0:T(8,128)(2,1)S(1)}, bf16[256,256]{1,0:T(8,128)(2,1)S(1)}, u32[]{:S(2)}, u32[]{:S(2)}) collective-permute-start(bf16[256,256]{1,0:T(8,128)(2,1)S(1)} %pad_maximum_fusion), channel_id=1, source_target_pairs={{0,8},{8,16},{16,24},{24,32},{32,40},{40,48},{48,56},{56,64},{64,7... | collective-permute-start | bytes 393224 | tf_op jit(solution)/shard_map/ppermute | solution.py:513
  3.4 2.9 %collective-permute-start.4 = (bf16[256,256]{1,0:T(8,128)(2,1)S(1)}, bf16[256,256]{1,0:T(8,128)(2,1)S(1)}, u32[]{:S(2)}, u32[]{:S(2)}) collective-permute-start(bf16[256,256]{1,0:T(8,128)(2,1)S(1)} %pad_maximum_fusion), channel_id=1, source_target_pairs={{0,16},{8,24},{16,32},{24,40},{32,48},{40,56},{48,64},{56,72},{64,... | collective-permute-start | bytes 393224 | tf_op jit(solution)/shard_map/ppermute | solution.py:513
  6.3 2.3 %collective-permute-start.3 = (bf16[256,256]{1,0:T(8,128)(2,1)S(1)}, bf16[256,256]{1,0:T(8,128)(2,1)S(1)}, u32[]{:S(2)}, u32[]{:S(2)}) collective-permute-start(bf16[256,256]{1,0:T(8,128)(2,1)S(1)} %pad_maximum_fusion), channel_id=1, source_target_pairs={{0,24},{8,32},{16,40},{24,48},{32,56},{40,64},{48,72},{56,80},{64,... | collective-permute-start | bytes 393224 | tf_op jit(solution)/shard_map/ppermute | solution.py:513
  8.6 1.5 %collective-permute-start.2 = (bf16[256,256]{1,0:T(8,128)(2,1)S(1)}, bf16[256,256]{1,0:T(8,128)(2,1)S(1)}, u32[]{:S(2)}, u32[]{:S(2)}) collective-permute-start(bf16[256,256]{1,0:T(8,128)(2,1)S(1)} %pad_maximum_fusion), channel_id=1, source_target_pairs={{0,32},{8,40},{16,48},{24,56},{32,64},{40,72},{48,80},{56,88},{64,... | collective-permute-start | bytes 393224 | tf_op jit(solution)/shard_map/ppermute | solution.py:513
  10.9 1.3 %and_select_fusion.2 = (s32[16]{0:T(128)S(1)}, s32[16]{0:T(128)S(1)}, s32[16]{0:T(128)}) fusion(s32[256]{0:T(256)S(1)} %select_reduce_fusion, s32[]{:T(128)S(6)} %select_n.73, s32[1,256]{1,0:T(1,128)} %param.15), kind=kLoop, calls=%fused_computation.25 | loop fusion | flops 480 | bytes 324 | tf_op jit(solution)/shard_map/jit(floor_divide)/jit(_where)/select_n | solution.py:498
  15.7 4.3 %far_pieces.1 = (bf16[512,1024]{1,0:T(8,128)(2,1)}, bf16[512,1024]{1,0:T(8,128)(2,1)}) custom-call(s32[21]{0:T(128)S(1)} %pad_add_fusion.refs_0_, bf16[256,8192]{1,0:T(8,128)(2,1)} %bitcast.29, bf16[256,8192]{1,0:T(8,128)(2,1)} %collective-permute-done.refs_1_.refs_2_, bf16[1024,256]{1,0:T(8,128)(2,1)S(1)} %turn.1.refs_3_, ...), custom_call_target="tpu_custom_call" | custom-call | flops 1073741824 | bytes 4194304 | tf_op jit(solution)/shard_map/far_pieces/pallas_call | solution.py:250
  21.2 2.0 %collective-permute-start.7 = (bf16[512,1024]{1,0:T(8,128)(2,1)}, bf16[512,1024]{1,0:T(8,128)(2,1)S(1)}, u32[]{:S(2)}, u32[]{:S(2)}) collective-permute-start(bf16[512,1024]{1,0:T(8,128)(2,1)} %get-tuple-element.20.refs_6_), channel_id=1, source_target_pairs={{0,96},{1,25},{8,104},{9,1},{16,112},{17,9},{24,120},{25,17},{32,0... | collective-permute-start | bytes 3145736 | tf_op jit(solution)/shard_map/ppermute | solution.py:44
  24.2 4.5 %near_pieces.1 = (bf16[512,1024]{1,0:T(8,128)(2,1)}, bf16[512,1024]{1,0:T(8,128)(2,1)}) custom-call(s32[21]{0:T(128)S(1)} %pad_add_fusion.refs_0_, bf16[256,8192]{1,0:T(8,128)(2,1)} %bitcast.30, bf16[256,8192]{1,0:T(8,128)(2,1)} %collective-permute-done.refs_1_.refs_2_, bf16[1024,256]{1,0:T(8,128)(2,1)S(1)} %turn.1.refs_3_, ...), custom_call_target="tpu_custom_call" | custom-call | flops 1073741824 | bytes 5242880 | tf_op jit(solution)/shard_map/near_pieces/pallas_call | solution.py:250
  29.3 1.5 %collective-permute-start.11 = (bf16[512,1024]{1,0:T(8,128)(2,1)}, bf16[512,1024]{1,0:T(8,128)(2,1)S(1)}, u32[]{:S(2)}, u32[]{:S(2)}) collective-permute-start(bf16[512,1024]{1,0:T(8,128)(2,1)} %get-tuple-element.21.after_ref), channel_id=1, source_target_pairs={{0,32},{1,9},{8,40},{9,17},{16,48},{17,25},{24,56},{25,1},{32,64},... | collective-permute-start | bytes 3145736 | tf_op jit(solution)/shard_map/ppermute | solution.py:44
  30.8 7.9 %project.1.refs_7_.g_ref = bf16[256,1024]{1,0:T(8,128)(2,1)S(1)} custom-call(bf16[256,8192]{1,0:T(8,128)(2,1)} %bitcast.31, bf16[8192,1024]{1,0:T(8,128)(2,1)} %weight_ref.1, bf16[512,1024]{1,0:T(8,128)(2,1)} %get-tuple-element.21.after_ref), custom_call_target="tpu_custom_call" | custom-call | flops 4294967296 | bytes 20971520 | tf_op jit(solution)/shard_map/project/pallas_call | solution.py:92
  38.8 4.6 %join_pieces.1 = (bf16[512,1024]{1,0:T(8,128)(2,1)}, bf16[512,1024]{1,0:T(8,128)(2,1)}) custom-call(s32[21]{0:T(128)S(1)} %pad_add_fusion.refs_0_, bf16[256,8192]{1,0:T(8,128)(2,1)} %bitcast.32, bf16[256,8192]{1,0:T(8,128)(2,1)} %collective-permute-done.refs_1_.refs_2_, bf16[1024,256]{1,0:T(8,128)(2,1)S(1)} %turn.1.refs_3_, ...), custom_call_target="tpu_custom_call" | custom-call | flops 1073741824 | bytes 7340032 | tf_op jit(solution)/shard_map/join_pieces/pallas_call | solution.py:250
  43.4 3.2 %collective-permute-start.14 = (bf16[512,1024]{1,0:T(8,128)(2,1)}, bf16[512,1024]{1,0:T(8,128)(2,1)}, u32[]{:S(2)}, u32[]{:S(2)}) collective-permute-start(bf16[512,1024]{1,0:T(8,128)(2,1)} %get-tuple-element.23.after_minus), channel_id=1, source_target_pairs={{0,96},{1,25},{8,104},{9,1},{16,112},{17,9},{24,120},{25,17},{32,0... | collective-permute-start | bytes 3145736 | tf_op jit(solution)/shard_map/ppermute | solution.py:44
  46.6 11.3 %attend.1 = (bf16[512,1024]{1,0:T(8,128)(2,1)}, f32[256,256]{1,0:T(8,128)}, bf16[256,256]{1,0:T(8,128)(2,1)}, bf16[256,512]{1,0:T(8,128)(2,1)}, bf16[256,256]{1,0:T(8,128)(2,1)}) custom-call(s32[1,256]{1,0:T(1,128)} %bitcast.43, s32[1,256]{1,0:T(1,128)} %add.164.pos_ref, bf16[256,1024]{1,0:T(8,128)(2,1)} %bitcast.44, ...), custom_call_target="tpu_custom_call" | custom-call | flops 3355443200 | bytes 8388608 | tf_op jit(solution)/shard_map/attend/pallas_call | solution.py:450
  57.9 4.0 %collective-permute-start.8 = (bf16[256,512]{1,0:T(8,128)(2,1)}, bf16[256,512]{1,0:T(8,128)(2,1)S(1)}, u32[]{:S(2)}, u32[]{:S(2)}) collective-permute-start(bf16[256,512]{1,0:T(8,128)(2,1)} %get-tuple-element.26), channel_id=1, source_target_pairs={{0,112},{8,120},{16,0},{24,8},{32,16},{40,24},{48,32},{56,40},{64,... | collective-permute-start | bytes 786440 | tf_op jit(solution)/shard_map/ppermute | solution.py:550
  62.2 4.5 %all-to-all-start = ((bf16[16,32,1024]{2,1,0:T(8,128)(2,1)}), bf16[16,32,1024]{2,1,0:T(8,128)(2,1)}, u32[]{:S(2)}, u32[]{:S(2)}) async-start(bf16[16,32,1024]{2,1,0:T(8,128)(2,1)} %bitcast.34), calls=%async_computation | async-start | bytes 2097152 | tf_op jit(solution)/shard_map/all_to_all | solution.py:542
  66.7 2.1 %collective-permute-done.8 = bf16[256,512]{1,0:T(8,128)(2,1)S(1)} collective-permute-done((bf16[256,512]{1,0:T(8,128)(2,1)}, bf16[256,512]{1,0:T(8,128)(2,1)S(1)}, u32[]{:S(2)}, u32[]{:S(2)}) %collective-permute-start.8) | collective-permute-done | bytes 262176 | tf_op jit(solution)/shard_map/ppermute | solution.py:550
  69.9 1.6 %add_convert_fusion.1 = bf16[256,256]{1,0:T(8,128)(2,1)} fusion(bf16[256,256]{1,0:T(8,128)(2,1)} %get-tuple-element.28, bf16[256,512]{1,0:T(8,128)(2,1)S(1)} %collective-permute-done.8), kind=kLoop, calls=%fused_computation.5 | loop fusion | flops 262144 | bytes 393216 | tf_op jit(solution)/shard_map/convert_element_type | solution.py:553
  71.5 5.9 %collective-permute-start.10 = (bf16[256,256]{1,0:T(8,128)(2,1)}, bf16[256,256]{1,0:T(8,128)(2,1)}, u32[]{:S(2)}, u32[]{:S(2)}) collective-permute-start(bf16[256,256]{1,0:T(8,128)(2,1)} %add_convert_fusion.1), channel_id=1, source_target_pairs={{0,120},{8,0},{16,8},{24,16},{32,24},{40,32},{48,40},{56,48},{64,5... | collective-permute-start | bytes 393224 | tf_op jit(solution)/shard_map/ppermute | solution.py:553
  78.6 5.3 %block_pieces.1 = (bf16[1024,256]{1,0:T(8,128)(2,1)}, bf16[1024,256]{1,0:T(8,128)(2,1)}, bf16[1024,256]{1,0:T(8,128)(2,1)}, bf16[1024,256]{1,0:T(8,128)(2,1)}) custom-call(s32[21]{0:T(128)S(1)} %copy-done.4, bf16[256,8192]{1,0:T(8,128)(2,1)} %bitcast.33, bf16[256,8192]{1,0:T(8,128)(2,1)} %collective-permute-done.refs_1_.refs_2_, ...), custom_call_target="tpu_custom_call" | custom-call | flops 1073741824 | bytes 8388608 | tf_op jit(solution)/shard_map/block_pieces/pallas_call | solution.py:250
  84.8 1.4 %collective-permute-start.17 = (bf16[1024,256]{1,0:T(8,128)(2,1)}, bf16[1024,256]{1,0:T(8,128)(2,1)S(1)}, u32[]{:S(2)}, u32[]{:S(2)}) collective-permute-start(bf16[1024,256]{1,0:T(8,128)(2,1)} %get-tuple-element.33), channel_id=1, source_target_pairs={{0,8},{1,33},{8,16},{9,41},{16,24},{17,49},{24,0},{25,57},{32,40},... | collective-permute-start | bytes 1572872 | tf_op jit(solution)/shard_map/ppermute | solution.py:44
  88.3 2.5 %fusion = bf16[1,256,1024]{2,1,0:T(8,128)(2,1)} fusion(bf16[512,1024]{1,0:T(8,128)(2,1)} %bitcast.12, s32[256]{0:T(256)} %add.156), kind=kOutput, calls=%fused_computation.2 | convolution fusion | flops 268828672 | bytes 1573888 | tf_op jit(solution)/shard_map/dot_general | solution.py:548
  90.8 4.2 %collective-permute-done.15.refs_1_ = bf16[1024,256]{1,0:T(8,128)(2,1)S(1)} collective-permute-done((bf16[1024,256]{1,0:T(8,128)(2,1)}, bf16[1024,256]{1,0:T(8,128)(2,1)S(1)}, u32[]{:S(2)}, u32[]{:S(2)}) %collective-permute-start.15) | collective-permute-done | bytes 524320 | tf_op jit(solution)/shard_map/ppermute | solution.py:44
  95.0 3.7 %collective-permute-done.16.refs_2_ = bf16[1024,256]{1,0:T(8,128)(2,1)S(1)} collective-permute-done((bf16[1024,256]{1,0:T(8,128)(2,1)}, bf16[1024,256]{1,0:T(8,128)(2,1)S(1)}, u32[]{:S(2)}, u32[]{:S(2)}) %collective-permute-start.16) | collective-permute-done | bytes 524320 | tf_op jit(solution)/shard_map/ppermute | solution.py:44
  98.7 1.4 %partial_gradient.1.partial_ref = f32[256,1024]{1,0:T(8,128)S(1)} custom-call(bf16[1024,256]{1,0:T(8,128)(2,1)} %get-tuple-element.30.refs_0_, bf16[1024,256]{1,0:T(8,128)(2,1)S(1)} %collective-permute-done.15.refs_1_, bf16[1024,256]{1,0:T(8,128)(2,1)S(1)} %collective-permute-done.16.refs_2_), custom_call_target="tpu_custom_call" | custom-call | flops 1048576 | bytes 3145728 | tf_op jit(solution)/shard_map/partial_gradient/pallas_call | solution.py:338
  (70 shorter events, 15.2 us)
Async XLA Ops:
  0.6 14.0 %copy-start = (s32[1,4096]{1,0:T(1,128)S(1)}, s32[1,4096]{1,0:T(1,128)}, u32[]{:S(2)}) copy-start(s32[1,4096]{1,0:T(1,128)} %param.14) | copy-start | bytes 49156
  0.6 13.2 %copy-start.10 = (s32[4]{0:T(128)S(1)}, s32[4]{0:T(128)}, u32[]{:S(2)}) copy-start(s32[4]{0:T(128)} %constant.86.clone.1) | copy-start | bytes 52
  0.7 11.8 %collective-permute-start = (bf16[256,8192]{1,0:T(8,128)(2,1)}, bf16[256,8192]{1,0:T(8,128)(2,1)}, u32[]{:S(2)}, u32[]{:S(2)}) collective-permute-start(bf16[256,8192]{1,0:T(8,128)(2,1)} %bitcast.28), channel_id=1, source_target_pairs={{0,1},{1,0},{2,3},{3,2},{4,5},{5,4},{6,7},{7,6},{8,9},{9,8},{10,11... | collective-permute-start | bytes 12582920 | tf_op jit(solution)/shard_map/ppermute | solution.py:48
  1.6 13.1 %collective-permute-start.5 = (bf16[256,256]{1,0:T(8,128)(2,1)S(1)}, bf16[256,256]{1,0:T(8,128)(2,1)S(1)}, u32[]{:S(2)}, u32[]{:S(2)}) collective-permute-start(bf16[256,256]{1,0:T(8,128)(2,1)S(1)} %pad_maximum_fusion), channel_id=1, source_target_pairs={{0,8},{8,16},{16,24},{24,32},{32,40},{40,48},{48,56},{56,64},{64,7... | collective-permute-start | bytes 393224 | tf_op jit(solution)/shard_map/ppermute | solution.py:513
  3.4 11.3 %collective-permute-start.4 = (bf16[256,256]{1,0:T(8,128)(2,1)S(1)}, bf16[256,256]{1,0:T(8,128)(2,1)S(1)}, u32[]{:S(2)}, u32[]{:S(2)}) collective-permute-start(bf16[256,256]{1,0:T(8,128)(2,1)S(1)} %pad_maximum_fusion), channel_id=1, source_target_pairs={{0,16},{8,24},{16,32},{24,40},{32,48},{40,56},{48,64},{56,72},{64,... | collective-permute-start | bytes 393224 | tf_op jit(solution)/shard_map/ppermute | solution.py:513
  6.3 8.5 %collective-permute-start.3 = (bf16[256,256]{1,0:T(8,128)(2,1)S(1)}, bf16[256,256]{1,0:T(8,128)(2,1)S(1)}, u32[]{:S(2)}, u32[]{:S(2)}) collective-permute-start(bf16[256,256]{1,0:T(8,128)(2,1)S(1)} %pad_maximum_fusion), channel_id=1, source_target_pairs={{0,24},{8,32},{16,40},{24,48},{32,56},{40,64},{48,72},{56,80},{64,... | collective-permute-start | bytes 393224 | tf_op jit(solution)/shard_map/ppermute | solution.py:513
  8.6 6.3 %collective-permute-start.2 = (bf16[256,256]{1,0:T(8,128)(2,1)S(1)}, bf16[256,256]{1,0:T(8,128)(2,1)S(1)}, u32[]{:S(2)}, u32[]{:S(2)}) collective-permute-start(bf16[256,256]{1,0:T(8,128)(2,1)S(1)} %pad_maximum_fusion), channel_id=1, source_target_pairs={{0,32},{8,40},{16,48},{24,56},{32,64},{40,72},{48,80},{56,88},{64,... | collective-permute-start | bytes 393224 | tf_op jit(solution)/shard_map/ppermute | solution.py:513
  13.7 2.0 %collective-permute-start.1 = (bf16[1024,256]{1,0:T(8,128)(2,1)S(1)}, bf16[1024,256]{1,0:T(8,128)(2,1)S(1)}, u32[]{:S(2)}, u32[]{:S(2)}) collective-permute-start(bf16[1024,256]{1,0:T(8,128)(2,1)S(1)} %turn.1.refs_3_), channel_id=1, source_target_pairs={{0,1},{1,0},{2,3},{3,2},{4,5},{5,4},{6,7},{7,6},{8,9},{9,8},{10,11... | collective-permute-start | bytes 1572872 | tf_op jit(solution)/shard_map/ppermute | solution.py:48
  14.7 24.1 %copy-start.3 = (s32[21]{0:T(128)}, s32[21]{0:T(128)S(1)}, u32[]{:S(2)}) copy-start(s32[21]{0:T(128)S(1)} %pad_add_fusion.refs_0_) | copy-start | bytes 256
  20.0 18.8 %collective-permute-start.6 = (bf16[512,1024]{1,0:T(8,128)(2,1)}, bf16[512,1024]{1,0:T(8,128)(2,1)S(1)}, u32[]{:S(2)}, u32[]{:S(2)}) collective-permute-start(bf16[512,1024]{1,0:T(8,128)(2,1)} %get-tuple-element.19.refs_5_), channel_id=1, source_target_pairs={{0,32},{1,9},{8,40},{9,17},{16,48},{17,25},{24,56},{25,1},{32,64},... | collective-permute-start | bytes 3145736 | tf_op jit(solution)/shard_map/ppermute | solution.py:44
  21.2 17.5 %collective-permute-start.7 = (bf16[512,1024]{1,0:T(8,128)(2,1)}, bf16[512,1024]{1,0:T(8,128)(2,1)S(1)}, u32[]{:S(2)}, u32[]{:S(2)}) collective-permute-start(bf16[512,1024]{1,0:T(8,128)(2,1)} %get-tuple-element.20.refs_6_), channel_id=1, source_target_pairs={{0,96},{1,25},{8,104},{9,1},{16,112},{17,9},{24,120},{25,17},{32,0... | collective-permute-start | bytes 3145736 | tf_op jit(solution)/shard_map/ppermute | solution.py:44
  28.7 42.8 %collective-permute-start.12 = (bf16[512,1024]{1,0:T(8,128)(2,1)}, bf16[512,1024]{1,0:T(8,128)(2,1)S(1)}, u32[]{:S(2)}, u32[]{:S(2)}) collective-permute-start(bf16[512,1024]{1,0:T(8,128)(2,1)} %get-tuple-element.29), channel_id=1, source_target_pairs={{0,96},{1,25},{8,104},{9,1},{16,112},{17,9},{24,120},{25,17},{32,0... | collective-permute-start | bytes 3145736 | tf_op jit(solution)/shard_map/ppermute | solution.py:44
  29.3 48.7 %collective-permute-start.11 = (bf16[512,1024]{1,0:T(8,128)(2,1)}, bf16[512,1024]{1,0:T(8,128)(2,1)S(1)}, u32[]{:S(2)}, u32[]{:S(2)}) collective-permute-start(bf16[512,1024]{1,0:T(8,128)(2,1)} %get-tuple-element.21.after_ref), channel_id=1, source_target_pairs={{0,32},{1,9},{8,40},{9,17},{16,48},{17,25},{24,56},{25,1},{32,64},... | collective-permute-start | bytes 3145736 | tf_op jit(solution)/shard_map/ppermute | solution.py:44
  43.3 34.7 %collective-permute-start.13 = (bf16[512,1024]{1,0:T(8,128)(2,1)}, bf16[512,1024]{1,0:T(8,128)(2,1)}, u32[]{:S(2)}, u32[]{:S(2)}) collective-permute-start(bf16[512,1024]{1,0:T(8,128)(2,1)} %get-tuple-element.22.after_plus), channel_id=1, source_target_pairs={{0,32},{1,9},{8,40},{9,17},{16,48},{17,25},{24,56},{25,1},{32,64},... | collective-permute-start | bytes 3145736 | tf_op jit(solution)/shard_map/ppermute | solution.py:44
  43.4 34.6 %collective-permute-start.14 = (bf16[512,1024]{1,0:T(8,128)(2,1)}, bf16[512,1024]{1,0:T(8,128)(2,1)}, u32[]{:S(2)}, u32[]{:S(2)}) collective-permute-start(bf16[512,1024]{1,0:T(8,128)(2,1)} %get-tuple-element.23.after_minus), channel_id=1, source_target_pairs={{0,96},{1,25},{8,104},{9,1},{16,112},{17,9},{24,120},{25,17},{32,0... | collective-permute-start | bytes 3145736 | tf_op jit(solution)/shard_map/ppermute | solution.py:44
  46.6 15.3 %copy-start.9 = (s32[16]{0:T(128)S(1)}, s32[16]{0:T(128)}, u32[]{:S(2)}) copy-start(s32[16]{0:T(128)} %get-tuple-element.38) | copy-start | bytes 196
  57.9 10.9 %collective-permute-start.8 = (bf16[256,512]{1,0:T(8,128)(2,1)}, bf16[256,512]{1,0:T(8,128)(2,1)S(1)}, u32[]{:S(2)}, u32[]{:S(2)}) collective-permute-start(bf16[256,512]{1,0:T(8,128)(2,1)} %get-tuple-element.26), channel_id=1, source_target_pairs={{0,112},{8,120},{16,0},{24,8},{32,16},{40,24},{48,32},{56,40},{64,... | collective-permute-start | bytes 786440 | tf_op jit(solution)/shard_map/ppermute | solution.py:550
  62.2 26.2 %all-to-all-start = ((bf16[16,32,1024]{2,1,0:T(8,128)(2,1)}), bf16[16,32,1024]{2,1,0:T(8,128)(2,1)}, u32[]{:S(2)}, u32[]{:S(2)}) async-start(bf16[16,32,1024]{2,1,0:T(8,128)(2,1)} %bitcast.34), calls=%async_computation | async-start | bytes 2097152 | tf_op jit(solution)/shard_map/all_to_all | solution.py:542
  68.8 9.2 %copy-start.6 = (bf16[256,512]{1,0:T(8,128)(2,1)}, bf16[256,512]{1,0:T(8,128)(2,1)S(1)}, u32[]{:S(2)}) copy-start(bf16[256,512]{1,0:T(8,128)(2,1)S(1)} %collective-permute-done.8) | copy-start | bytes 786436
  68.8 17.4 %collective-permute-start.9 = (bf16[256,256]{1,0:T(8,128)(2,1)}, bf16[256,256]{1,0:T(8,128)(2,1)}, u32[]{:S(2)}, u32[]{:S(2)}) collective-permute-start(bf16[256,256]{1,0:T(8,128)(2,1)} %get-tuple-element.27), channel_id=1, source_target_pairs={{0,96},{8,104},{16,112},{24,120},{32,0},{40,8},{48,16},{56,24},{64... | collective-permute-start | bytes 393224 | tf_op jit(solution)/shard_map/ppermute | solution.py:551
  71.5 15.1 %collective-permute-start.10 = (bf16[256,256]{1,0:T(8,128)(2,1)}, bf16[256,256]{1,0:T(8,128)(2,1)}, u32[]{:S(2)}, u32[]{:S(2)}) collective-permute-start(bf16[256,256]{1,0:T(8,128)(2,1)} %add_convert_fusion.1), channel_id=1, source_target_pairs={{0,120},{8,0},{16,8},{24,16},{32,24},{40,32},{48,40},{56,48},{64,5... | collective-permute-start | bytes 393224 | tf_op jit(solution)/shard_map/ppermute | solution.py:553
  84.0 11.1 %collective-permute-start.15 = (bf16[1024,256]{1,0:T(8,128)(2,1)}, bf16[1024,256]{1,0:T(8,128)(2,1)S(1)}, u32[]{:S(2)}, u32[]{:S(2)}) collective-permute-start(bf16[1024,256]{1,0:T(8,128)(2,1)} %get-tuple-element.31), channel_id=1, source_target_pairs={{0,16},{1,65},{8,24},{9,73},{16,0},{17,81},{24,8},{25,89},{32,48},... | collective-permute-start | bytes 1572872 | tf_op jit(solution)/shard_map/ppermute | solution.py:44
  84.2 14.5 %collective-permute-start.16 = (bf16[1024,256]{1,0:T(8,128)(2,1)}, bf16[1024,256]{1,0:T(8,128)(2,1)S(1)}, u32[]{:S(2)}, u32[]{:S(2)}) collective-permute-start(bf16[1024,256]{1,0:T(8,128)(2,1)} %get-tuple-element.32), channel_id=1, source_target_pairs={{0,24},{1,97},{8,0},{9,105},{16,8},{17,113},{24,16},{25,121},{32,5... | collective-permute-start | bytes 1572872 | tf_op jit(solution)/shard_map/ppermute | solution.py:44
  84.8 15.7 %collective-permute-start.17 = (bf16[1024,256]{1,0:T(8,128)(2,1)}, bf16[1024,256]{1,0:T(8,128)(2,1)S(1)}, u32[]{:S(2)}, u32[]{:S(2)}) collective-permute-start(bf16[1024,256]{1,0:T(8,128)(2,1)} %get-tuple-element.33), channel_id=1, source_target_pairs={{0,8},{1,33},{8,16},{9,41},{16,24},{17,49},{24,0},{25,57},{32,40},... | collective-permute-start | bytes 1572872 | tf_op jit(solution)/shard_map/ppermute | solution.py:44
  (6 other events, 38.2 us)
